TPU v7x, 128 devices: a whole 4x4x4 slice. The times are simulated.
128 devices in a mesh: rows: 2 (over core), vocab: 64 (over z, y, x).
Axes of the slice: x: 4, y: 4, z: 4, core: 2. Of those that a mesh axis runs over, the one named last changes fastest.
Arguments:
- hidden_states: bfloat16 [512, 2048], P('rows'), may hold values from -30 to 30
- head_weight: bfloat16 [2048, 155648], P('rows', 'vocab'), may hold values from -2.5 to 2.5
- target_logits: bfloat16 [512, 155648], P('rows', 'vocab'), may hold values from -40 to 330
Outputs:
- divergence: float32 [512], P('rows')
- hidden_grad: float32 [512, 2048], P('rows')
- head_grad: float32 [2048, 155648], P('rows', 'vocab')
All inputs are finite; a program needn't handle non-finite values.
Results may differ from a plain program's by a relative error of at most 0.0044.
Values may be sent and summed in bfloat16 or wider, within the bound.
No kernel may reach another device: no remote copies, remote signals or barrier semaphores. Data moves between devices by JAX's collectives and lax.ppermute only.
A program may use at most 128 MiB of HBM per device.

v0:
```python
import jax
import jax.numpy as jnp
from jax import lax
from jax.sharding import PartitionSpec as P


def softmax_grad(target_logits, draft):
    target = target_logits.astype(jnp.float32)
    peak_t = jnp.max(target, axis=1)
    peak_q = jnp.max(draft, axis=1)
    top_t, top_q = lax.pmax((peak_t, peak_q), "vocab")
    exp_t = jnp.exp(target - top_t[:, None])
    exp_q = jnp.exp(draft - top_q[:, None])
    sum_t, cross, sum_q = lax.psum(
        (jnp.sum(exp_t, axis=1), jnp.sum(exp_t * (target - draft), axis=1), jnp.sum(exp_q, axis=1)),
        "vocab",
    )
    divergence = cross / sum_t - top_t - jnp.log(sum_t) + top_q + jnp.log(sum_q)
    factor = target_logits.shape[1] * lax.axis_size("vocab") / 1024.0
    dlogits = ((exp_q / sum_q[:, None] - exp_t / sum_t[:, None]) * factor).astype(jnp.bfloat16)
    return (divergence, dlogits)


def shards(hidden_states, head_weight, target_logits):
    full_weight = lax.all_gather(head_weight, "rows", axis=0, tiled=True)
    draft = jnp.dot(hidden_states, full_weight, preferred_element_type=jnp.float32)
    divergence, dlogits = softmax_grad(target_logits, draft)
    partial_back = lax.dot_general(
        dlogits, full_weight, (((1,), (1,)), ((), ())), preferred_element_type=jnp.float32
    )
    hidden_grad = lax.psum(partial_back, "vocab")
    head_grad = lax.psum_scatter(
        lax.dot_general(
            hidden_states, dlogits, (((0,), (0,)), ((), ())), preferred_element_type=jnp.float32
        ),
        "rows",
        scatter_dimension=0,
        tiled=True,
    )
    return (divergence, hidden_grad, head_grad)


def solution(mesh):
    placed = (P("rows", None), P("rows", "vocab"), P("rows", "vocab"))
    return jax.shard_map(
        shards,
        mesh=mesh,
        in_specs=placed,
        out_specs=(P("rows"), P("rows", None), P("rows", "vocab")),
        check_vma=False,
    )
```

profile of v0, /device:TPU:0, one launch (start us, length us, event | category | flops | bytes accessed | tf_op | source)
XLA Modules:
  0.0 587.6 jit_solution(7768573413923590387)
XLA Ops:
  7.2 0.0 copy-start
  7.2 0.0 copy-start.1
  7.2 0.0 all-gather.2.cloned.1.call-start
  7.2 0.7 all-gather.2.cloned.1.call-update
  7.9 0.0 reduce-scatter.2.cloned.1.call-start
  8.0 0.6 copy-done.1
  8.6 0.2 reduce_max.23
  8.8 28.4 %all-gather.2.cloned.1.call-done = bf16[2048,2432]{1,0:T(8,128)(2,1)} async-done(((bf16[1024,2432]{1,0:T(8,128)(2,1)}), bf16[2048,2432]{1,0:T(8,128)(2,1)}) %all-gather.2.cloned.1.call-update) | async-done | bytes 9961488 | tf_op jit(solution)/shard_map/all_gather | solution.py:25
  37.2 0.0 copy-done
  37.2 8.2 %fusion.12 = (f32[256]{0:T(256)S(1)}, f32[256,2432]{1,0:T(8,128)}) fusion(bf16[256,2048]{1,0:T(8,128)(2,1)S(1)} %copy-done, bf16[2048,2432]{1,0:T(8,128)(2,1)} %all-gather.2.cloned.1.call-done), kind=kOutput, calls=%fused_computation.15 | convolution fusion | flops 2550759168 | bytes 13501440 | tf_op jit(solution)/shard_map/dot_general | solution.py:26
  45.4 179.1 %all-reduce.1 = (f32[256]{0:T(256)S(1)}, f32[256]{0:T(256)S(1)}) all-reduce(bf16[256]{0:T(256)(128)(2,1)S(1)} %reduce_max.23, f32[256]{0:T(256)S(1)} %get-tuple-element.14), channel_id=1, replica_groups=mesh['rows'=2,'vocab'=64] {'vocab'}, use_global_device_ids=true, to_apply=%region_1.0 | all-reduce | flops 512 | bytes 3584 | tf_op jit(solution)/shard_map/pmax | solution.py:11
  224.4 2.9 fusion.4
  227.3 171.7 %all-reduce = (f32[256]{0:T(256)S(1)}, f32[256]{0:T(256)S(1)}, f32[256]{0:T(256)S(1)}) all-reduce(f32[256]{0:T(256)S(1)} %get-tuple-element.7, f32[256]{0:T(256)S(1)} %get-tuple-element.8, f32[256]{0:T(256)S(1)} %get-tuple-element.6), channel_id=1, replica_groups=mesh['rows'=2,'vocab'=64] {'vocab'}, use_global_device_ids=true, to_apply=%region_9.0 | all-reduce | flops 768 | bytes 6144 | tf_op jit(solution)/shard_map/psum | solution.py:14
  399.1 11.9 %convolution_bitcast_fusion = f32[2048,2432]{0,1:T(8,128)} fusion(bf16[256,2048]{1,0:T(8,128)(2,1)S(1)} %copy-done, bf16[256,2432]{1,0:T(8,128)(2,1)S(1)} %copy-done.1, f32[256,2432]{1,0:T(8,128)} %get-tuple-element.15, f32[256]{0:T(256)S(1)} %get-tuple-element.10, f32[256]{0:T(256)S(1)} %get-tuple-element.9, f32[256]{0:T(256)S(1)} %get-tuple-element.13, ...), kind=kOutput, calls=%fused_computation | convolution fusion | flops 2555117568 | bytes 24711168 | tf_op jit(solution)/shard_map/dot_general | solution.py:33
  410.9 0.0 reduce-scatter.2.cloned.1.call-update
  410.9 0.0 all-reduce.4.cloned.1.call-start
  411.0 9.6 %fusion.10 = f32[256,2048]{1,0:T(8,128)} fusion(bf16[2048,2432]{1,0:T(8,128)(2,1)} %all-gather.2.cloned.1.call-done, bf16[256,2432]{1,0:T(8,128)(2,1)S(1)} %copy-done.1, f32[256,2432]{1,0:T(8,128)} %get-tuple-element.15, f32[256]{0:T(256)S(1)} %get-tuple-element.10, f32[256]{0:T(256)S(1)} %get-tuple-element.9, f32[256]{0:T(256)S(1)} %get-tuple-element.13, ...), kind=kOutput, calls=%fused_computation.14 | convolution fusion | flops 2555117568 | bytes 15798272 | tf_op jit(solution)/shard_map/dot_general | solution.py:28
  420.6 0.0 all-reduce.4.cloned.1.call-update
  420.6 0.6 log_add_fusion
  421.2 17.3 %reduce-scatter.2.cloned.1.call-done = f32[1024,2432]{0,1:T(8,128)} async-done(((f32[2048,2432]{0,1:T(8,128)}), f32[1024,2432]{0,1:T(8,128)}) %reduce-scatter.2.cloned.1.call-update) | async-done | bytes 9961488 | tf_op jit(solution)/shard_map/reduce_scatter | solution.py:32
  438.5 10.6 %copy.6 = f32[1024,2432]{1,0:T(8,128)} copy(f32[1024,2432]{0,1:T(8,128)} %reduce-scatter.2.cloned.1.call-done) | data formatting | bytes 19922944
  449.1 128.8 %all-reduce.4.cloned.1.call-done = f32[256,2048]{1,0:T(8,128)} async-done(((f32[256,2048]{1,0:T(8,128)}), f32[256,2048]{1,0:T(8,128)}) %all-reduce.4.cloned.1.call-update) | async-done | bytes 2097168 | tf_op jit(solution)/shard_map/psum | solution.py:31
  578.0 3.1 copy.8
Async XLA Ops:
  7.2 30.1 %copy-start = (bf16[256,2048]{1,0:T(8,128)(2,1)S(1)}, bf16[256,2048]{1,0:T(8,128)(2,1)}, u32[]{:S(2)}) copy-start(bf16[256,2048]{1,0:T(8,128)(2,1)} %param.3) | copy-start | bytes 3145732
  7.2 1.4 copy-start.1
  7.2 30.0 %all-gather.2.cloned.1.call-start = ((), (), s32[]{:S(2)}) async-start(), calls=%async_computation.1 | async-start | bytes 14942208 | tf_op jit(solution)/shard_map/all_gather | solution.py:25
  7.9 430.6 %reduce-scatter.2.cloned.1.call-start = ((), (), s32[]{:S(2)}) async-start(), calls=%async_computation.3 | async-start | bytes 29884416 | tf_op jit(solution)/shard_map/reduce_scatter | solution.py:32
  410.9 167.0 %all-reduce.4.cloned.1.call-start = ((), (), s32[]{:S(2)}) async-start(), calls=%async_computation.2 | async-start | bytes 4194304 | tf_op jit(solution)/shard_map/psum | solution.py:31
Sparse Core Ops, SparseCore 0:
  9.7 27.4 all-gather.1
  411.1 27.4 reduce-scatter.1
  444.0 133.9 all-reduce.3
where the time goes:
time: 588 us
  blocking collectives  351 us (60%)
  waiting for transfers between devices  175 us (30%)
  matrix products  29.6 us (5%)
  local copies, waits for them, and re-layouts  14.4 us (2%)
  between operations  13.8 us (2%)
    pmax x1, blocking collectives, softmax_grad(): top_t, top_q = lax.pmax((peak_t, peak_q), 'vocab')  179 us
    psum x1, blocking collectives, softmax_grad(): lax.psum((jnp.sum(exp_t, axis=1), jnp.sum(exp_t * (target - draft), axis=...  172 us
    psum x1, waiting for transfers between devices, shards(): hidden_grad = lax.psum(partial_back, 'vocab')  129 us
    all_gather x1, waiting for transfers between devices, shards(): full_weight = lax.all_gather(head_weight, 'rows', axis=0, tiled=True)  28.4 us
    reduce_scatter x1, waiting for transfers between devices, shards(): lax.psum_scatter(lax.dot_general(hidden_states, dlogits, (((0,), (0,)), (...  17.3 us
    unnamed x6, local copies, waits for them, and re-layouts  14.4 us
    dot_general x1, matrix products, shards(): lax.dot_general(hidden_states, dlogits, (((0,), (0,)), ((), ())), preferr...  11.9 us
  transfers between devices with their start and end apart: 3, of which 3 were waited for; matrix products, arithmetic and copies ran while one was open for 4% of the time, Pallas kernels for 0%

commit v1 on v0

v1 whole, which is shorter than its diff:
```python
import jax
import jax.numpy as jnp
from jax import lax
from jax.sharding import PartitionSpec as P

SWAP = ((0, 1), (1, 0))


def dot(a, b, ca, cb):
    return lax.dot_general(a, b, (((ca,), (cb,)), ((), ())), preferred_element_type=jnp.float32)


def swap(x):
    return lax.ppermute(x, "rows", SWAP)


def to_all(x, n):
    return lax.all_to_all(jnp.broadcast_to(x[None], (n,) + x.shape), "vocab", 0, 0)


def shards(hidden, weight, target_logits):
    n = lax.axis_size("vocab")
    row = lax.axis_index("rows")
    tokens, width = hidden.shape
    half = weight.shape[0]
    vocab = target_logits.shape[1]

    with jax.named_scope("swap_weight"):
        weight_o = swap(weight)
    mine = lax.dynamic_slice_in_dim(hidden, row * half, half, 1)
    theirs = lax.dynamic_slice_in_dim(hidden, (1 - row) * half, half, 1)
    with jax.named_scope("swap_hidden"):
        mine_o = swap(theirs)

    with jax.named_scope("draft"):
        draft = dot(mine, weight, 1, 0) + dot(theirs, weight_o, 1, 0)

    with jax.named_scope("stats"):
        target = target_logits.astype(jnp.float32)
        peak_t = jnp.max(target, axis=1)
        peak_q = jnp.max(draft, axis=1)
        exp_t = jnp.exp(target - peak_t[:, None])
        part = jnp.stack(
            [
                peak_t,
                jnp.sum(exp_t, axis=1),
                jnp.sum(exp_t * (target - draft), axis=1),
                peak_q,
                jnp.sum(jnp.exp(draft - peak_q[:, None]), axis=1),
            ]
        )
    with jax.named_scope("share_stats"):
        parts = to_all(part, n)
    with jax.named_scope("merge_stats"):
        top_t = jnp.max(parts[:, 0], axis=0)
        top_q = jnp.max(parts[:, 3], axis=0)
        scale_t = jnp.exp(parts[:, 0] - top_t)
        scale_q = jnp.exp(parts[:, 3] - top_q)
        sum_t = jnp.sum(parts[:, 1] * scale_t, axis=0)
        cross = jnp.sum(parts[:, 2] * scale_t, axis=0)
        sum_q = jnp.sum(parts[:, 4] * scale_q, axis=0)
        lse_t = top_t + jnp.log(sum_t)
        lse_q = top_q + jnp.log(sum_q)
        divergence = cross / sum_t - lse_t + lse_q

    with jax.named_scope("dlogits"):
        factor = vocab * n / 1024.0
        p = jnp.exp(target - lse_t[:, None])
        q = jnp.exp(draft - lse_q[:, None])
        dlogits = ((q - p) * factor).astype(jnp.bfloat16)
    with jax.named_scope("swap_dlogits"):
        dlogits_o = swap(dlogits)

    with jax.named_scope("hidden_grad"):
        back = jnp.concatenate([dot(dlogits, weight, 1, 1), dot(dlogits, weight_o, 1, 1)], axis=1)
        back = back.astype(jnp.bfloat16).reshape(n, tokens // n, width)
    with jax.named_scope("scatter_sum"):
        terms = lax.all_to_all(back, "vocab", 0, 0)
    with jax.named_scope("sum"):
        total = jnp.sum(terms.astype(jnp.float32), axis=0)
        total = jnp.roll(total, row * half, axis=1).astype(jnp.bfloat16)
    with jax.named_scope("gather"):
        hidden_grad = to_all(total, n).reshape(tokens, width).astype(jnp.float32)

    with jax.named_scope("head_grad"):
        head_grad = dot(mine, dlogits, 0, 0) + dot(mine_o, dlogits_o, 0, 0)
    return (divergence, hidden_grad, head_grad)


def solution(mesh):
    return jax.shard_map(
        shards,
        mesh=mesh,
        in_specs=(P("rows", None), P("rows", "vocab"), P("rows", "vocab")),
        out_specs=(P("rows"), P("rows", None), P("rows", "vocab")),
        check_vma=False,
    )
```

time: 588 us -> 103 us (0.18)
  blocking collectives: 351 us -> 25.1 us
  waiting for transfers between devices: 175 us -> 28.1 us
  between operations: 13.8 us -> 0.8 us
  starting transfers between devices: 0.12 us -> 10.2 us
  local copies, waits for them, and re-layouts: 14.4 us -> 5.88 us
    pmax x1 -> x0, blocking collectives: 179 us -> none  [softmax_grad(): top_t, top_q = lax.pmax((peak_t, peak_q), 'vocab')]
    psum x1 -> x0, blocking collectives: 172 us -> none  [softmax_grad(): lax.psum((jnp.sum(exp_t, axis=1), jnp.sum(exp_t * (target - draft), axis=...]
    psum x1 -> x0, waiting for transfers between devices: 129 us -> none  [shards(): hidden_grad = lax.psum(partial_back, 'vocab')]
    all_gather x1 -> x0, waiting for transfers between devices: 28.4 us -> none  [shards(): full_weight = lax.all_gather(head_weight, 'rows', axis=0, tiled=True)]
    all_to_all x0 -> x2, waiting for transfers between devices: none -> 25.3 us  [the longest x1 17.3 us: shards(): terms = lax.all_to_all(back, 'vocab', 0, 0)]
    all_to_all x0 -> x1, blocking collectives: none -> 25.1 us  [to_all(): lax.all_to_all(jnp.broadcast_to(x[None], (n,) + x.shape), 'vocab', 0, 0)]
    reduce_scatter x1 -> x0, waiting for transfers between devices: 17.3 us -> none  [shards(): lax.psum_scatter(lax.dot_general(hidden_states, dlogits, (((0,), (0,)), (...]
    unnamed x6 -> x10, local copies, waits for them, and re-layouts: 14.4 us -> 1.47 us
  transfers between devices with their start and end apart: 3 -> 5, of which waited for: 3 -> 3; matrix products, arithmetic and copies ran while one was open for 4% -> 16% of each run, Pallas kernels for 0% -> 0%
where the time goes in v1:
time: 103 us; the launch traced here: 102 us
  waiting for transfers between devices  28.1 us (27%)
  matrix products  25.5 us (25%)
  blocking collectives  25.1 us (24%)
  starting transfers between devices  10.2 us (10%)
  other arithmetic  6.73 us (7%)
  local copies, waits for them, and re-layouts  5.88 us (6%)
    dot_general x6, matrix products, dot(): lax.dot_general(a, b, (((ca,), (cb,)), ((), ())), preferred_element_type=...  25.5 us
    all_to_all x1, blocking collectives, to_all(): lax.all_to_all(jnp.broadcast_to(x[None], (n,) + x.shape), 'vocab', 0, 0)  25.1 us
    all_to_all x1, waiting for transfers between devices, shards(): terms = lax.all_to_all(back, 'vocab', 0, 0)  17.3 us
    all_to_all x1, waiting for transfers between devices, to_all(): lax.all_to_all(jnp.broadcast_to(x[None], (n,) + x.shape), 'vocab', 0, 0)  8.06 us
    all_to_all x1, starting transfers between devices, to_all(): lax.all_to_all(jnp.broadcast_to(x[None], (n,) + x.shape), 'vocab', 0, 0)  4.83 us
    all_to_all x1, starting transfers between devices, shards(): terms = lax.all_to_all(back, 'vocab', 0, 0)  4.73 us
    ppermute x3, waiting for transfers between devices, swap(): return lax.ppermute(x, 'rows', SWAP)  2.77 us
  transfers between devices with their start and end apart: 5, of which 3 were waited for; matrix products, arithmetic and copies ran while one was open for 16% of the time, Pallas kernels for 0%

profile of v1, /device:TPU:0, one launch (start us, length us, event | category | flops | bytes accessed | tf_op | source)
XLA Modules:
  0.0 102.4 jit_solution(5632077140882985676)
XLA Ops:
  0.6 0.0 copy-start
  0.6 0.1 collective-permute-start
  0.7 1.6 %reduce_max.45 = bf16[256]{0:T(256)(128)(2,1)S(1)} reduce(bf16[256,2432]{1,0:T(8,128)(2,1)} %param.5, bf16[]{:T(256)} %constant.30.clone.1), dimensions={1}, to_apply=%region_0.0 | reduce | flops 622336 | bytes 1245698 | tf_op jit(solution)/shard_map/stats/reduce_max | solution.py:40
  2.4 0.0 copy-done
  2.4 0.0 copy-start.4
  2.4 4.1 %fusion.10 = f32[256,2432]{1,0:T(8,128)S(1)} fusion(bf16[1024,2432]{1,0:T(8,128)(2,1)} %param.4, bf16[256,2048]{1,0:T(8,128)(2,1)S(1)} %copy-done, s32[]{:T(128)S(6)} %select_n.19), kind=kOutput, calls=%fused_computation.20 | convolution fusion | flops 1275068416 | bytes 7995396 | tf_op jit(solution)/shard_map/draft/dot_general | solution.py:10
  6.6 0.0 copy-start.1
  6.6 2.8 %collective-permute-done = bf16[1024,2432]{1,0:T(8,128)(2,1)} collective-permute-done((bf16[1024,2432]{1,0:T(8,128)(2,1)}, bf16[1024,2432]{1,0:T(8,128)(2,1)}, u32[]{:S(2)}, u32[]{:S(2)}) %collective-permute-start) | collective-permute-done | bytes 4980768 | tf_op jit(solution)/shard_map/swap_weight/ppermute | solution.py:14
  9.4 0.0 copy-done.4
  9.4 4.1 %fusion.25 = (f32[256]{0:T(256)S(1)}, f32[256,2432]{1,0:T(8,128)S(1)}) fusion(f32[256,2432]{1,0:T(8,128)S(1)} %fusion.10, bf16[256,1024]{1,0:T(8,128)(2,1)S(1)} %constant_dynamic-slice_fusion, bf16[1024,2432]{1,0:T(8,128)(2,1)} %collective-permute-done), kind=kOutput, calls=%fused_computation.47 | convolution fusion | flops 1276313344 | bytes 10486784 | tf_op jit(solution)/shard_map/draft/dot_general | solution.py:10
  13.4 0.0 copy-start.2
  13.4 1.4 %copy-done.2 = f32[256,2432]{1,0:T(8,128)} copy-done((f32[256,2432]{1,0:T(8,128)}, f32[256,2432]{1,0:T(8,128)S(1)}, u32[]{:S(2)}) %copy-start.2) | copy-done | bytes 2490392
  14.9 0.0 copy-done.1
  14.9 1.2 %exponential_reduce_fusion = (f32[256]{0:T(256)S(1)}, f32[256]{0:T(256)S(1)}, f32[256]{0:T(256)S(1)}) fusion(f32[256,2432]{1,0:T(8,128)S(1)} %get-tuple-element.19, f32[256]{0:T(256)S(1)} %get-tuple-element.18, f32[256]{0:T(256)S(1)} %reduce_max.52, bf16[256,2432]{1,0:T(8,128)(2,1)S(1)} %copy-done.1), kind=kLoop, calls=%fused_computation.13 | loop fusion | flops 4979968 | bytes 3740672 | tf_op jit(solution)/shard_map/stats/reduce_sum | solution.py:49
  16.1 0.0 copy-start.3
  16.2 25.1 %all_to_all.15 = f32[64,5,256]{2,1,0:T(8,128)S(1)} all-to-all(f32[64,5,256]{2,1,0:T(8,128)S(1)} %broadcast_in_dim.4), channel_id=1, replica_groups=mesh['rows'=2,'vocab'=64] {'vocab'}, dimensions={0} | all-to-all | bytes 655360 | tf_op jit(solution)/shard_map/share_stats/all_to_all | solution.py:18
  41.3 0.3 slice_reduce_fusion.1
  41.6 0.6 subtract_add_fusion
  42.2 0.0 copy-done.3
  42.2 0.8 fusion.7
  43.0 4.8 %convolution_convert_fusion.1 = bf16[256,1024]{1,0:T(8,128)(2,1)} fusion(bf16[256,2432]{1,0:T(8,128)(2,1)S(1)} %fusion.7, bf16[1024,2432]{1,0:T(8,128)(2,1)} %param.4), kind=kOutput, calls=%fused_computation.16 | convolution fusion | flops 1275330560 | bytes 6750208 | tf_op jit(solution)/shard_map/hidden_grad/dot_general | solution.py:10
  47.8 4.0 %convolution_convert_fusion = bf16[256,1024]{1,0:T(8,128)(2,1)S(1)} fusion(bf16[256,2432]{1,0:T(8,128)(2,1)S(1)} %fusion.7, bf16[1024,2432]{1,0:T(8,128)(2,1)} %collective-permute-done), kind=kOutput, calls=%fused_computation.15 | convolution fusion | flops 1275330560 | bytes 6750208 | tf_op jit(solution)/shard_map/hidden_grad/dot_general | solution.py:10
  51.7 0.2 concatenate.14
  51.9 1.2 %concatenate.13 = bf16[64,4,1024]{2,1,0:T(4,128)(2,1)S(1)} reshape(bf16[256,1024]{1,0:T(8,128)(2,1)} %convolution_convert_fusion.1) | data formatting | bytes 1048576 | tf_op jit(solution)/shard_map/hidden_grad/concatenate | solution.py:75
  53.2 1.6 %pad_maximum_fusion = bf16[64,4,2048]{2,1,0:T(4,128)(2,1)} fusion(bf16[64,4,1024]{2,1,0:T(4,128)(2,1)S(1)} %concatenate.14, bf16[64,4,1024]{2,1,0:T(4,128)(2,1)S(1)} %concatenate.13), kind=kLoop, calls=%fused_computation.17 | loop fusion | flops 2097152 | bytes 2097152 | tf_op jit(solution)/shard_map/hidden_grad/concatenate | solution.py:75
  54.8 4.7 %all-to-all-start.1 = ((bf16[64,4,2048]{2,1,0:T(4,128)(2,1)}), bf16[64,4,2048]{2,1,0:T(4,128)(2,1)S(1)}, u32[]{:S(2)}, u32[]{:S(2)}) async-start(bf16[64,4,2048]{2,1,0:T(4,128)(2,1)} %pad_maximum_fusion), calls=%async_computation.1 | async-start | bytes 2097152 | tf_op jit(solution)/shard_map/scatter_sum/all_to_all | solution.py:78
  59.5 0.1 collective-permute-start.2
  59.6 0.5 collective-permute-start.1
  60.1 17.3 %all-to-all-done.1 = bf16[64,4,2048]{2,1,0:T(4,128)(2,1)S(1)} async-done(((bf16[64,4,2048]{2,1,0:T(4,128)(2,1)}), bf16[64,4,2048]{2,1,0:T(4,128)(2,1)S(1)}, u32[]{:S(2)}, u32[]{:S(2)}) %all-to-all-start.1) | async-done | bytes 1048608 | tf_op jit(solution)/shard_map/scatter_sum/all_to_all | solution.py:78
  77.4 0.4 convert_reduce_fusion
  77.8 0.1 fusion.22
  78.0 1.5 %broadcast_in_dim.5 = bf16[64,4,2048]{2,1,0:T(4,128)(2,1)} broadcast(bf16[4,2048]{1,0:T(4,128)(2,1)S(1)} %fusion.22), dimensions={1,2} | broadcast | bytes 1064960 | tf_op jit(solution)/shard_map/gather/broadcast_in_dim | solution.py:18
  79.4 4.8 %all-to-all-start.2 = ((bf16[64,4,2048]{2,1,0:T(4,128)(2,1)}), bf16[64,4,2048]{2,1,0:T(4,128)(2,1)S(1)}, u32[]{:S(2)}, u32[]{:S(2)}) async-start(bf16[64,4,2048]{2,1,0:T(4,128)(2,1)} %broadcast_in_dim.5), calls=%async_computation.2 | async-start | bytes 2097152 | tf_op jit(solution)/shard_map/gather/all_to_all | solution.py:18
  84.3 1.6 %fusion.8 = f32[1024,2432]{1,0:T(8,128)S(1)} fusion(bf16[256,2432]{1,0:T(8,128)(2,1)S(1)} %fusion.7, bf16[256,2048]{1,0:T(8,128)(2,1)S(1)} %copy-done, s32[]{:T(128)S(6)} %select_n.19), kind=kOutput, calls=%fused_computation.18 | convolution fusion | flops 1275068416 | bytes 11730948 | tf_op jit(solution)/shard_map/head_grad/dot_general | solution.py:10
  85.8 0.0 collective-permute-done.1
  85.9 0.0 collective-permute-done.2
  85.9 7.0 %convolution_add_fusion = f32[1024,2432]{1,0:T(8,128)} fusion(f32[1024,2432]{1,0:T(8,128)S(1)} %fusion.8, bf16[256,1024]{1,0:T(8,128)(2,1)} %collective-permute-done.1, bf16[256,2432]{1,0:T(8,128)(2,1)} %collective-permute-done.2), kind=kOutput, calls=%fused_computation | convolution fusion | flops 1277558784 | bytes 21692416 | tf_op jit(solution)/shard_map/head_grad/dot_general | solution.py:10
  92.9 8.1 %all-to-all-done.2 = bf16[64,4,2048]{2,1,0:T(4,128)(2,1)S(1)} async-done(((bf16[64,4,2048]{2,1,0:T(4,128)(2,1)}), bf16[64,4,2048]{2,1,0:T(4,128)(2,1)S(1)}, u32[]{:S(2)}, u32[]{:S(2)}) %all-to-all-start.2) | async-done | bytes 1048608 | tf_op jit(solution)/shard_map/gather/all_to_all | solution.py:18
  101.0 1.4 %reshape.44 = f32[256,2048]{1,0:T(8,128)} reshape(bf16[64,4,2048]{2,1,0:T(4,128)(2,1)S(1)} %all-to-all-done.2) | data formatting | bytes 3145728 | tf_op jit(solution)/shard_map/gather/convert_element_type | solution.py:83
  (5 shorter events, 0.2 us)
Async XLA Ops:
  0.6 1.7 %copy-start = (bf16[256,2048]{1,0:T(8,128)(2,1)S(1)}, bf16[256,2048]{1,0:T(8,128)(2,1)}, u32[]{:S(2)}) copy-start(bf16[256,2048]{1,0:T(8,128)(2,1)} %param.3) | copy-start | bytes 3145732
  0.6 8.7 %collective-permute-start = (bf16[1024,2432]{1,0:T(8,128)(2,1)}, bf16[1024,2432]{1,0:T(8,128)(2,1)}, u32[]{:S(2)}, u32[]{:S(2)}) collective-permute-start(bf16[1024,2432]{1,0:T(8,128)(2,1)} %param.4), channel_id=1, source_target_pairs={{0,64},{64,0},{1,65},{65,1},{2,66},{66,2},{3,67},{67,3},{4,68},{68... | collective-permute-start | bytes 14942216 | tf_op jit(solution)/shard_map/swap_weight/ppermute | solution.py:14
  2.4 6.9 %copy-start.4 = (bf16[256,1024]{1,0:T(8,128)(2,1)}, bf16[256,1024]{1,0:T(8,128)(2,1)S(1)}, u32[]{:S(2)}) copy-start(bf16[256,1024]{1,0:T(8,128)(2,1)S(1)} %constant_dynamic-slice_fusion) | copy-start | bytes 1572868
  6.6 8.3 %copy-start.1 = (bf16[256,2432]{1,0:T(8,128)(2,1)S(1)}, bf16[256,2432]{1,0:T(8,128)(2,1)}, u32[]{:S(2)}) copy-start(bf16[256,2432]{1,0:T(8,128)(2,1)} %param.5) | copy-start | bytes 3735556
  13.4 1.5 %copy-start.2 = (f32[256,2432]{1,0:T(8,128)}, f32[256,2432]{1,0:T(8,128)S(1)}, u32[]{:S(2)}) copy-start(f32[256,2432]{1,0:T(8,128)S(1)} %get-tuple-element.19) | copy-start | bytes 7471108
  16.1 26.1 %copy-start.3 = (f32[256,2432]{1,0:T(8,128)S(1)}, f32[256,2432]{1,0:T(8,128)}, u32[]{:S(2)}) copy-start(f32[256,2432]{1,0:T(8,128)} %copy-done.2) | copy-start | bytes 7471108
  54.8 22.6 %all-to-all-start.1 = ((bf16[64,4,2048]{2,1,0:T(4,128)(2,1)}), bf16[64,4,2048]{2,1,0:T(4,128)(2,1)S(1)}, u32[]{:S(2)}, u32[]{:S(2)}) async-start(bf16[64,4,2048]{2,1,0:T(4,128)(2,1)} %pad_maximum_fusion), calls=%async_computation.1 | async-start | bytes 2097152 | tf_op jit(solution)/shard_map/scatter_sum/all_to_all | solution.py:78
  59.5 26.3 %collective-permute-start.2 = (bf16[256,2432]{1,0:T(8,128)(2,1)S(1)}, bf16[256,2432]{1,0:T(8,128)(2,1)}, u32[]{:S(2)}, u32[]{:S(2)}) collective-permute-start(bf16[256,2432]{1,0:T(8,128)(2,1)S(1)} %fusion.7), channel_id=1, source_target_pairs={{0,64},{64,0},{1,65},{65,1},{2,66},{66,2},{3,67},{67,3},{4,68},{68... | collective-permute-start | bytes 3735560 | tf_op jit(solution)/shard_map/swap_dlogits/ppermute | solution.py:14
  59.6 26.2 %collective-permute-start.1 = (bf16[256,1024]{1,0:T(8,128)(2,1)}, bf16[256,1024]{1,0:T(8,128)(2,1)}, u32[]{:S(2)}, u32[]{:S(2)}) collective-permute-start(bf16[256,1024]{1,0:T(8,128)(2,1)} %copy-done.4), channel_id=1, source_target_pairs={{0,64},{64,0},{1,65},{65,1},{2,66},{66,2},{3,67},{67,3},{4,68},{68... | collective-permute-start | bytes 1572872 | tf_op jit(solution)/shard_map/swap_hidden/ppermute | solution.py:14
  79.4 21.5 %all-to-all-start.2 = ((bf16[64,4,2048]{2,1,0:T(4,128)(2,1)}), bf16[64,4,2048]{2,1,0:T(4,128)(2,1)S(1)}, u32[]{:S(2)}, u32[]{:S(2)}) async-start(bf16[64,4,2048]{2,1,0:T(4,128)(2,1)} %broadcast_in_dim.5), calls=%async_computation.2 | async-start | bytes 2097152 | tf_op jit(solution)/shard_map/gather/all_to_all | solution.py:18

commit v2 on v1

v2 whole, which is shorter than its diff:
```python
import functools
import jax
import jax.numpy as jnp
from jax import lax
from jax.experimental import pallas as pl
from jax.experimental.pallas import tpu as pltpu
from jax.sharding import PartitionSpec as P

SWAP = ((0, 1), (1, 0))
TOKENS_PIECE = 16
COLS_PIECE = 512
BLOCK = 640
LIMIT = 40 * 1024 * 1024
F32, BF16 = jnp.float32, jnp.bfloat16


def dot(a, b, ca, cb):
    return lax.dot_general(a, b, (((ca,), (cb,)), ((), ())), preferred_element_type=F32)


def swap(x):
    return lax.ppermute(x, "rows", SWAP)


def params(**kw):
    return pltpu.CompilerParams(vmem_limit_bytes=LIMIT, **kw)


def whole(shape):
    return pl.BlockSpec(shape, lambda *_: (0,) * len(shape))


def lanes_to_rows(columns):
    lane = lax.broadcasted_iota(jnp.int32, (columns[0].shape[0], 128), 1)
    packed = jnp.zeros(lane.shape, F32)
    for i, column in enumerate(columns):
        packed = jnp.where(lane == i, column, packed)
    return packed.T[:8]


def running(first, peak_ref, sum_ref, values):
    peak = jnp.max(values, axis=1, keepdims=True)
    old = jnp.where(first, peak, peak_ref[...])
    new = jnp.maximum(old, peak)
    kept = jnp.where(first, 0.0, sum_ref[...])
    sum_ref[...] = kept * jnp.exp(old - new) + jnp.sum(jnp.exp(values - new), axis=1, keepdims=True)
    peak_ref[...] = new


def own_kernel(vocab, mine, weight, target, acc, stat, peak, total):
    j = pl.program_id(0)
    acc[...] = dot(mine[...], weight[...], 1, 0)
    inside = j * BLOCK + lax.broadcasted_iota(jnp.int32, target.shape, 1) < vocab
    running(j == 0, peak, total, jnp.where(inside, target[...].astype(F32), -jnp.inf))

    @pl.when(j == pl.num_programs(0) - 1)
    def _():
        lane = lax.broadcasted_iota(jnp.int32, stat.shape, 1)
        stat[...] = jnp.where(lane == 0, peak[...], total[...])


def own_part(mine, weight, target):
    tokens, half = mine.shape
    vocab = target.shape[1]
    column = lambda j: (0, j)
    return pl.pallas_call(
        functools.partial(own_kernel, vocab),
        grid=(pl.cdiv(vocab, BLOCK),),
        in_specs=[
            whole((tokens, half)),
            pl.BlockSpec((half, BLOCK), column),
            pl.BlockSpec((tokens, BLOCK), column),
        ],
        out_specs=[pl.BlockSpec((tokens, BLOCK), column), whole((tokens, 128))],
        out_shape=[
            jax.ShapeDtypeStruct((tokens, vocab), F32),
            jax.ShapeDtypeStruct((tokens, 128), F32),
        ],
        scratch_shapes=[pltpu.VMEM((tokens, 1), F32)] * 2,
        compiler_params=params(),
        cost_estimate=pl.CostEstimate(flops=2 * tokens * half * vocab, bytes_accessed=2 * half * vocab, transcendentals=0),
        name="own_part",
    )(mine, weight, target)


def draft_kernel(vocab, theirs, weight, acc, target, stat, draft, out, peak, total, cross):
    j = pl.program_id(0)
    first = j == 0
    value = acc[...] + dot(theirs[...], weight[...], 1, 0)
    draft[...] = value
    inside = j * BLOCK + lax.broadcasted_iota(jnp.int32, target.shape, 1) < vocab
    running(first, peak, total, jnp.where(inside, value, -jnp.inf))
    wide = target[...].astype(F32)
    term = jnp.where(inside, jnp.exp(wide - stat[:, :1]) * (wide - value), 0.0)
    cross[...] = jnp.where(first, 0.0, cross[...]) + jnp.sum(term, axis=1, keepdims=True)

    @pl.when(j == pl.num_programs(0) - 1)
    def _():
        out[...] = lanes_to_rows([stat[:, :1], stat[:, 1:2], cross[...], peak[...], total[...]])


def draft_part(theirs, weight, acc, target, stat):
    tokens, half = theirs.shape
    vocab = target.shape[1]
    column = lambda j: (0, j)
    return pl.pallas_call(
        functools.partial(draft_kernel, vocab),
        grid=(pl.cdiv(vocab, BLOCK),),
        in_specs=[
            whole((tokens, half)),
            pl.BlockSpec((half, BLOCK), column),
            pl.BlockSpec((tokens, BLOCK), column),
            pl.BlockSpec((tokens, BLOCK), column),
            whole((tokens, 128)),
        ],
        out_specs=[pl.BlockSpec((tokens, BLOCK), column), whole((8, tokens))],
        out_shape=[
            jax.ShapeDtypeStruct((tokens, vocab), F32),
            jax.ShapeDtypeStruct((8, tokens), F32),
        ],
        scratch_shapes=[pltpu.VMEM((tokens, 1), F32)] * 3,
        compiler_params=params(),
        cost_estimate=pl.CostEstimate(flops=2 * tokens * half * vocab, bytes_accessed=2 * half * vocab, transcendentals=0),
        name="draft_part",
    )(theirs, weight, acc, target, stat)


def back_kernel(factor, row, parts, draft, target, weight, weight_o, divergence, dlogits, out, buffer, sems):
    half = weight.shape[0]
    per = half // COLS_PIECE
    copies = []
    for j in range(2 * per):
        source = (weight, weight_o)[j // per].at[pl.ds(j % per * COLS_PIECE, COLS_PIECE)]
        copies.append(pltpu.make_async_copy(source, buffer.at[j], sems.at[j]))
        copies[-1].start()

    peaks_t, peaks_q = parts[:, 0, :], parts[:, 3, :]
    top_t = jnp.max(peaks_t, axis=0, keepdims=True)
    top_q = jnp.max(peaks_q, axis=0, keepdims=True)
    scale_t, scale_q = jnp.exp(peaks_t - top_t), jnp.exp(peaks_q - top_q)
    sum_t = jnp.sum(parts[:, 1, :] * scale_t, axis=0, keepdims=True)
    cross = jnp.sum(parts[:, 2, :] * scale_t, axis=0, keepdims=True)
    sum_q = jnp.sum(parts[:, 4, :] * scale_q, axis=0, keepdims=True)
    lse_t, lse_q = top_t + jnp.log(sum_t), top_q + jnp.log(sum_q)
    divergence[...] = cross / sum_t - lse_t + lse_q
    tokens = lse_t.shape[1]
    line = lax.broadcasted_iota(jnp.int32, (128, tokens), 0)
    turned = jnp.where(line == 0, lse_t, lse_q).T
    lse_t, lse_q = turned[:, :1], turned[:, 1:2]

    probs_q = jnp.exp(draft[...] - lse_q)
    probs_t = jnp.exp(target[...].astype(F32) - lse_t)
    dlogits[...] = ((probs_q - probs_t) * factor).astype(BF16)

    for j in range(2 * per):
        copies[j].wait()
        block = dot(dlogits[...], buffer[j], 1, 1).astype(BF16)
        place = lax.rem(row[0] * per + j, 2 * per)
        for i in range(tokens // TOKENS_PIECE):
            out[i * 2 * per + place] = block[i * TOKENS_PIECE : (i + 1) * TOKENS_PIECE]


def back_part(factor, row, parts, draft, target, weight, weight_o):
    tokens, vocab = draft.shape
    half = weight.shape[0]
    n = parts.shape[0]
    pieces = (tokens // TOKENS_PIECE) * (2 * half // COLS_PIECE)
    hbm = pl.BlockSpec(memory_space=pl.ANY)
    vmem = pl.BlockSpec(memory_space=pltpu.VMEM)
    return pl.pallas_call(
        functools.partial(back_kernel, factor),
        in_specs=[pl.BlockSpec(memory_space=pltpu.SMEM), vmem, vmem, vmem, hbm, hbm],
        out_specs=[vmem, vmem, vmem],
        out_shape=[
            jax.ShapeDtypeStruct((1, tokens), F32),
            jax.ShapeDtypeStruct((tokens, vocab), BF16),
            jax.ShapeDtypeStruct((pieces, TOKENS_PIECE, COLS_PIECE), BF16),
        ],
        scratch_shapes=[
            pltpu.VMEM((2 * half // COLS_PIECE, COLS_PIECE, vocab), BF16),
            pltpu.SemaphoreType.DMA((2 * half // COLS_PIECE,)),
        ],
        compiler_params=params(),
        cost_estimate=pl.CostEstimate(flops=4 * tokens * half * vocab, bytes_accessed=4 * half * vocab, transcendentals=0),
        name="back_part",
    )(row, parts, draft, target, weight, weight_o)


def sum_kernel(terms, out):
    total = terms[0].astype(F32)
    for i in range(1, terms.shape[0]):
        total = total + terms[i].astype(F32)
    out[...] = jnp.broadcast_to(total.astype(BF16)[None], out.shape)


def sum_part(terms):
    return pl.pallas_call(
        sum_kernel,
        out_shape=jax.ShapeDtypeStruct(terms.shape, BF16),
        compiler_params=params(),
        name="sum_part",
    )(terms)


def join_kernel(pieces, out):
    across = out.shape[1] // COLS_PIECE
    for i in range(pieces.shape[0]):
        rows = pl.ds(i // across * TOKENS_PIECE, TOKENS_PIECE)
        out[rows, pl.ds(i % across * COLS_PIECE, COLS_PIECE)] = pieces[i].astype(F32)


def join_part(pieces, tokens, width):
    steps = 4
    return pl.pallas_call(
        join_kernel,
        grid=(steps,),
        in_specs=[pl.BlockSpec((pieces.shape[0] // steps,) + pieces.shape[1:], lambda i: (i, 0, 0))],
        out_specs=pl.BlockSpec((tokens // steps, width), lambda i: (i, 0)),
        out_shape=jax.ShapeDtypeStruct((tokens, width), F32),
        compiler_params=params(),
        name="join_part",
    )(pieces)


def shards(hidden, weight, target):
    n = lax.axis_size("vocab")
    row = lax.axis_index("rows")
    tokens, width = hidden.shape
    half, vocab = weight.shape

    with jax.named_scope("swap_weight"):
        weight_o = swap(weight)
    mine = lax.dynamic_slice_in_dim(hidden, row * half, half, 1)
    theirs = lax.dynamic_slice_in_dim(hidden, (1 - row) * half, half, 1)
    with jax.named_scope("swap_hidden"):
        mine_o = swap(theirs)

    acc, stat = own_part(mine, weight, target)
    draft, part = draft_part(theirs, weight_o, acc, target, stat)
    with jax.named_scope("share_stats"):
        parts = lax.all_to_all(jnp.broadcast_to(part[None], (n,) + part.shape), "vocab", 0, 0)
    divergence, dlogits, pieces = back_part(
        vocab * n / 1024.0, jnp.full((1,), row, jnp.int32), parts, draft, target, weight, weight_o
    )
    with jax.named_scope("swap_dlogits"):
        dlogits_o = swap(dlogits)
    with jax.named_scope("scatter_sum"):
        terms = lax.all_to_all(pieces, "vocab", 0, 0)
    totals = sum_part(terms)
    with jax.named_scope("gather"):
        gathered = lax.all_to_all(totals, "vocab", 0, 0)
    hidden_grad = join_part(gathered, tokens, width)

    with jax.named_scope("head_grad"):
        head_grad = dot(mine, dlogits, 0, 0) + dot(mine_o, dlogits_o, 0, 0)
    return (divergence.reshape(tokens), hidden_grad, head_grad)


def solution(mesh):
    return jax.shard_map(
        shards,
        mesh=mesh,
        in_specs=(P("rows", None), P("rows", "vocab"), P("rows", "vocab")),
        out_specs=(P("rows"), P("rows", None), P("rows", "vocab")),
        check_vma=False,
    )
```

time: 103 us -> 98.3 us (0.954)
  Pallas kernels: 0 us -> 18.3 us
  matrix products: 25.5 us -> 8.56 us
  other arithmetic: 6.73 us -> 0.01 us
  waiting for transfers between devices: 28.1 us -> 30.1 us
    pallas_call x0 -> x5, Pallas kernels: none -> 18.3 us  [the longest x1 6.18 us: draft_part(): pl.pallas_call(functools.partial(draft_kernel, vocab), grid=(pl.cdiv(voca...]
    dot_general x6 -> x2, matrix products: 25.5 us -> 8.56 us  [dot(): lax.dot_general(a, b, (((ca,), (cb,)), ((), ())), preferred_element_type=...]
    all_to_all x2, waiting for transfers between devices: 25.3 us -> 29.1 us  [the longest x1 19.3 us: shards(): terms = lax.all_to_all(pieces, 'vocab', 0, 0)]
    unnamed x10, local copies, waits for them, and re-layouts: 1.47 us -> 3.53 us
    reduce_max x3 -> x0, other arithmetic: 1.89 us -> none  [the longest x2 1.62 us: shards(): peak_t = jnp.max(target, axis=1)]
    ppermute x3, waiting for transfers between devices: 2.77 us -> 0.95 us  [swap(): return lax.ppermute(x, 'rows', SWAP)]
    reduce_sum x3 -> x0, other arithmetic: 1.69 us -> none  [the longest x1 1.2 us: shards(): jnp.sum(jnp.exp(draft - peak_q[:, None]), axis=1)]
    concatenate x1 -> x0, other arithmetic: 1.62 us -> none  [shards(): jnp.concatenate([dot(dlogits, weight, 1, 1), dot(dlogits, weight_o, 1, 1)...]
  transfers between devices with their start and end apart: 5 -> 5, of which waited for: 3 -> 3; matrix products, arithmetic and copies ran while one was open for 16% -> 10% of each run, Pallas kernels for 0% -> 5%
where the time goes in v2:
time: 98.3 us; the launch traced here: 97.9 us
  waiting for transfers between devices  30.1 us (31%)
  blocking collectives  25 us (25%)
  Pallas kernels  18.3 us (19%)
  starting transfers between devices  10.3 us (10%)
  matrix products  8.56 us (9%)
  local copies, waits for them, and re-layouts  4.91 us (5%)
    all_to_all x1, blocking collectives, shards(): lax.all_to_all(jnp.broadcast_to(part[None], (n,) + part.shape), 'vocab',...  25 us
    all_to_all x1, waiting for transfers between devices, shards(): terms = lax.all_to_all(pieces, 'vocab', 0, 0)  19.3 us
    all_to_all x1, waiting for transfers between devices, shards(): gathered = lax.all_to_all(totals, 'vocab', 0, 0)  9.87 us
    dot_general x2, matrix products, dot(): lax.dot_general(a, b, (((ca,), (cb,)), ((), ())), preferred_element_type=...  8.56 us
    pallas_call x1, Pallas kernels, draft_part(): pl.pallas_call(functools.partial(draft_kernel, vocab), grid=(pl.cdiv(voca...  6.18 us
    pallas_call x1, Pallas kernels, back_part(): pl.pallas_call(functools.partial(back_kernel, factor), in_specs=[pl.Block...  5.37 us
    all_to_all x1, starting transfers between devices, shards(): gathered = lax.all_to_all(totals, 'vocab', 0, 0)  4.96 us
    all_to_all x1, starting transfers between devices, shards(): terms = lax.all_to_all(pieces, 'vocab', 0, 0)  4.73 us
  transfers between devices with their start and end apart: 5, of which 3 were waited for; matrix products, arithmetic and copies ran while one was open for 10% of the time, Pallas kernels for 5%

profile of v2, /device:TPU:0, one launch (start us, length us, event | category | flops | bytes accessed | tf_op | source)
XLA Modules:
  0.0 97.9 jit_solution(15479188095852126780)
XLA Ops:
  0.6 0.0 copy-start.1
  0.6 0.1 collective-permute-start
  0.7 1.4 %constant_dynamic-slice_fusion = (bf16[256,1024]{1,0:T(8,128)(2,1)S(1)}, bf16[256,1024]{1,0:T(8,128)(2,1)S(1)}) fusion(bf16[256,2048]{1,0:T(8,128)(2,1)} %param.3, s32[]{:T(128)S(6)} %select_n.7, s32[]{:T(128)S(6)} %select_n.6), kind=kLoop, calls=%fused_computation.1 | loop fusion | bytes 2097160 | tf_op jit(solution)/shard_map/dynamic_slice | solution.py:233
  2.1 0.1 copy-done.1
  2.2 0.0 copy-start
  2.2 2.4 %copy-done = bf16[1024,2432]{1,0:T(8,128)(2,1)S(1)} copy-done((bf16[1024,2432]{1,0:T(8,128)(2,1)S(1)}, bf16[1024,2432]{1,0:T(8,128)(2,1)}, u32[]{:S(2)}) %copy-start) | copy-done | bytes 4980760
  4.7 3.7 %own_part.1 = (f32[256,2432]{1,0:T(8,128)S(1)}, f32[256,128]{1,0:T(8,128)S(1)}) custom-call(bf16[256,1024]{1,0:T(8,128)(2,1)S(1)} %get-tuple-element.17.mine, bf16[1024,2432]{1,0:T(8,128)(2,1)S(1)} %copy-done, bf16[256,2432]{1,0:T(8,128)(2,1)S(1)} %copy-done.1), custom_call_target="tpu_custom_call" | custom-call | flops 1275068416 | bytes 4980736 | tf_op jit(solution)/shard_map/own_part/pallas_call | solution.py:66
  8.4 0.9 collective-permute-done.weight.weight_o
  9.3 0.0 slice-start
  9.3 0.0 slice-start.1
  9.3 6.2 %draft_part.1 = (f32[256,2432]{1,0:T(8,128)S(1)}, f32[8,256]{1,0:T(8,128)S(1)}) custom-call(bf16[256,1024]{1,0:T(8,128)(2,1)S(1)} %get-tuple-element.18.theirs, bf16[1024,2432]{1,0:T(8,128)(2,1)} %collective-permute-done.weight.weight_o, f32[256,2432]{1,0:T(8,128)S(1)} %get-tuple-element.10.acc, bf16[256,2432]{1,0:T(8,128)(2,1)S(1)} %copy-done.1, ...), custom_call_target="tpu_custom_call" | custom-call | flops 1275068416 | bytes 4980736 | tf_op jit(solution)/shard_map/draft_part/pallas_call | solution.py:106
  15.6 25.0 %all_to_all.15.parts = f32[64,8,256]{2,1,0:T(8,128)S(1)} all-to-all(f32[64,8,256]{2,1,0:T(8,128)S(1)} %broadcast_in_dim.10), channel_id=1, replica_groups=mesh['rows'=2,'vocab'=64] {'vocab'}, dimensions={0} | all-to-all | bytes 1048576 | tf_op jit(solution)/shard_map/share_stats/all_to_all | solution.py:241
  40.5 0.0 slice-done
  40.5 0.0 slice-done.1
  40.5 5.4 %back_part.1 = (f32[1,256]{1,0:T(1,128)}, bf16[256,2432]{1,0:T(8,128)(2,1)S(1)}, bf16[64,16,512]{2,1,0:T(8,128)(2,1)S(1)}) custom-call(s32[1]{0:T(128)} %bitcast.row, f32[64,8,256]{2,1,0:T(8,128)S(1)} %all_to_all.15.parts, f32[256,2432]{1,0:T(8,128)S(1)} %get-tuple-element.13.draft, bf16[256,2432]{1,0:T(8,128)(2,1)S(1)} %copy-done.1, ...), custom_call_target="tpu_custom_call" | custom-call | flops 2550136832 | bytes 9961472 | tf_op jit(solution)/shard_map/back_part/pallas_call | solution.py:170
  45.9 0.0 copy-start.2
  45.9 1.0 copy-done.2
  46.9 0.0 collective-permute-start.2
  46.9 4.7 %all-to-all-start.1 = ((bf16[64,16,512]{2,1,0:T(8,128)(2,1)}), bf16[64,16,512]{2,1,0:T(8,128)(2,1)S(1)}, u32[]{:S(2)}, u32[]{:S(2)}) async-start(bf16[64,16,512]{2,1,0:T(8,128)(2,1)} %copy-done.2), calls=%async_computation.1 | async-start | bytes 2097152 | tf_op jit(solution)/shard_map/scatter_sum/all_to_all | solution.py:248
  51.6 0.5 collective-permute-start.1
  52.2 19.3 %all-to-all-done.1.terms = bf16[64,16,512]{2,1,0:T(8,128)(2,1)S(1)} async-done(((bf16[64,16,512]{2,1,0:T(8,128)(2,1)}), bf16[64,16,512]{2,1,0:T(8,128)(2,1)S(1)}, u32[]{:S(2)}, u32[]{:S(2)}) %all-to-all-start.1) | async-done | bytes 1048608 | tf_op jit(solution)/shard_map/scatter_sum/all_to_all | solution.py:248
  71.4 1.2 %sum_part.1 = bf16[64,16,512]{2,1,0:T(8,128)(2,1)} custom-call(bf16[64,16,512]{2,1,0:T(8,128)(2,1)S(1)} %all-to-all-done.1.terms), custom_call_target="tpu_custom_call" | custom-call | tf_op jit(solution)/shard_map/sum_part/pallas_call | solution.py:197
  72.6 5.0 %all-to-all-start.2 = ((bf16[64,16,512]{2,1,0:T(8,128)(2,1)}), bf16[64,16,512]{2,1,0:T(8,128)(2,1)S(1)}, u32[]{:S(2)}, u32[]{:S(2)}) async-start(bf16[64,16,512]{2,1,0:T(8,128)(2,1)} %sum_part.1), calls=%async_computation.2 | async-start | bytes 2097152 | tf_op jit(solution)/shard_map/gather/all_to_all | solution.py:251
  77.6 0.0 collective-permute-done.1
  77.6 0.0 collective-permute-done.2
  77.6 3.0 %fusion = f32[1024,2432]{1,0:T(8,128)S(1)} fusion(bf16[256,1024]{1,0:T(8,128)(2,1)} %collective-permute-done.1, bf16[256,2432]{1,0:T(8,128)(2,1)} %collective-permute-done.2), kind=kOutput, calls=%fused_computation.3 | convolution fusion | flops 1275068416 | bytes 11730944 | tf_op jit(solution)/shard_map/head_grad/dot_general | solution.py:18
  80.6 5.5 %convolution_add_fusion = f32[1024,2432]{1,0:T(8,128)} fusion(f32[1024,2432]{1,0:T(8,128)S(1)} %fusion, bf16[256,1024]{1,0:T(8,128)(2,1)S(1)} %get-tuple-element.17.mine, bf16[256,2432]{1,0:T(8,128)(2,1)S(1)} %get-tuple-element.16), kind=kOutput, calls=%fused_computation | convolution fusion | flops 1277558784 | bytes 21692416 | tf_op jit(solution)/shard_map/head_grad/dot_general | solution.py:18
  86.2 9.9 %all-to-all-done.2.pieces = bf16[64,16,512]{2,1,0:T(8,128)(2,1)S(1)} async-done(((bf16[64,16,512]{2,1,0:T(8,128)(2,1)}), bf16[64,16,512]{2,1,0:T(8,128)(2,1)S(1)}, u32[]{:S(2)}, u32[]{:S(2)}) %all-to-all-start.2) | async-done | bytes 1048608 | tf_op jit(solution)/shard_map/gather/all_to_all | solution.py:251
  96.1 1.8 %join_part.1 = f32[256,2048]{1,0:T(8,128)} custom-call(bf16[64,16,512]{2,1,0:T(8,128)(2,1)S(1)} %all-to-all-done.2.pieces), custom_call_target="tpu_custom_call" | custom-call | tf_op jit(solution)/shard_map/join_part/pallas_call | solution.py:214
  (2 shorter events, 0.0 us)
Async XLA Ops:
  0.6 1.6 %copy-start.1 = (bf16[256,2432]{1,0:T(8,128)(2,1)S(1)}, bf16[256,2432]{1,0:T(8,128)(2,1)}, u32[]{:S(2)}) copy-start(bf16[256,2432]{1,0:T(8,128)(2,1)} %target.5) | copy-start | bytes 3735556
  0.6 8.7 %collective-permute-start = (bf16[1024,2432]{1,0:T(8,128)(2,1)}, bf16[1024,2432]{1,0:T(8,128)(2,1)}, u32[]{:S(2)}, u32[]{:S(2)}) collective-permute-start(bf16[1024,2432]{1,0:T(8,128)(2,1)} %weight.3), channel_id=1, source_target_pairs={{0,64},{64,0},{1,65},{65,1},{2,66},{66,2},{3,67},{67,3},{4,68},{68... | collective-permute-start | bytes 14942216 | tf_op jit(solution)/shard_map/swap_weight/ppermute | solution.py:22
  2.2 2.4 %copy-start = (bf16[1024,2432]{1,0:T(8,128)(2,1)S(1)}, bf16[1024,2432]{1,0:T(8,128)(2,1)}, u32[]{:S(2)}) copy-start(bf16[1024,2432]{1,0:T(8,128)(2,1)} %weight.3) | copy-start | bytes 14942212
  9.3 31.2 %slice-start = ((s8[4980736]{0:T(1024)(128)(4,1)}), s8[4194304]{0:T(1024)(128)(4,1)S(1)}, s32[]{:S(2)}) async-start(s8[4980736]{0:T(1024)(128)(4,1)} %bitcast.6), calls=%async_computation.3 | async-start | bytes 8388608
  9.3 31.2 %slice-start.1 = ((s8[4980736]{0:T(1024)(128)(4,1)}), s8[786432]{0:T(1024)(128)(4,1)S(1)}, s32[]{:S(2)}) async-start(s8[4980736]{0:T(1024)(128)(4,1)} %bitcast.6), calls=%async_computation.4 | async-start | bytes 1572864
  45.9 1.0 copy-start.2
  46.9 30.7 %collective-permute-start.2 = (bf16[256,2432]{1,0:T(8,128)(2,1)S(1)}, bf16[256,2432]{1,0:T(8,128)(2,1)}, u32[]{:S(2)}, u32[]{:S(2)}) collective-permute-start(bf16[256,2432]{1,0:T(8,128)(2,1)S(1)} %get-tuple-element.16), channel_id=1, source_target_pairs={{0,64},{64,0},{1,65},{65,1},{2,66},{66,2},{3,67},{67,3},{4,68},{68... | collective-permute-start | bytes 3735560 | tf_op jit(solution)/shard_map/swap_dlogits/ppermute | solution.py:22
  46.9 24.5 %all-to-all-start.1 = ((bf16[64,16,512]{2,1,0:T(8,128)(2,1)}), bf16[64,16,512]{2,1,0:T(8,128)(2,1)S(1)}, u32[]{:S(2)}, u32[]{:S(2)}) async-start(bf16[64,16,512]{2,1,0:T(8,128)(2,1)} %copy-done.2), calls=%async_computation.1 | async-start | bytes 2097152 | tf_op jit(solution)/shard_map/scatter_sum/all_to_all | solution.py:248
  51.6 26.0 %collective-permute-start.1 = (bf16[256,1024]{1,0:T(8,128)(2,1)S(1)}, bf16[256,1024]{1,0:T(8,128)(2,1)}, u32[]{:S(2)}, u32[]{:S(2)}) collective-permute-start(bf16[256,1024]{1,0:T(8,128)(2,1)S(1)} %get-tuple-element.18.theirs), channel_id=1, source_target_pairs={{0,64},{64,0},{1,65},{65,1},{2,66},{66,2},{3,67},{67,3},{4,68},{68... | collective-permute-start | bytes 1572872 | tf_op jit(solution)/shard_map/swap_hidden/ppermute | solution.py:22
  72.6 23.4 %all-to-all-start.2 = ((bf16[64,16,512]{2,1,0:T(8,128)(2,1)}), bf16[64,16,512]{2,1,0:T(8,128)(2,1)S(1)}, u32[]{:S(2)}, u32[]{:S(2)}) async-start(bf16[64,16,512]{2,1,0:T(8,128)(2,1)} %sum_part.1), calls=%async_computation.2 | async-start | bytes 2097152 | tf_op jit(solution)/shard_map/gather/all_to_all | solution.py:251

commit v3 on v2

v3 whole, which is shorter than its diff:
```python
import functools
import math
import jax
import jax.numpy as jnp
from jax import lax
from jax.experimental import pallas as pl
from jax.experimental.pallas import tpu as pltpu
from jax.sharding import PartitionSpec as P

SWAP = ((0, 1), (1, 0))
TOKENS_PIECE = 16
COLS_PIECE = 512
BLOCK = 640
LOG2E = math.log2(math.e)
F32, BF16 = jnp.float32, jnp.bfloat16
VMEM = pl.BlockSpec(memory_space=pltpu.VMEM)
HBM = pl.BlockSpec(memory_space=pltpu.HBM)


def dot(a, b, ca, cb):
    return lax.dot_general(a, b, (((ca,), (cb,)), ((), ())), preferred_element_type=F32)


def swap(x):
    return lax.ppermute(x, "rows", SWAP)


def params(mib):
    return pltpu.CompilerParams(vmem_limit_bytes=mib * 1024 * 1024)


def cost(flops, moved):
    return pl.CostEstimate(flops=flops, bytes_accessed=moved, transcendentals=0)


def exp(x):
    return jnp.exp2(x * LOG2E)


def blocks(n):
    return [(c, min(c + BLOCK, n)) for c in range(0, n, BLOCK)]


def tiles(x):
    return [x[:, c : c + 128] for c in range(0, x.shape[1], 128)]


def own_kernel(mine, weight, target, acc, probs, stat):
    vocab = target.shape[1]
    for c, e in blocks(vocab):
        acc[:, c:e] = dot(mine[...], weight[:, c:e], 1, 0)
    wide = target[...].astype(F32)
    peak = jnp.max(wide, axis=1, keepdims=True)
    terms = exp(wide - peak)
    total = jnp.sum(terms, axis=1, keepdims=True)
    terms = terms / total
    probs[...] = terms
    mean = jnp.sum(terms * wide, axis=1, keepdims=True)
    lane = lax.broadcasted_iota(jnp.int32, stat.shape, 1)
    stat[...] = jnp.where(lane == 0, peak + jnp.log(total), mean)


def own_part(mine, weight, target):
    tokens, half = mine.shape
    vocab = target.shape[1]
    return pl.pallas_call(
        own_kernel,
        in_specs=[VMEM] * 3,
        out_specs=[VMEM] * 3,
        out_shape=[
            jax.ShapeDtypeStruct((tokens, vocab), F32),
            jax.ShapeDtypeStruct((tokens, vocab), F32),
            jax.ShapeDtypeStruct((tokens, 128), F32),
        ],
        compiler_params=params(24),
        cost_estimate=cost(2 * tokens * half * vocab, 2 * half * vocab),
        name="own_part",
    )(mine, weight, target)


def draft_kernel(theirs, acc, probs, stat, weight, draft, out, buffer, sems):
    tokens, vocab = draft.shape
    copies = []
    for j, (c, e) in enumerate(blocks(vocab)):
        part = pl.ds(c, e - c)
        copies.append(pltpu.make_async_copy(weight.at[:, part], buffer.at[:, part], sems.at[j]))
        copies[-1].start()
    peak = jnp.full((tokens, 128), -jnp.inf, F32)
    cross = jnp.zeros((tokens, 128), F32)
    for j, (c, e) in enumerate(blocks(vocab)):
        copies[j].wait()
        value = acc[:, c:e] + dot(theirs[...], buffer[:, c:e], 1, 0)
        draft[:, c:e] = value
        for tile, weighed in zip(tiles(value), tiles(probs[:, c:e] * value)):
            peak = jnp.maximum(peak, tile)
            cross = cross + weighed
    top = jnp.max(peak, axis=1, keepdims=True)
    total = jnp.zeros((tokens, 128), F32)
    for tile in tiles(draft[...]):
        total = total + exp(tile - top)
    lse_q = top + jnp.log(jnp.sum(total, axis=1, keepdims=True))
    mean = stat[:, 1:2] - jnp.sum(cross, axis=1, keepdims=True)
    lane = lax.broadcasted_iota(jnp.int32, stat.shape, 1)
    rows = jnp.where(lane == 0, stat[:, :1], jnp.where(lane == 1, mean, lse_q)).T
    for i in range(3):
        out[:, i * tokens : (i + 1) * tokens] = rows[i : i + 1]


def draft_part(theirs, acc, probs, stat, weight):
    tokens, half = theirs.shape
    vocab = acc.shape[1]
    return pl.pallas_call(
        draft_kernel,
        in_specs=[VMEM] * 4 + [HBM],
        out_specs=[VMEM] * 2,
        out_shape=[
            jax.ShapeDtypeStruct((tokens, vocab), F32),
            jax.ShapeDtypeStruct((1, 3 * tokens), F32),
        ],
        scratch_shapes=[pltpu.VMEM((half, vocab), BF16), pltpu.SemaphoreType.DMA((len(blocks(vocab)),))],
        compiler_params=params(24),
        cost_estimate=cost(2 * tokens * half * vocab, 2 * half * vocab),
        name="draft_part",
    )(theirs, acc, probs, stat, weight)


def back_kernel(factor, row, parts, draft, target, weight, weight_o, divergence, dlogits, out, stage, sems):
    half = weight.shape[0]
    per = half // COLS_PIECE
    tokens = draft.shape[0]
    each_t, mean, each_q = (parts[:, :, i * tokens : (i + 1) * tokens] for i in range(3))
    top_t, top_q = jnp.max(each_t, axis=0), jnp.max(each_q, axis=0)
    scale_t = exp(each_t - top_t)
    sum_t = jnp.sum(scale_t, axis=0)
    sum_q = jnp.sum(exp(each_q - top_q), axis=0)
    lse_t, lse_q = top_t + jnp.log(sum_t), top_q + jnp.log(sum_q)
    divergence[...] = jnp.sum(scale_t * mean, axis=0) / sum_t - lse_t + lse_q
    line = lax.broadcasted_iota(jnp.int32, (128, tokens), 0)
    turned = jnp.where(line == 0, lse_t, lse_q).T
    lse_t, lse_q = turned[:, :1], turned[:, 1:2]

    for c, e in blocks(draft.shape[1]):
        probs_q = exp(draft[:, c:e] - lse_q)
        probs_t = exp(target[:, c:e].astype(F32) - lse_t)
        dlogits[:, c:e] = ((probs_q - probs_t) * factor).astype(BF16)

    copies = []
    for j in range(2 * per):
        source = (weight, weight_o)[j // per]
        rows = source[j % per * COLS_PIECE : (j % per + 1) * COLS_PIECE]
        block = dot(dlogits[...], rows, 1, 1).astype(BF16)
        stage[j] = block.reshape(tokens // TOKENS_PIECE, TOKENS_PIECE, COLS_PIECE)
        place = lax.rem(row[0] * per + j, 2 * per)
        copies.append(pltpu.make_async_copy(stage.at[j], out.at[:, place], sems.at[j]))
        copies[-1].start()
    for copy in copies:
        copy.wait()


def back_part(factor, row, parts, draft, target, weight, weight_o):
    tokens, vocab = draft.shape
    half = weight.shape[0]
    down, across = tokens // TOKENS_PIECE, 2 * half // COLS_PIECE
    return pl.pallas_call(
        functools.partial(back_kernel, factor),
        in_specs=[pl.BlockSpec(memory_space=pltpu.SMEM)] + [VMEM] * 5,
        out_specs=[VMEM, VMEM, HBM],
        out_shape=[
            jax.ShapeDtypeStruct((1, tokens), F32),
            jax.ShapeDtypeStruct((tokens, vocab), BF16),
            jax.ShapeDtypeStruct((down, across, TOKENS_PIECE, COLS_PIECE), BF16),
        ],
        scratch_shapes=[
            pltpu.VMEM((across, down, TOKENS_PIECE, COLS_PIECE), BF16),
            pltpu.SemaphoreType.DMA((across,)),
        ],
        compiler_params=params(24),
        cost_estimate=cost(4 * tokens * half * vocab, 4 * half * vocab),
        name="back_part",
    )(row, parts, draft, target, weight, weight_o)


def sum_kernel(terms, out):
    total = terms[0].astype(F32)
    for i in range(1, terms.shape[0]):
        total = total + terms[i].astype(F32)
    out[...] = jnp.broadcast_to(total.astype(BF16)[None], out.shape)


def sum_part(terms):
    return pl.pallas_call(
        sum_kernel,
        in_specs=[VMEM],
        out_specs=VMEM,
        out_shape=jax.ShapeDtypeStruct(terms.shape, BF16),
        compiler_params=params(8),
        name="sum_part",
    )(terms)


def join_kernel(pieces, out, stage, sems):
    tokens, width = out.shape
    across = width // COLS_PIECE
    steps = sems.shape[0]
    copies = []
    for step in range(steps):
        rows = pl.ds(step * tokens // steps, tokens // steps)
        for i in range(step * pieces.shape[0] // steps, (step + 1) * pieces.shape[0] // steps):
            down = pl.ds(i // across * TOKENS_PIECE, TOKENS_PIECE)
            stage[down, pl.ds(i % across * COLS_PIECE, COLS_PIECE)] = pieces[i].astype(F32)
        copies.append(pltpu.make_async_copy(stage.at[rows], out.at[rows], sems.at[step]))
        copies[-1].start()
    for copy in copies:
        copy.wait()


def join_part(pieces, tokens, width):
    return pl.pallas_call(
        join_kernel,
        in_specs=[VMEM],
        out_specs=HBM,
        out_shape=jax.ShapeDtypeStruct((tokens, width), F32),
        scratch_shapes=[pltpu.VMEM((tokens, width), F32), pltpu.SemaphoreType.DMA((4,))],
        compiler_params=params(8),
        name="join_part",
    )(pieces)


def head_kernel(mine, mine_o, dlogits, dlogits_o, out):
    out[...] = dot(mine[...], dlogits[...], 0, 0) + dot(mine_o[...], dlogits_o[...], 0, 0)


def head_part(mine, mine_o, dlogits, dlogits_o):
    tokens, half = mine.shape
    vocab = dlogits.shape[1]
    step = 128
    column = pl.BlockSpec((tokens, step), lambda j: (0, j))
    return pl.pallas_call(
        head_kernel,
        grid=(half // step,),
        in_specs=[column, column, VMEM, VMEM],
        out_specs=pl.BlockSpec((step, vocab), lambda j: (j, 0)),
        out_shape=jax.ShapeDtypeStruct((half, vocab), F32),
        compiler_params=params(16),
        cost_estimate=cost(4 * tokens * half * vocab, 4 * half * vocab),
        name="head_part",
    )(mine, mine_o, dlogits, dlogits_o)


def shards(hidden, weight, target):
    n = lax.axis_size("vocab")
    row = lax.axis_index("rows")
    tokens, width = hidden.shape
    half, vocab = weight.shape

    with jax.named_scope("swap_weight"):
        weight_o = swap(weight)
    mine = lax.dynamic_slice_in_dim(hidden, row * half, half, 1)
    theirs = lax.dynamic_slice_in_dim(hidden, (1 - row) * half, half, 1)
    with jax.named_scope("swap_hidden"):
        mine_o = swap(theirs)

    acc, probs, stat = own_part(mine, weight, target)
    draft, part = draft_part(theirs, acc, probs, stat, weight_o)
    with jax.named_scope("share_stats"):
        parts = lax.all_to_all(jnp.broadcast_to(part[None], (n,) + part.shape), "vocab", 0, 0)
    divergence, dlogits, pieces = back_part(
        vocab * n / 1024.0, jnp.full((1,), row, jnp.int32), parts, draft, target, weight, weight_o
    )
    with jax.named_scope("swap_dlogits"):
        dlogits_o = swap(dlogits)
    with jax.named_scope("scatter_sum"):
        terms = lax.all_to_all(pieces.reshape(n, TOKENS_PIECE, COLS_PIECE), "vocab", 0, 0)
    totals = sum_part(terms)
    with jax.named_scope("gather"):
        gathered = lax.all_to_all(totals, "vocab", 0, 0)
    hidden_grad = join_part(gathered, tokens, width)
    head_grad = head_part(mine, mine_o, dlogits, dlogits_o)
    return (divergence.reshape(tokens), hidden_grad, head_grad)


def solution(mesh):
    return jax.shard_map(
        shards,
        mesh=mesh,
        in_specs=(P("rows", None), P("rows", "vocab"), P("rows", "vocab")),
        out_specs=(P("rows"), P("rows", None), P("rows", "vocab")),
        check_vma=False,
    )
```

time: 98.3 us -> 96.5 us (0.982)
  matrix products: 8.56 us -> 0 us
  Pallas kernels: 18.3 us -> 24.5 us
  local copies, waits for them, and re-layouts: 4.91 us -> 10.5 us
  blocking collectives: 25 us -> 21.6 us
  waiting for transfers between devices: 30.1 us -> 28.8 us
    dot_general x2 -> x0, matrix products: 8.56 us -> none  [dot(): lax.dot_general(a, b, (((ca,), (cb,)), ((), ())), preferred_element_type=...]
    unnamed x10 -> x12, local copies, waits for them, and re-layouts: 3.53 us -> 9.08 us
    pallas_call x4 -> x5, Pallas kernels: 13 us -> 17.2 us  [the longest x1 8.3 us: head_part(): pl.pallas_call(head_kernel, grid=(half // step,), in_specs=[column, colum...]
    all_to_all x1, blocking collectives: 25 us -> 21.6 us  [shards(): lax.all_to_all(jnp.broadcast_to(part[None], (n,) + part.shape), 'vocab',...]
    ppermute x3, waiting for transfers between devices: 0.95 us -> 4.33 us  [swap(): return lax.ppermute(x, 'rows', SWAP)]
    all_to_all x1, waiting for transfers between devices: 9.87 us -> 6.49 us  [shards(): gathered = lax.all_to_all(totals, 'vocab', 0, 0)]
    pallas_call x1, Pallas kernels: 5.37 us -> 7.23 us  [back_part(): pl.pallas_call(functools.partial(back_kernel, factor), in_specs=[pl.Block...]
    all_to_all x1, waiting for transfers between devices: 19.3 us -> 18 us  [shards(): lax.all_to_all(pieces.reshape(n, TOKENS_PIECE, COLS_PIECE), 'vocab', 0, 0)]
  transfers between devices with their start and end apart: 5 -> 5, of which waited for: 3 -> 4; matrix products, arithmetic and copies ran while one was open for 10% -> 1% of each run, Pallas kernels for 5% -> 12%
where the time goes in v3:
time: 96.5 us; the launch traced here: 95.9 us
  waiting for transfers between devices  28.8 us (30%)
  Pallas kernels  24.5 us (25%)
  blocking collectives  21.6 us (22%)
  local copies, waits for them, and re-layouts  10.5 us (11%)
  starting transfers between devices  9.81 us (10%)
    all_to_all x1, blocking collectives, shards(): lax.all_to_all(jnp.broadcast_to(part[None], (n,) + part.shape), 'vocab',...  21.6 us
    all_to_all x1, waiting for transfers between devices, shards(): lax.all_to_all(pieces.reshape(n, TOKENS_PIECE, COLS_PIECE), 'vocab', 0, 0)  18 us
    unnamed x12, local copies, waits for them, and re-layouts  9.08 us
    pallas_call x1, Pallas kernels, head_part(): pl.pallas_call(head_kernel, grid=(half // step,), in_specs=[column, colum...  8.3 us
    pallas_call x1, Pallas kernels, back_part(): pl.pallas_call(functools.partial(back_kernel, factor), in_specs=[pl.Block...  7.23 us
    all_to_all x1, waiting for transfers between devices, shards(): gathered = lax.all_to_all(totals, 'vocab', 0, 0)  6.49 us
    all_to_all x1, starting transfers between devices, shards(): lax.all_to_all(pieces.reshape(n, TOKENS_PIECE, COLS_PIECE), 'vocab', 0, 0)  4.9 us
    all_to_all x1, starting transfers between devices, shards(): gathered = lax.all_to_all(totals, 'vocab', 0, 0)  4.65 us
  transfers between devices with their start and end apart: 5, of which 4 were waited for; matrix products, arithmetic and copies ran while one was open for 1% of the time, Pallas kernels for 12%

profile of v3, /device:TPU:0, one launch (start us, length us, event | category | flops | bytes accessed | tf_op | source)
XLA Modules:
  0.0 95.9 jit_solution(2785320812149681251)
XLA Ops:
  0.6 0.0 copy-start.2
  0.6 0.1 collective-permute-start
  0.7 1.4 %constant_dynamic-slice_fusion = (bf16[256,1024]{1,0:T(8,128)(2,1)S(1)}, bf16[256,1024]{1,0:T(8,128)(2,1)S(1)}) fusion(bf16[256,2048]{1,0:T(8,128)(2,1)} %param.3, s32[]{:T(128)S(6)} %select_n.7, s32[]{:T(128)S(6)} %select_n.6), kind=kLoop, calls=%fused_computation | loop fusion | bytes 2097160 | tf_op jit(solution)/shard_map/dynamic_slice | solution.py:258
  2.1 0.1 copy-done.2
  2.2 0.0 copy-start
  2.2 2.4 %copy-done = bf16[1024,2432]{1,0:T(8,128)(2,1)S(1)} copy-done((bf16[1024,2432]{1,0:T(8,128)(2,1)S(1)}, bf16[1024,2432]{1,0:T(8,128)(2,1)}, u32[]{:S(2)}) %copy-start) | copy-done | bytes 4980760
  4.7 2.3 %own_part.1 = (f32[256,2432]{1,0:T(8,128)S(1)}, f32[256,2432]{1,0:T(8,128)S(1)}, f32[256,128]{1,0:T(8,128)S(1)}) custom-call(bf16[256,1024]{1,0:T(8,128)(2,1)S(1)} %get-tuple-element.19.mine, bf16[1024,2432]{1,0:T(8,128)(2,1)S(1)} %copy-done, bf16[256,2432]{1,0:T(8,128)(2,1)S(1)} %copy-done.2), custom_call_target="tpu_custom_call" | custom-call | flops 1275068416 | bytes 4980736 | tf_op jit(solution)/shard_map/own_part/pallas_call | solution.py:66
  6.9 2.4 %collective-permute-done.weight.weight_o = bf16[1024,2432]{1,0:T(8,128)(2,1)} collective-permute-done((bf16[1024,2432]{1,0:T(8,128)(2,1)}, bf16[1024,2432]{1,0:T(8,128)(2,1)}, u32[]{:S(2)}, u32[]{:S(2)}) %collective-permute-start) | collective-permute-done | bytes 4980768 | tf_op jit(solution)/shard_map/swap_weight/ppermute | solution.py:25
  9.3 4.1 %draft_part.1 = (f32[256,2432]{1,0:T(8,128)S(1)}, f32[1,768]{1,0:T(1,128)S(1)}) custom-call(bf16[256,1024]{1,0:T(8,128)(2,1)S(1)} %get-tuple-element.20.theirs, f32[256,2432]{1,0:T(8,128)S(1)} %get-tuple-element.11.acc, f32[256,2432]{1,0:T(8,128)S(1)} %get-tuple-element.12.probs, f32[256,128]{1,0:T(8,128)S(1)} %get-tuple-element.13.stat, ...), custom_call_target="tpu_custom_call" | custom-call | flops 1275068416 | bytes 4980736 | tf_op jit(solution)/shard_map/draft_part/pallas_call | solution.py:112
  13.4 0.0 copy-start.3
  13.4 1.4 %copy-done.3 = f32[256,2432]{1,0:T(8,128)} copy-done((f32[256,2432]{1,0:T(8,128)}, f32[256,2432]{1,0:T(8,128)S(1)}, u32[]{:S(2)}) %copy-start.3) | copy-done | bytes 2490392
  14.9 0.1 broadcast_in_dim.13
  15.0 21.6 %all_to_all.15.parts = f32[64,1,768]{2,1,0:T(1,128)S(1)} all-to-all(f32[64,1,768]{2,1,0:T(1,128)S(1)} %broadcast_in_dim.13), channel_id=1, replica_groups=mesh['rows'=2,'vocab'=64] {'vocab'}, dimensions={0} | all-to-all | bytes 393216 | tf_op jit(solution)/shard_map/share_stats/all_to_all | solution.py:266
  36.6 0.0 copy-start.1
  36.6 2.4 %copy-done.1 = bf16[1024,2432]{1,0:T(8,128)(2,1)S(1)} copy-done((bf16[1024,2432]{1,0:T(8,128)(2,1)S(1)}, bf16[1024,2432]{1,0:T(8,128)(2,1)}, u32[]{:S(2)}) %copy-start.1) | copy-done | bytes 4980760
  39.0 0.0 copy-start.4
  39.0 1.7 %copy-done.4 = f32[256,2432]{1,0:T(8,128)S(1)} copy-done((f32[256,2432]{1,0:T(8,128)S(1)}, f32[256,2432]{1,0:T(8,128)}, u32[]{:S(2)}) %copy-start.4) | copy-done | bytes 2490392
  40.7 7.2 %back_part.1 = (f32[1,256]{1,0:T(1,128)}, bf16[256,2432]{1,0:T(8,128)(2,1)S(1)}, bf16[16,4,16,512]{3,2,1,0:T(8,128)(2,1)S(1)}) custom-call(s32[1]{0:T(128)} %bitcast.row, f32[64,1,768]{2,1,0:T(1,128)S(1)} %all_to_all.15.parts, f32[256,2432]{1,0:T(8,128)S(1)} %copy-done.4, bf16[256,2432]{1,0:T(8,128)(2,1)S(1)} %copy-done.2, bf16[1024,2432]{1,0:T(8,128)(2,1)S(1)} %copy-done.1, ...), custom_call_target="tpu_custom_call" | custom-call | flops 2550136832 | bytes 9961472 | tf_op jit(solution)/shard_map/back_part/pallas_call | solution.py:164
  47.9 0.0 copy-start.5
  47.9 1.0 %copy-done.5 = bf16[16,4,16,512]{3,2,1,0:T(8,128)(2,1)} copy-done((bf16[16,4,16,512]{3,2,1,0:T(8,128)(2,1)}, bf16[16,4,16,512]{3,2,1,0:T(8,128)(2,1)S(1)}, u32[]{:S(2)}) %copy-start.5) | copy-done | bytes 1048600
  48.9 4.9 %all-to-all-start.1 = ((bf16[64,16,512]{2,1,0:T(8,128)(2,1)}), bf16[64,16,512]{2,1,0:T(8,128)(2,1)S(1)}, u32[]{:S(2)}, u32[]{:S(2)}) async-start(bf16[64,16,512]{2,1,0:T(8,128)(2,1)} %bitcast.3), calls=%async_computation.1 | async-start | bytes 2097152 | tf_op jit(solution)/shard_map/scatter_sum/all_to_all | solution.py:273
  53.8 0.1 collective-permute-start.2
  53.9 18.0 %all-to-all-done.1.terms = bf16[64,16,512]{2,1,0:T(8,128)(2,1)S(1)} async-done(((bf16[64,16,512]{2,1,0:T(8,128)(2,1)}), bf16[64,16,512]{2,1,0:T(8,128)(2,1)S(1)}, u32[]{:S(2)}, u32[]{:S(2)}) %all-to-all-start.1) | async-done | bytes 1048608 | tf_op jit(solution)/shard_map/scatter_sum/all_to_all | solution.py:273
  71.9 1.2 %sum_part.1 = bf16[64,16,512]{2,1,0:T(8,128)(2,1)} custom-call(bf16[64,16,512]{2,1,0:T(8,128)(2,1)S(1)} %all-to-all-done.1.terms), custom_call_target="tpu_custom_call" | custom-call | tf_op jit(solution)/shard_map/sum_part/pallas_call | solution.py:191
  73.1 4.7 %all-to-all-start.2 = ((bf16[64,16,512]{2,1,0:T(8,128)(2,1)}), bf16[64,16,512]{2,1,0:T(8,128)(2,1)S(1)}, u32[]{:S(2)}, u32[]{:S(2)}) async-start(bf16[64,16,512]{2,1,0:T(8,128)(2,1)} %sum_part.1), calls=%async_computation.2 | async-start | bytes 2097152 | tf_op jit(solution)/shard_map/gather/all_to_all | solution.py:276
  77.8 0.1 collective-permute-start.1
  77.8 1.9 %collective-permute-done.1.mine_o = bf16[256,1024]{1,0:T(8,128)(2,1)S(1)} collective-permute-done((bf16[256,1024]{1,0:T(8,128)(2,1)S(1)}, bf16[256,1024]{1,0:T(8,128)(2,1)S(1)}, u32[]{:S(2)}, u32[]{:S(2)}) %collective-permute-start.1) | collective-permute-done | bytes 524320 | tf_op jit(solution)/shard_map/swap_hidden/ppermute | solution.py:25
  79.7 0.0 collective-permute-done.2.dlogits_o
  79.7 8.3 %head_part.1 = f32[1024,2432]{1,0:T(8,128)} custom-call(bf16[256,1024]{1,0:T(8,128)(2,1)S(1)} %get-tuple-element.19.mine, bf16[256,1024]{1,0:T(8,128)(2,1)S(1)} %collective-permute-done.1.mine_o, bf16[256,2432]{1,0:T(8,128)(2,1)S(1)} %get-tuple-element.18.dlogits, bf16[256,2432]{1,0:T(8,128)(2,1)} %collective-permute-done.2.dlogits_o), custom_call_target="tpu_custom_call" | custom-call | flops 2550136832 | bytes 9961472 | tf_op jit(solution)/shard_map/head_part/pallas_call | solution.py:238
  88.1 6.5 %all-to-all-done.2.pieces = bf16[64,16,512]{2,1,0:T(8,128)(2,1)S(1)} async-done(((bf16[64,16,512]{2,1,0:T(8,128)(2,1)}), bf16[64,16,512]{2,1,0:T(8,128)(2,1)S(1)}, u32[]{:S(2)}, u32[]{:S(2)}) %all-to-all-start.2) | async-done | bytes 1048608 | tf_op jit(solution)/shard_map/gather/all_to_all | solution.py:276
  94.5 1.4 %join_part.1 = f32[256,2048]{1,0:T(8,128)} custom-call(bf16[64,16,512]{2,1,0:T(8,128)(2,1)S(1)} %all-to-all-done.2.pieces), custom_call_target="tpu_custom_call" | custom-call | tf_op jit(solution)/shard_map/join_part/pallas_call | solution.py:218
  (1 shorter events, 0.0 us)
Async XLA Ops:
  0.6 1.6 %copy-start.2 = (bf16[256,2432]{1,0:T(8,128)(2,1)S(1)}, bf16[256,2432]{1,0:T(8,128)(2,1)}, u32[]{:S(2)}) copy-start(bf16[256,2432]{1,0:T(8,128)(2,1)} %target.3) | copy-start | bytes 3735556
  0.6 8.7 %collective-permute-start = (bf16[1024,2432]{1,0:T(8,128)(2,1)}, bf16[1024,2432]{1,0:T(8,128)(2,1)}, u32[]{:S(2)}, u32[]{:S(2)}) collective-permute-start(bf16[1024,2432]{1,0:T(8,128)(2,1)} %weight.3), channel_id=1, source_target_pairs={{0,64},{64,0},{1,65},{65,1},{2,66},{66,2},{3,67},{67,3},{4,68},{68... | collective-permute-start | bytes 14942216 | tf_op jit(solution)/shard_map/swap_weight/ppermute | solution.py:25
  2.2 2.4 %copy-start = (bf16[1024,2432]{1,0:T(8,128)(2,1)S(1)}, bf16[1024,2432]{1,0:T(8,128)(2,1)}, u32[]{:S(2)}) copy-start(bf16[1024,2432]{1,0:T(8,128)(2,1)} %weight.3) | copy-start | bytes 14942212
  13.4 1.5 %copy-start.3 = (f32[256,2432]{1,0:T(8,128)}, f32[256,2432]{1,0:T(8,128)S(1)}, u32[]{:S(2)}) copy-start(f32[256,2432]{1,0:T(8,128)S(1)} %get-tuple-element.15.draft) | copy-start | bytes 7471108
  36.6 2.4 %copy-start.1 = (bf16[1024,2432]{1,0:T(8,128)(2,1)S(1)}, bf16[1024,2432]{1,0:T(8,128)(2,1)}, u32[]{:S(2)}) copy-start(bf16[1024,2432]{1,0:T(8,128)(2,1)} %weight.3) | copy-start | bytes 14942212
  39.0 1.7 %copy-start.4 = (f32[256,2432]{1,0:T(8,128)S(1)}, f32[256,2432]{1,0:T(8,128)}, u32[]{:S(2)}) copy-start(f32[256,2432]{1,0:T(8,128)} %copy-done.3) | copy-start | bytes 7471108
  47.9 1.0 %copy-start.5 = (bf16[16,4,16,512]{3,2,1,0:T(8,128)(2,1)}, bf16[16,4,16,512]{3,2,1,0:T(8,128)(2,1)S(1)}, u32[]{:S(2)}) copy-start(bf16[16,4,16,512]{3,2,1,0:T(8,128)(2,1)S(1)} %get-tuple-element.17) | copy-start | bytes 3145732
  48.9 23.0 %all-to-all-start.1 = ((bf16[64,16,512]{2,1,0:T(8,128)(2,1)}), bf16[64,16,512]{2,1,0:T(8,128)(2,1)S(1)}, u32[]{:S(2)}, u32[]{:S(2)}) async-start(bf16[64,16,512]{2,1,0:T(8,128)(2,1)} %bitcast.3), calls=%async_computation.1 | async-start | bytes 2097152 | tf_op jit(solution)/shard_map/scatter_sum/all_to_all | solution.py:273
  53.8 25.9 %collective-permute-start.2 = (bf16[256,2432]{1,0:T(8,128)(2,1)S(1)}, bf16[256,2432]{1,0:T(8,128)(2,1)}, u32[]{:S(2)}, u32[]{:S(2)}) collective-permute-start(bf16[256,2432]{1,0:T(8,128)(2,1)S(1)} %get-tuple-element.18.dlogits), channel_id=1, source_target_pairs={{0,64},{64,0},{1,65},{65,1},{2,66},{66,2},{3,67},{67,3},{4,68},{68... | collective-permute-start | bytes 3735560 | tf_op jit(solution)/shard_map/swap_dlogits/ppermute | solution.py:25
  73.1 21.4 %all-to-all-start.2 = ((bf16[64,16,512]{2,1,0:T(8,128)(2,1)}), bf16[64,16,512]{2,1,0:T(8,128)(2,1)S(1)}, u32[]{:S(2)}, u32[]{:S(2)}) async-start(bf16[64,16,512]{2,1,0:T(8,128)(2,1)} %sum_part.1), calls=%async_computation.2 | async-start | bytes 2097152 | tf_op jit(solution)/shard_map/gather/all_to_all | solution.py:276
  77.8 2.0 %collective-permute-start.1 = (bf16[256,1024]{1,0:T(8,128)(2,1)S(1)}, bf16[256,1024]{1,0:T(8,128)(2,1)S(1)}, u32[]{:S(2)}, u32[]{:S(2)}) collective-permute-start(bf16[256,1024]{1,0:T(8,128)(2,1)S(1)} %get-tuple-element.20.theirs), channel_id=1, source_target_pairs={{0,64},{64,0},{1,65},{65,1},{2,66},{66,2},{3,67},{67,3},{4,68},{68... | collective-permute-start | bytes 1572872 | tf_op jit(solution)/shard_map/swap_hidden/ppermute | solution.py:25

commit v4 on v3

--- a/solution.py
+++ b/solution.py
@@ -11,10 +11,12 @@
 TOKENS_PIECE = 16
 COLS_PIECE = 512
 BLOCK = 640
+AHEAD = 2
 LOG2E = math.log2(math.e)
 F32, BF16 = jnp.float32, jnp.bfloat16
 VMEM = pl.BlockSpec(memory_space=pltpu.VMEM)
 HBM = pl.BlockSpec(memory_space=pltpu.HBM)
+ANY = pl.BlockSpec(memory_space=pl.ANY)
 
 
 def dot(a, b, ca, cb):
@@ -78,25 +80,31 @@
     )(mine, weight, target)
 
 
-def draft_kernel(theirs, acc, probs, stat, weight, draft, out, buffer, sems):
-    tokens, vocab = draft.shape
-    copies = []
+def draft_kernel(theirs, acc, probs, stat, weight, draft, out, buffer, stage, sems, out_sems):
+    tokens, vocab = stage.shape
+    copies, results = [], []
     for j, (c, e) in enumerate(blocks(vocab)):
         part = pl.ds(c, e - c)
         copies.append(pltpu.make_async_copy(weight.at[:, part], buffer.at[:, part], sems.at[j]))
-        copies[-1].start()
+    for copy in copies[:AHEAD]:
+        copy.start()
     peak = jnp.full((tokens, 128), -jnp.inf, F32)
     cross = jnp.zeros((tokens, 128), F32)
     for j, (c, e) in enumerate(blocks(vocab)):
         copies[j].wait()
+        for copy in copies[j + AHEAD : j + AHEAD + 1]:
+            copy.start()
         value = acc[:, c:e] + dot(theirs[...], buffer[:, c:e], 1, 0)
-        draft[:, c:e] = value
+        stage[:, c:e] = value
+        part = pl.ds(c, e - c)
+        results.append(pltpu.make_async_copy(stage.at[:, part], draft.at[:, part], out_sems.at[j]))
+        results[-1].start()
         for tile, weighed in zip(tiles(value), tiles(probs[:, c:e] * value)):
             peak = jnp.maximum(peak, tile)
             cross = cross + weighed
     top = jnp.max(peak, axis=1, keepdims=True)
     total = jnp.zeros((tokens, 128), F32)
-    for tile in tiles(draft[...]):
+    for tile in tiles(stage[...]):
         total = total + exp(tile - top)
     lse_q = top + jnp.log(jnp.sum(total, axis=1, keepdims=True))
     mean = stat[:, 1:2] - jnp.sum(cross, axis=1, keepdims=True)
@@ -104,30 +112,48 @@
     rows = jnp.where(lane == 0, stat[:, :1], jnp.where(lane == 1, mean, lse_q)).T
     for i in range(3):
         out[:, i * tokens : (i + 1) * tokens] = rows[i : i + 1]
+    for result in results:
+        result.wait()
 
 
 def draft_part(theirs, acc, probs, stat, weight):
     tokens, half = theirs.shape
     vocab = acc.shape[1]
+    steps = len(blocks(vocab))
     return pl.pallas_call(
         draft_kernel,
-        in_specs=[VMEM] * 4 + [HBM],
-        out_specs=[VMEM] * 2,
+        in_specs=[VMEM] * 4 + [ANY],
+        out_specs=[ANY, VMEM],
         out_shape=[
             jax.ShapeDtypeStruct((tokens, vocab), F32),
             jax.ShapeDtypeStruct((1, 3 * tokens), F32),
         ],
-        scratch_shapes=[pltpu.VMEM((half, vocab), BF16), pltpu.SemaphoreType.DMA((len(blocks(vocab)),))],
-        compiler_params=params(24),
+        scratch_shapes=[
+            pltpu.VMEM((half, vocab), BF16),
+            pltpu.VMEM((tokens, vocab), F32),
+            pltpu.SemaphoreType.DMA((steps,)),
+            pltpu.SemaphoreType.DMA((steps,)),
+        ],
+        compiler_params=params(20),
         cost_estimate=cost(2 * tokens * half * vocab, 2 * half * vocab),
         name="draft_part",
     )(theirs, acc, probs, stat, weight)
 
 
-def back_kernel(factor, row, parts, draft, target, weight, weight_o, divergence, dlogits, out, stage, sems):
+def back_kernel(
+    factor, row, parts, draft, target, weight, weight_o, divergence, dlogits, out, buffer, stage, sems, out_sems
+):
     half = weight.shape[0]
     per = half // COLS_PIECE
     tokens = draft.shape[0]
+    down = tokens // TOKENS_PIECE
+    loads, copies = [], []
+    for j in range(2 * per):
+        source = (weight, weight_o)[j // per].at[pl.ds(j % per * COLS_PIECE, COLS_PIECE)]
+        loads.append(pltpu.make_async_copy(source, buffer.at[j], sems.at[j]))
+    for load in loads[:AHEAD]:
+        load.start()
+
     each_t, mean, each_q = (parts[:, :, i * tokens : (i + 1) * tokens] for i in range(3))
     top_t, top_q = jnp.max(each_t, axis=0), jnp.max(each_q, axis=0)
     scale_t = exp(each_t - top_t)
@@ -144,14 +170,14 @@
         probs_t = exp(target[:, c:e].astype(F32) - lse_t)
         dlogits[:, c:e] = ((probs_q - probs_t) * factor).astype(BF16)
 
-    copies = []
     for j in range(2 * per):
-        source = (weight, weight_o)[j // per]
-        rows = source[j % per * COLS_PIECE : (j % per + 1) * COLS_PIECE]
-        block = dot(dlogits[...], rows, 1, 1).astype(BF16)
-        stage[j] = block.reshape(tokens // TOKENS_PIECE, TOKENS_PIECE, COLS_PIECE)
+        loads[j].wait()
+        for load in loads[j + AHEAD : j + AHEAD + 1]:
+            load.start()
+        block = dot(dlogits[...], buffer[j], 1, 1).astype(BF16)
+        stage[j] = block.reshape(down, TOKENS_PIECE, COLS_PIECE)
         place = lax.rem(row[0] * per + j, 2 * per)
-        copies.append(pltpu.make_async_copy(stage.at[j], out.at[:, place], sems.at[j]))
+        copies.append(pltpu.make_async_copy(stage.at[j], out.at[pl.ds(place * down, down)], out_sems.at[j]))
         copies[-1].start()
     for copy in copies:
         copy.wait()
@@ -163,15 +189,17 @@
     down, across = tokens // TOKENS_PIECE, 2 * half // COLS_PIECE
     return pl.pallas_call(
         functools.partial(back_kernel, factor),
-        in_specs=[pl.BlockSpec(memory_space=pltpu.SMEM)] + [VMEM] * 5,
-        out_specs=[VMEM, VMEM, HBM],
+        in_specs=[pl.BlockSpec(memory_space=pltpu.SMEM)] + [VMEM] * 3 + [ANY] * 2,
+        out_specs=[VMEM, VMEM, ANY],
         out_shape=[
             jax.ShapeDtypeStruct((1, tokens), F32),
             jax.ShapeDtypeStruct((tokens, vocab), BF16),
-            jax.ShapeDtypeStruct((down, across, TOKENS_PIECE, COLS_PIECE), BF16),
+            jax.ShapeDtypeStruct((down * across, TOKENS_PIECE, COLS_PIECE), BF16),
         ],
         scratch_shapes=[
+            pltpu.VMEM((across, COLS_PIECE, vocab), BF16),
             pltpu.VMEM((across, down, TOKENS_PIECE, COLS_PIECE), BF16),
+            pltpu.SemaphoreType.DMA((across,)),
             pltpu.SemaphoreType.DMA((across,)),
         ],
         compiler_params=params(24),
@@ -200,14 +228,15 @@
 
 def join_kernel(pieces, out, stage, sems):
     tokens, width = out.shape
-    across = width // COLS_PIECE
+    down = tokens // TOKENS_PIECE
     steps = sems.shape[0]
     copies = []
     for step in range(steps):
         rows = pl.ds(step * tokens // steps, tokens // steps)
-        for i in range(step * pieces.shape[0] // steps, (step + 1) * pieces.shape[0] // steps):
-            down = pl.ds(i // across * TOKENS_PIECE, TOKENS_PIECE)
-            stage[down, pl.ds(i % across * COLS_PIECE, COLS_PIECE)] = pieces[i].astype(F32)
+        for i in range(step * down // steps, (step + 1) * down // steps):
+            for j in range(width // COLS_PIECE):
+                place = pl.ds(i * TOKENS_PIECE, TOKENS_PIECE), pl.ds(j * COLS_PIECE, COLS_PIECE)
+                stage[place] = pieces[j * down + i].astype(F32)
         copies.append(pltpu.make_async_copy(stage.at[rows], out.at[rows], sems.at[step]))
         copies[-1].start()
     for copy in copies:
@@ -270,7 +299,7 @@
     with jax.named_scope("swap_dlogits"):
         dlogits_o = swap(dlogits)
     with jax.named_scope("scatter_sum"):
-        terms = lax.all_to_all(pieces.reshape(n, TOKENS_PIECE, COLS_PIECE), "vocab", 0, 0)
+        terms = lax.all_to_all(pieces, "vocab", 0, 0)
     totals = sum_part(terms)
     with jax.named_scope("gather"):
         gathered = lax.all_to_all(totals, "vocab", 0, 0)

time: 96.5 us -> 96.1 us (level)
    pallas_call x1, Pallas kernels: 7.23 us -> 6.13 us  [back_part(): pl.pallas_call(functools.partial(back_kernel, factor), in_specs=[pl.Block...]
where the time goes in v4:
time: 96.1 us; the launch traced here: 95.5 us
  waiting for transfers between devices  28.8 us (30%)
  Pallas kernels  24.1 us (25%)
  blocking collectives  21.6 us (22%)
  local copies, waits for them, and re-layouts  10.5 us (11%)
  starting transfers between devices  9.82 us (10%)
    all_to_all x1, blocking collectives, shards(): lax.all_to_all(jnp.broadcast_to(part[None], (n,) + part.shape), 'vocab',...  21.6 us
    all_to_all x1, waiting for transfers between devices, shards(): terms = lax.all_to_all(pieces, 'vocab', 0, 0)  18 us
    unnamed x12, local copies, waits for them, and re-layouts  9.08 us
    pallas_call x1, Pallas kernels, head_part(): pl.pallas_call(head_kernel, grid=(half // step,), in_specs=[column, colum...  8.3 us
    all_to_all x1, waiting for transfers between devices, shards(): gathered = lax.all_to_all(totals, 'vocab', 0, 0)  6.48 us
    pallas_call x1, Pallas kernels, back_part(): pl.pallas_call(functools.partial(back_kernel, factor), in_specs=[pl.Block...  6.13 us
    all_to_all x1, starting transfers between devices, shards(): terms = lax.all_to_all(pieces, 'vocab', 0, 0)  4.9 us
    pallas_call x1, Pallas kernels, draft_part(): pl.pallas_call(draft_kernel, in_specs=[VMEM] * 4 + [ANY], out_specs=[ANY,...  4.78 us
  transfers between devices with their start and end apart: 5, of which 4 were waited for; matrix products, arithmetic and copies ran while one was open for 1% of the time, Pallas kernels for 12%

profile of v4, /device:TPU:0, one launch (start us, length us, event | category | flops | bytes accessed | tf_op | source)
XLA Modules:
  0.0 95.5 jit_solution(17913469148399848355)
XLA Ops:
  0.6 0.0 copy-start.2
  0.6 0.1 collective-permute-start
  0.7 1.4 %constant_dynamic-slice_fusion = (bf16[256,1024]{1,0:T(8,128)(2,1)S(1)}, bf16[256,1024]{1,0:T(8,128)(2,1)S(1)}) fusion(bf16[256,2048]{1,0:T(8,128)(2,1)} %param.3, s32[]{:T(128)S(6)} %select_n.7, s32[]{:T(128)S(6)} %select_n.6), kind=kLoop, calls=%fused_computation | loop fusion | bytes 2097160 | tf_op jit(solution)/shard_map/dynamic_slice | solution.py:287
  2.1 0.1 copy-done.2
  2.2 0.0 copy-start
  2.2 2.4 %copy-done = bf16[1024,2432]{1,0:T(8,128)(2,1)S(1)} copy-done((bf16[1024,2432]{1,0:T(8,128)(2,1)S(1)}, bf16[1024,2432]{1,0:T(8,128)(2,1)}, u32[]{:S(2)}) %copy-start) | copy-done | bytes 4980760
  4.7 2.3 %own_part.1 = (f32[256,2432]{1,0:T(8,128)S(1)}, f32[256,2432]{1,0:T(8,128)S(1)}, f32[256,128]{1,0:T(8,128)S(1)}) custom-call(bf16[256,1024]{1,0:T(8,128)(2,1)S(1)} %get-tuple-element.19.mine, bf16[1024,2432]{1,0:T(8,128)(2,1)S(1)} %copy-done, bf16[256,2432]{1,0:T(8,128)(2,1)S(1)} %copy-done.2), custom_call_target="tpu_custom_call" | custom-call | flops 1275068416 | bytes 4980736 | tf_op jit(solution)/shard_map/own_part/pallas_call | solution.py:68
  6.9 2.4 %collective-permute-done.weight.weight_o = bf16[1024,2432]{1,0:T(8,128)(2,1)} collective-permute-done((bf16[1024,2432]{1,0:T(8,128)(2,1)}, bf16[1024,2432]{1,0:T(8,128)(2,1)}, u32[]{:S(2)}, u32[]{:S(2)}) %collective-permute-start) | collective-permute-done | bytes 4980768 | tf_op jit(solution)/shard_map/swap_weight/ppermute | solution.py:27
  9.3 4.8 %draft_part.1 = (f32[256,2432]{1,0:T(8,128)S(1)}, f32[1,768]{1,0:T(1,128)S(1)}) custom-call(bf16[256,1024]{1,0:T(8,128)(2,1)S(1)} %get-tuple-element.20.theirs, f32[256,2432]{1,0:T(8,128)S(1)} %get-tuple-element.11.acc, f32[256,2432]{1,0:T(8,128)S(1)} %get-tuple-element.12.probs, f32[256,128]{1,0:T(8,128)S(1)} %get-tuple-element.13.stat, ...), custom_call_target="tpu_custom_call" | custom-call | flops 1275068416 | bytes 4980736 | tf_op jit(solution)/shard_map/draft_part/pallas_call | solution.py:123
  14.1 0.0 copy-start.3
  14.1 1.4 %copy-done.3 = f32[256,2432]{1,0:T(8,128)} copy-done((f32[256,2432]{1,0:T(8,128)}, f32[256,2432]{1,0:T(8,128)S(1)}, u32[]{:S(2)}) %copy-start.3) | copy-done | bytes 2490392
  15.6 0.1 broadcast_in_dim.13
  15.7 21.6 %all_to_all.15.parts = f32[64,1,768]{2,1,0:T(1,128)S(1)} all-to-all(f32[64,1,768]{2,1,0:T(1,128)S(1)} %broadcast_in_dim.13), channel_id=1, replica_groups=mesh['rows'=2,'vocab'=64] {'vocab'}, dimensions={0} | all-to-all | bytes 393216 | tf_op jit(solution)/shard_map/share_stats/all_to_all | solution.py:295
  37.3 0.0 copy-start.1
  37.3 2.4 %copy-done.1 = bf16[1024,2432]{1,0:T(8,128)(2,1)S(1)} copy-done((bf16[1024,2432]{1,0:T(8,128)(2,1)S(1)}, bf16[1024,2432]{1,0:T(8,128)(2,1)}, u32[]{:S(2)}) %copy-start.1) | copy-done | bytes 4980760
  39.7 0.0 copy-start.4
  39.7 1.7 %copy-done.4 = f32[256,2432]{1,0:T(8,128)S(1)} copy-done((f32[256,2432]{1,0:T(8,128)S(1)}, f32[256,2432]{1,0:T(8,128)}, u32[]{:S(2)}) %copy-start.4) | copy-done | bytes 2490392
  41.4 6.1 %back_part.1 = (f32[1,256]{1,0:T(1,128)}, bf16[256,2432]{1,0:T(8,128)(2,1)S(1)}, bf16[64,16,512]{2,1,0:T(8,128)(2,1)S(1)}) custom-call(s32[1]{0:T(128)} %bitcast.row, f32[64,1,768]{2,1,0:T(1,128)S(1)} %all_to_all.15.parts, f32[256,2432]{1,0:T(8,128)S(1)} %copy-done.4, bf16[256,2432]{1,0:T(8,128)(2,1)S(1)} %copy-done.2, bf16[1024,2432]{1,0:T(8,128)(2,1)S(1)} %copy-done.1, ...), custom_call_target="tpu_custom_call" | custom-call | flops 2550136832 | bytes 9961472 | tf_op jit(solution)/shard_map/back_part/pallas_call | solution.py:190
  47.5 0.0 copy-start.5
  47.5 1.0 %copy-done.5 = bf16[64,16,512]{2,1,0:T(8,128)(2,1)} copy-done((bf16[64,16,512]{2,1,0:T(8,128)(2,1)}, bf16[64,16,512]{2,1,0:T(8,128)(2,1)S(1)}, u32[]{:S(2)}) %copy-start.5) | copy-done | bytes 1048600
  48.5 4.9 %all-to-all-start.1 = ((bf16[64,16,512]{2,1,0:T(8,128)(2,1)}), bf16[64,16,512]{2,1,0:T(8,128)(2,1)S(1)}, u32[]{:S(2)}, u32[]{:S(2)}) async-start(bf16[64,16,512]{2,1,0:T(8,128)(2,1)} %copy-done.5), calls=%async_computation.1 | async-start | bytes 2097152 | tf_op jit(solution)/shard_map/scatter_sum/all_to_all | solution.py:302
  53.4 0.1 collective-permute-start.2
  53.5 18.0 %all-to-all-done.1.terms = bf16[64,16,512]{2,1,0:T(8,128)(2,1)S(1)} async-done(((bf16[64,16,512]{2,1,0:T(8,128)(2,1)}), bf16[64,16,512]{2,1,0:T(8,128)(2,1)S(1)}, u32[]{:S(2)}, u32[]{:S(2)}) %all-to-all-start.1) | async-done | bytes 1048608 | tf_op jit(solution)/shard_map/scatter_sum/all_to_all | solution.py:302
  71.5 1.2 %sum_part.1 = bf16[64,16,512]{2,1,0:T(8,128)(2,1)} custom-call(bf16[64,16,512]{2,1,0:T(8,128)(2,1)S(1)} %all-to-all-done.1.terms), custom_call_target="tpu_custom_call" | custom-call | tf_op jit(solution)/shard_map/sum_part/pallas_call | solution.py:219
  72.7 4.7 %all-to-all-start.2 = ((bf16[64,16,512]{2,1,0:T(8,128)(2,1)}), bf16[64,16,512]{2,1,0:T(8,128)(2,1)S(1)}, u32[]{:S(2)}, u32[]{:S(2)}) async-start(bf16[64,16,512]{2,1,0:T(8,128)(2,1)} %sum_part.1), calls=%async_computation.2 | async-start | bytes 2097152 | tf_op jit(solution)/shard_map/gather/all_to_all | solution.py:305
  77.4 0.1 collective-permute-start.1
  77.4 1.9 %collective-permute-done.1.mine_o = bf16[256,1024]{1,0:T(8,128)(2,1)S(1)} collective-permute-done((bf16[256,1024]{1,0:T(8,128)(2,1)S(1)}, bf16[256,1024]{1,0:T(8,128)(2,1)S(1)}, u32[]{:S(2)}, u32[]{:S(2)}) %collective-permute-start.1) | collective-permute-done | bytes 524320 | tf_op jit(solution)/shard_map/swap_hidden/ppermute | solution.py:27
  79.3 0.0 collective-permute-done.2.dlogits_o
  79.3 8.3 %head_part.1 = f32[1024,2432]{1,0:T(8,128)} custom-call(bf16[256,1024]{1,0:T(8,128)(2,1)S(1)} %get-tuple-element.19.mine, bf16[256,1024]{1,0:T(8,128)(2,1)S(1)} %collective-permute-done.1.mine_o, bf16[256,2432]{1,0:T(8,128)(2,1)S(1)} %get-tuple-element.18.dlogits, bf16[256,2432]{1,0:T(8,128)(2,1)} %collective-permute-done.2.dlogits_o), custom_call_target="tpu_custom_call" | custom-call | flops 2550136832 | bytes 9961472 | tf_op jit(solution)/shard_map/head_part/pallas_call | solution.py:267
  87.6 6.5 %all-to-all-done.2.pieces = bf16[64,16,512]{2,1,0:T(8,128)(2,1)S(1)} async-done(((bf16[64,16,512]{2,1,0:T(8,128)(2,1)}), bf16[64,16,512]{2,1,0:T(8,128)(2,1)S(1)}, u32[]{:S(2)}, u32[]{:S(2)}) %all-to-all-start.2) | async-done | bytes 1048608 | tf_op jit(solution)/shard_map/gather/all_to_all | solution.py:305
  94.1 1.4 %join_part.1 = f32[256,2048]{1,0:T(8,128)} custom-call(bf16[64,16,512]{2,1,0:T(8,128)(2,1)S(1)} %all-to-all-done.2.pieces), custom_call_target="tpu_custom_call" | custom-call | tf_op jit(solution)/shard_map/join_part/pallas_call | solution.py:247
  (1 shorter events, 0.0 us)
Async XLA Ops:
  0.6 1.6 %copy-start.2 = (bf16[256,2432]{1,0:T(8,128)(2,1)S(1)}, bf16[256,2432]{1,0:T(8,128)(2,1)}, u32[]{:S(2)}) copy-start(bf16[256,2432]{1,0:T(8,128)(2,1)} %target.3) | copy-start | bytes 3735556
  0.6 8.7 %collective-permute-start = (bf16[1024,2432]{1,0:T(8,128)(2,1)}, bf16[1024,2432]{1,0:T(8,128)(2,1)}, u32[]{:S(2)}, u32[]{:S(2)}) collective-permute-start(bf16[1024,2432]{1,0:T(8,128)(2,1)} %weight.3), channel_id=1, source_target_pairs={{0,64},{64,0},{1,65},{65,1},{2,66},{66,2},{3,67},{67,3},{4,68},{68... | collective-permute-start | bytes 14942216 | tf_op jit(solution)/shard_map/swap_weight/ppermute | solution.py:27
  2.2 2.4 %copy-start = (bf16[1024,2432]{1,0:T(8,128)(2,1)S(1)}, bf16[1024,2432]{1,0:T(8,128)(2,1)}, u32[]{:S(2)}) copy-start(bf16[1024,2432]{1,0:T(8,128)(2,1)} %weight.3) | copy-start | bytes 14942212
  14.1 1.5 %copy-start.3 = (f32[256,2432]{1,0:T(8,128)}, f32[256,2432]{1,0:T(8,128)S(1)}, u32[]{:S(2)}) copy-start(f32[256,2432]{1,0:T(8,128)S(1)} %get-tuple-element.15.draft) | copy-start | bytes 7471108
  37.3 2.4 %copy-start.1 = (bf16[1024,2432]{1,0:T(8,128)(2,1)S(1)}, bf16[1024,2432]{1,0:T(8,128)(2,1)}, u32[]{:S(2)}) copy-start(bf16[1024,2432]{1,0:T(8,128)(2,1)} %weight.3) | copy-start | bytes 14942212
  39.7 1.7 %copy-start.4 = (f32[256,2432]{1,0:T(8,128)S(1)}, f32[256,2432]{1,0:T(8,128)}, u32[]{:S(2)}) copy-start(f32[256,2432]{1,0:T(8,128)} %copy-done.3) | copy-start | bytes 7471108
  47.5 1.0 %copy-start.5 = (bf16[64,16,512]{2,1,0:T(8,128)(2,1)}, bf16[64,16,512]{2,1,0:T(8,128)(2,1)S(1)}, u32[]{:S(2)}) copy-start(bf16[64,16,512]{2,1,0:T(8,128)(2,1)S(1)} %get-tuple-element.17) | copy-start | bytes 3145732
  48.5 23.0 %all-to-all-start.1 = ((bf16[64,16,512]{2,1,0:T(8,128)(2,1)}), bf16[64,16,512]{2,1,0:T(8,128)(2,1)S(1)}, u32[]{:S(2)}, u32[]{:S(2)}) async-start(bf16[64,16,512]{2,1,0:T(8,128)(2,1)} %copy-done.5), calls=%async_computation.1 | async-start | bytes 2097152 | tf_op jit(solution)/shard_map/scatter_sum/all_to_all | solution.py:302
  53.4 25.9 %collective-permute-start.2 = (bf16[256,2432]{1,0:T(8,128)(2,1)S(1)}, bf16[256,2432]{1,0:T(8,128)(2,1)}, u32[]{:S(2)}, u32[]{:S(2)}) collective-permute-start(bf16[256,2432]{1,0:T(8,128)(2,1)S(1)} %get-tuple-element.18.dlogits), channel_id=1, source_target_pairs={{0,64},{64,0},{1,65},{65,1},{2,66},{66,2},{3,67},{67,3},{4,68},{68... | collective-permute-start | bytes 3735560 | tf_op jit(solution)/shard_map/swap_dlogits/ppermute | solution.py:27
  72.7 21.4 %all-to-all-start.2 = ((bf16[64,16,512]{2,1,0:T(8,128)(2,1)}), bf16[64,16,512]{2,1,0:T(8,128)(2,1)S(1)}, u32[]{:S(2)}, u32[]{:S(2)}) async-start(bf16[64,16,512]{2,1,0:T(8,128)(2,1)} %sum_part.1), calls=%async_computation.2 | async-start | bytes 2097152 | tf_op jit(solution)/shard_map/gather/all_to_all | solution.py:305
  77.4 2.0 %collective-permute-start.1 = (bf16[256,1024]{1,0:T(8,128)(2,1)S(1)}, bf16[256,1024]{1,0:T(8,128)(2,1)S(1)}, u32[]{:S(2)}, u32[]{:S(2)}) collective-permute-start(bf16[256,1024]{1,0:T(8,128)(2,1)S(1)} %get-tuple-element.20.theirs), channel_id=1, source_target_pairs={{0,64},{64,0},{1,65},{65,1},{2,66},{66,2},{3,67},{67,3},{4,68},{68... | collective-permute-start | bytes 1572872 | tf_op jit(solution)/shard_map/swap_hidden/ppermute | solution.py:27

commit v5 on v3

--- a/solution.py
+++ b/solution.py
@@ -11,10 +11,12 @@
 TOKENS_PIECE = 16
 COLS_PIECE = 512
 BLOCK = 640
+AHEAD = 2
 LOG2E = math.log2(math.e)
 F32, BF16 = jnp.float32, jnp.bfloat16
 VMEM = pl.BlockSpec(memory_space=pltpu.VMEM)
 HBM = pl.BlockSpec(memory_space=pltpu.HBM)
+ANY = pl.BlockSpec(memory_space=pl.ANY)
 
 
 def dot(a, b, ca, cb):
@@ -43,6 +45,10 @@
 
 def tiles(x):
     return [x[:, c : c + 128] for c in range(0, x.shape[1], 128)]
+
+
+def stat_rows(tokens):
+    return pl.cdiv(3 * tokens // 128, 8) * 8
 
 
 def own_kernel(mine, weight, target, acc, probs, stat):
@@ -84,11 +90,14 @@
     for j, (c, e) in enumerate(blocks(vocab)):
         part = pl.ds(c, e - c)
         copies.append(pltpu.make_async_copy(weight.at[:, part], buffer.at[:, part], sems.at[j]))
-        copies[-1].start()
+    for copy in copies[:AHEAD]:
+        copy.start()
     peak = jnp.full((tokens, 128), -jnp.inf, F32)
     cross = jnp.zeros((tokens, 128), F32)
     for j, (c, e) in enumerate(blocks(vocab)):
         copies[j].wait()
+        for copy in copies[j + AHEAD : j + AHEAD + 1]:
+            copy.start()
         value = acc[:, c:e] + dot(theirs[...], buffer[:, c:e], 1, 0)
         draft[:, c:e] = value
         for tile, weighed in zip(tiles(value), tiles(probs[:, c:e] * value)):
@@ -102,82 +111,93 @@
     mean = stat[:, 1:2] - jnp.sum(cross, axis=1, keepdims=True)
     lane = lax.broadcasted_iota(jnp.int32, stat.shape, 1)
     rows = jnp.where(lane == 0, stat[:, :1], jnp.where(lane == 1, mean, lse_q)).T
+    out[...] = jnp.zeros(out.shape, F32)
     for i in range(3):
-        out[:, i * tokens : (i + 1) * tokens] = rows[i : i + 1]
+        for k in range(tokens // 128):
+            at = i * (tokens // 128) + k
+            out[at : at + 1] = rows[i : i + 1, k * 128 : (k + 1) * 128]
 
 
 def draft_part(theirs, acc, probs, stat, weight):
     tokens, half = theirs.shape
     vocab = acc.shape[1]
+    steps = len(blocks(vocab))
     return pl.pallas_call(
         draft_kernel,
-        in_specs=[VMEM] * 4 + [HBM],
-        out_specs=[VMEM] * 2,
+        in_specs=[VMEM] * 4 + [ANY],
+        out_specs=[VMEM] * 3,
         out_shape=[
             jax.ShapeDtypeStruct((tokens, vocab), F32),
-            jax.ShapeDtypeStruct((1, 3 * tokens), F32),
+            jax.ShapeDtypeStruct((stat_rows(tokens), 128), F32),
+            jax.ShapeDtypeStruct((half, vocab), BF16),
         ],
-        scratch_shapes=[pltpu.VMEM((half, vocab), BF16), pltpu.SemaphoreType.DMA((len(blocks(vocab)),))],
-        compiler_params=params(24),
+        scratch_shapes=[pltpu.SemaphoreType.DMA((steps,))],
+        compiler_params=params(20),
         cost_estimate=cost(2 * tokens * half * vocab, 2 * half * vocab),
         name="draft_part",
     )(theirs, acc, probs, stat, weight)
 
 
-def back_kernel(factor, row, parts, draft, target, weight, weight_o, divergence, dlogits, out, stage, sems):
-    half = weight.shape[0]
-    per = half // COLS_PIECE
-    tokens = draft.shape[0]
-    each_t, mean, each_q = (parts[:, :, i * tokens : (i + 1) * tokens] for i in range(3))
-    top_t, top_q = jnp.max(each_t, axis=0), jnp.max(each_q, axis=0)
-    scale_t = exp(each_t - top_t)
-    sum_t = jnp.sum(scale_t, axis=0)
-    sum_q = jnp.sum(exp(each_q - top_q), axis=0)
-    lse_t, lse_q = top_t + jnp.log(sum_t), top_q + jnp.log(sum_q)
-    divergence[...] = jnp.sum(scale_t * mean, axis=0) / sum_t - lse_t + lse_q
-    line = lax.broadcasted_iota(jnp.int32, (128, tokens), 0)
-    turned = jnp.where(line == 0, lse_t, lse_q).T
-    lse_t, lse_q = turned[:, :1], turned[:, 1:2]
-
+def logits_kernel(factor, parts, draft, target, divergence, dlogits):
+    lines = draft.shape[0] // 128
+    every = parts[...]
+    top = jnp.max(every, axis=0)
+    scale = exp(every - top)
+    lse = top + jnp.log(jnp.sum(scale, axis=0))
+    cross = jnp.sum(scale[:, :lines] * every[:, lines : 2 * lines], axis=0)
+    mean = cross / jnp.sum(scale[:, :lines], axis=0)
+    result = mean - lse[:lines] + lse[2 * lines : 3 * lines]
+    for k in range(lines):
+        divergence[:, k * 128 : (k + 1) * 128] = result[k : k + 1]
+    turned = jnp.concatenate([lse, jnp.zeros((128 - lse.shape[0], 128), F32)], axis=0).T
+    lse_t = jnp.concatenate([turned[:, k : k + 1] for k in range(lines)], axis=0)
+    lse_q = jnp.concatenate([turned[:, 2 * lines + k : 2 * lines + k + 1] for k in range(lines)], axis=0)
     for c, e in blocks(draft.shape[1]):
         probs_q = exp(draft[:, c:e] - lse_q)
         probs_t = exp(target[:, c:e].astype(F32) - lse_t)
         dlogits[:, c:e] = ((probs_q - probs_t) * factor).astype(BF16)
 
-    copies = []
-    for j in range(2 * per):
-        source = (weight, weight_o)[j // per]
-        rows = source[j % per * COLS_PIECE : (j % per + 1) * COLS_PIECE]
-        block = dot(dlogits[...], rows, 1, 1).astype(BF16)
-        stage[j] = block.reshape(tokens // TOKENS_PIECE, TOKENS_PIECE, COLS_PIECE)
-        place = lax.rem(row[0] * per + j, 2 * per)
-        copies.append(pltpu.make_async_copy(stage.at[j], out.at[:, place], sems.at[j]))
-        copies[-1].start()
-    for copy in copies:
-        copy.wait()
-
-
-def back_part(factor, row, parts, draft, target, weight, weight_o):
+
+def logits_part(factor, parts, draft, target):
     tokens, vocab = draft.shape
-    half = weight.shape[0]
-    down, across = tokens // TOKENS_PIECE, 2 * half // COLS_PIECE
-    return pl.pallas_call(
-        functools.partial(back_kernel, factor),
-        in_specs=[pl.BlockSpec(memory_space=pltpu.SMEM)] + [VMEM] * 5,
-        out_specs=[VMEM, VMEM, HBM],
+    return pl.pallas_call(
+        functools.partial(logits_kernel, factor),
+        in_specs=[VMEM] * 3,
+        out_specs=[VMEM] * 2,
         out_shape=[
             jax.ShapeDtypeStruct((1, tokens), F32),
             jax.ShapeDtypeStruct((tokens, vocab), BF16),
-            jax.ShapeDtypeStruct((down, across, TOKENS_PIECE, COLS_PIECE), BF16),
         ],
-        scratch_shapes=[
-            pltpu.VMEM((across, down, TOKENS_PIECE, COLS_PIECE), BF16),
-            pltpu.SemaphoreType.DMA((across,)),
-        ],
-        compiler_params=params(24),
+        compiler_params=params(16),
+        cost_estimate=cost(8 * tokens * vocab, 8 * tokens * vocab),
+        name="logits_part",
+    )(parts, draft, target)
+
+
+def back_kernel(row, dlogits, weight, weight_o, out):
+    half = weight.shape[0]
+    per = half // COLS_PIECE
+    down = dlogits.shape[0] // TOKENS_PIECE
+    for j in range(2 * per):
+        rows = pl.ds(j % per * COLS_PIECE, COLS_PIECE)
+        block = dot(dlogits[...], (weight, weight_o)[j // per][rows], 1, 1).astype(BF16)
+        place = lax.rem(row[0] * per + j, 2 * per)
+        out[pl.ds(place * down, down)] = block.reshape(down, TOKENS_PIECE, COLS_PIECE)
+
+
+def back_part(row, dlogits, weight, weight_o):
+    tokens, vocab = dlogits.shape
+    half = weight.shape[0]
+    pieces = (tokens // TOKENS_PIECE) * (2 * half // COLS_PIECE)
+    return pl.pallas_call(
+        back_kernel,
+        in_specs=[pl.BlockSpec(memory_space=pltpu.SMEM)] + [VMEM] * 3,
+        out_specs=VMEM,
+        out_shape=jax.ShapeDtypeStruct((pieces, TOKENS_PIECE, COLS_PIECE), BF16),
+        compiler_params=params(16),
         cost_estimate=cost(4 * tokens * half * vocab, 4 * half * vocab),
         name="back_part",
-    )(row, parts, draft, target, weight, weight_o)
+    )(row, dlogits, weight, weight_o)
 
 
 def sum_kernel(terms, out):
@@ -200,14 +220,15 @@
 
 def join_kernel(pieces, out, stage, sems):
     tokens, width = out.shape
-    across = width // COLS_PIECE
+    down = tokens // TOKENS_PIECE
     steps = sems.shape[0]
     copies = []
     for step in range(steps):
         rows = pl.ds(step * tokens // steps, tokens // steps)
-        for i in range(step * pieces.shape[0] // steps, (step + 1) * pieces.shape[0] // steps):
-            down = pl.ds(i // across * TOKENS_PIECE, TOKENS_PIECE)
-            stage[down, pl.ds(i % across * COLS_PIECE, COLS_PIECE)] = pieces[i].astype(F32)
+        for i in range(step * down // steps, (step + 1) * down // steps):
+            for j in range(width // COLS_PIECE):
+                place = pl.ds(i * TOKENS_PIECE, TOKENS_PIECE), pl.ds(j * COLS_PIECE, COLS_PIECE)
+                stage[place] = pieces[j * down + i].astype(F32)
         copies.append(pltpu.make_async_copy(stage.at[rows], out.at[rows], sems.at[step]))
         copies[-1].start()
     for copy in copies:
@@ -261,16 +282,15 @@
         mine_o = swap(theirs)
 
     acc, probs, stat = own_part(mine, weight, target)
-    draft, part = draft_part(theirs, acc, probs, stat, weight_o)
+    draft, part, weight_o = draft_part(theirs, acc, probs, stat, weight_o)
     with jax.named_scope("share_stats"):
         parts = lax.all_to_all(jnp.broadcast_to(part[None], (n,) + part.shape), "vocab", 0, 0)
-    divergence, dlogits, pieces = back_part(
-        vocab * n / 1024.0, jnp.full((1,), row, jnp.int32), parts, draft, target, weight, weight_o
-    )
+    divergence, dlogits = logits_part(vocab * n / 1024.0, parts, draft, target)
     with jax.named_scope("swap_dlogits"):
         dlogits_o = swap(dlogits)
+    pieces = back_part(jnp.full((1,), row, jnp.int32), dlogits, weight, weight_o)
     with jax.named_scope("scatter_sum"):
-        terms = lax.all_to_all(pieces.reshape(n, TOKENS_PIECE, COLS_PIECE), "vocab", 0, 0)
+        terms = lax.all_to_all(pieces, "vocab", 0, 0)
     totals = sum_part(terms)
     with jax.named_scope("gather"):
         gathered = lax.all_to_all(totals, "vocab", 0, 0)

time: 96.5 us -> 89.7 us (0.930)
  local copies, waits for them, and re-layouts: 10.5 us -> 4.9 us
  Pallas kernels: 24.5 us -> 22.9 us
    unnamed x12 -> x10, local copies, waits for them, and re-layouts: 9.08 us -> 3.53 us
    pallas_call x1, Pallas kernels: 1.23 us -> 0.24 us  [sum_part(): pl.pallas_call(sum_kernel, in_specs=[VMEM], out_specs=VMEM, out_shape=jax...]
    pallas_call x2 -> x3, Pallas kernels: 11.3 us -> 10.7 us  [the longest x1 5.19 us: draft_part(): pl.pallas_call(draft_kernel, in_specs=[VMEM] * 4 + [ANY], out_specs=[VMEM...]
  transfers between devices with their start and end apart: 5 -> 5, of which waited for: 4 -> 4; matrix products, arithmetic and copies ran while one was open for 1% -> 2% of each run, Pallas kernels for 12% -> 12%
where the time goes in v5:
time: 89.7 us; the launch traced here: 89.3 us
  waiting for transfers between devices  28.8 us (32%)
  Pallas kernels  22.9 us (26%)
  blocking collectives  22.2 us (25%)
  starting transfers between devices  9.77 us (11%)
  local copies, waits for them, and re-layouts  4.9 us (5%)
    all_to_all x1, blocking collectives, shards(): lax.all_to_all(jnp.broadcast_to(part[None], (n,) + part.shape), 'vocab',...  22.2 us
    all_to_all x1, waiting for transfers between devices, shards(): terms = lax.all_to_all(pieces, 'vocab', 0, 0)  18 us
    pallas_call x1, Pallas kernels, head_part(): pl.pallas_call(head_kernel, grid=(half // step,), in_specs=[column, colum...  8.3 us
    all_to_all x1, waiting for transfers between devices, shards(): gathered = lax.all_to_all(totals, 'vocab', 0, 0)  6.51 us
    pallas_call x1, Pallas kernels, draft_part(): pl.pallas_call(draft_kernel, in_specs=[VMEM] * 4 + [ANY], out_specs=[VMEM...  5.19 us
    all_to_all x1, starting transfers between devices, shards(): terms = lax.all_to_all(pieces, 'vocab', 0, 0)  4.86 us
    all_to_all x1, starting transfers between devices, shards(): gathered = lax.all_to_all(totals, 'vocab', 0, 0)  4.65 us
    ppermute x3, waiting for transfers between devices, swap(): return lax.ppermute(x, 'rows', SWAP)  4.33 us
  transfers between devices with their start and end apart: 5, of which 4 were waited for; matrix products, arithmetic and copies ran while one was open for 2% of the time, Pallas kernels for 12%

profile of v5, /device:TPU:0, one launch (start us, length us, event | category | flops | bytes accessed | tf_op | source)
XLA Modules:
  0.0 89.3 jit_solution(17909336414414938283)
XLA Ops:
  0.6 0.0 copy-start.1
  0.6 0.1 collective-permute-start
  0.7 1.4 %constant_dynamic-slice_fusion = (bf16[256,1024]{1,0:T(8,128)(2,1)S(1)}, bf16[256,1024]{1,0:T(8,128)(2,1)S(1)}) fusion(bf16[256,2048]{1,0:T(8,128)(2,1)} %param.3, s32[]{:T(128)S(6)} %select_n.7, s32[]{:T(128)S(6)} %select_n.6), kind=kLoop, calls=%fused_computation | loop fusion | bytes 2097160 | tf_op jit(solution)/shard_map/dynamic_slice | solution.py:279
  2.1 0.1 copy-done.1
  2.2 0.0 copy-start
  2.2 2.4 %copy-done = bf16[1024,2432]{1,0:T(8,128)(2,1)S(1)} copy-done((bf16[1024,2432]{1,0:T(8,128)(2,1)S(1)}, bf16[1024,2432]{1,0:T(8,128)(2,1)}, u32[]{:S(2)}) %copy-start) | copy-done | bytes 4980760
  4.7 2.3 %own_part.1 = (f32[256,2432]{1,0:T(8,128)S(1)}, f32[256,2432]{1,0:T(8,128)S(1)}, f32[256,128]{1,0:T(8,128)S(1)}) custom-call(bf16[256,1024]{1,0:T(8,128)(2,1)S(1)} %get-tuple-element.19.mine, bf16[1024,2432]{1,0:T(8,128)(2,1)S(1)} %copy-done, bf16[256,2432]{1,0:T(8,128)(2,1)S(1)} %copy-done.1), custom_call_target="tpu_custom_call" | custom-call | flops 1275068416 | bytes 4980736 | tf_op jit(solution)/shard_map/own_part/pallas_call | solution.py:72
  6.9 2.4 %collective-permute-done.weight = bf16[1024,2432]{1,0:T(8,128)(2,1)} collective-permute-done((bf16[1024,2432]{1,0:T(8,128)(2,1)}, bf16[1024,2432]{1,0:T(8,128)(2,1)}, u32[]{:S(2)}, u32[]{:S(2)}) %collective-permute-start) | collective-permute-done | bytes 4980768 | tf_op jit(solution)/shard_map/swap_weight/ppermute | solution.py:27
  9.3 0.0 slice-start
  9.3 0.0 slice-start.1
  9.3 5.2 %draft_part.1 = (f32[256,2432]{1,0:T(8,128)S(1)}, f32[8,128]{1,0:T(8,128)S(1)}, bf16[1024,2432]{1,0:T(8,128)(2,1)S(1)}) custom-call(bf16[256,1024]{1,0:T(8,128)(2,1)S(1)} %get-tuple-element.20.theirs, f32[256,2432]{1,0:T(8,128)S(1)} %get-tuple-element.11.acc, f32[256,2432]{1,0:T(8,128)S(1)} %get-tuple-element.12.probs, ...), custom_call_target="tpu_custom_call" | custom-call | flops 1275068416 | bytes 4980736 | tf_op jit(solution)/shard_map/draft_part/pallas_call | solution.py:125
  14.6 22.2 %all_to_all.15.parts = f32[64,8,128]{2,1,0:T(8,128)S(1)} all-to-all(f32[64,8,128]{2,1,0:T(8,128)S(1)} %broadcast_in_dim.4), channel_id=1, replica_groups=mesh['rows'=2,'vocab'=64] {'vocab'}, dimensions={0} | all-to-all | bytes 524288 | tf_op jit(solution)/shard_map/share_stats/all_to_all | solution.py:287
  36.8 1.6 %logits_part.1 = (f32[1,256]{1,0:T(1,128)}, bf16[256,2432]{1,0:T(8,128)(2,1)S(1)}) custom-call(f32[64,8,128]{2,1,0:T(8,128)S(1)} %all_to_all.15.parts, f32[256,2432]{1,0:T(8,128)S(1)} %get-tuple-element.15.draft, bf16[256,2432]{1,0:T(8,128)(2,1)S(1)} %copy-done.1), custom_call_target="tpu_custom_call" | custom-call | flops 4980736 | bytes 4980736 | tf_op jit(solution)/shard_map/logits_part/pallas_call | solution.py:163
  38.4 0.0 slice-done
  38.4 0.0 slice-done.1
  38.4 3.9 %back_part.1 = bf16[64,16,512]{2,1,0:T(8,128)(2,1)} custom-call(s32[1]{0:T(128)} %bitcast.1.row, bf16[256,2432]{1,0:T(8,128)(2,1)S(1)} %get-tuple-element.17.dlogits, bf16[1024,2432]{1,0:T(8,128)(2,1)S(1)} %bitcast.3, bf16[1024,2432]{1,0:T(8,128)(2,1)S(1)} %get-tuple-element.18.weight_o), custom_call_target="tpu_custom_call" | custom-call | flops 2550136832 | bytes 9961472 | tf_op jit(solution)/shard_map/back_part/pallas_call | solution.py:192
  42.3 4.9 %all-to-all-start.1 = ((bf16[64,16,512]{2,1,0:T(8,128)(2,1)}), bf16[64,16,512]{2,1,0:T(8,128)(2,1)S(1)}, u32[]{:S(2)}, u32[]{:S(2)}) async-start(bf16[64,16,512]{2,1,0:T(8,128)(2,1)} %back_part.1), calls=%async_computation.1 | async-start | bytes 2097152 | tf_op jit(solution)/shard_map/scatter_sum/all_to_all | solution.py:293
  47.2 0.1 collective-permute-start.2
  47.2 18.0 %all-to-all-done.1.terms = bf16[64,16,512]{2,1,0:T(8,128)(2,1)S(1)} async-done(((bf16[64,16,512]{2,1,0:T(8,128)(2,1)}), bf16[64,16,512]{2,1,0:T(8,128)(2,1)S(1)}, u32[]{:S(2)}, u32[]{:S(2)}) %all-to-all-start.1) | async-done | bytes 1048608 | tf_op jit(solution)/shard_map/scatter_sum/all_to_all | solution.py:293
  65.2 0.2 sum_part.1
  65.5 0.0 copy-start.2
  65.5 1.0 %copy-done.2 = bf16[64,16,512]{2,1,0:T(8,128)(2,1)} copy-done((bf16[64,16,512]{2,1,0:T(8,128)(2,1)}, bf16[64,16,512]{2,1,0:T(8,128)(2,1)S(1)}, u32[]{:S(2)}) %copy-start.2) | copy-done | bytes 1048600
  66.5 4.7 %all-to-all-start.2 = ((bf16[64,16,512]{2,1,0:T(8,128)(2,1)}), bf16[64,16,512]{2,1,0:T(8,128)(2,1)S(1)}, u32[]{:S(2)}, u32[]{:S(2)}) async-start(bf16[64,16,512]{2,1,0:T(8,128)(2,1)} %copy-done.2), calls=%async_computation.2 | async-start | bytes 2097152 | tf_op jit(solution)/shard_map/gather/all_to_all | solution.py:296
  71.1 0.1 collective-permute-start.1
  71.2 1.9 %collective-permute-done.1.mine_o = bf16[256,1024]{1,0:T(8,128)(2,1)S(1)} collective-permute-done((bf16[256,1024]{1,0:T(8,128)(2,1)S(1)}, bf16[256,1024]{1,0:T(8,128)(2,1)S(1)}, u32[]{:S(2)}, u32[]{:S(2)}) %collective-permute-start.1) | collective-permute-done | bytes 524320 | tf_op jit(solution)/shard_map/swap_hidden/ppermute | solution.py:27
  73.1 0.0 collective-permute-done.2.dlogits_o
  73.1 8.3 %head_part.1 = f32[1024,2432]{1,0:T(8,128)} custom-call(bf16[256,1024]{1,0:T(8,128)(2,1)S(1)} %get-tuple-element.19.mine, bf16[256,1024]{1,0:T(8,128)(2,1)S(1)} %collective-permute-done.1.mine_o, bf16[256,2432]{1,0:T(8,128)(2,1)S(1)} %get-tuple-element.17.dlogits, bf16[256,2432]{1,0:T(8,128)(2,1)} %collective-permute-done.2.dlogits_o), custom_call_target="tpu_custom_call" | custom-call | flops 2550136832 | bytes 9961472 | tf_op jit(solution)/shard_map/head_part/pallas_call | solution.py:259
  81.4 6.5 %all-to-all-done.2.pieces = bf16[64,16,512]{2,1,0:T(8,128)(2,1)S(1)} async-done(((bf16[64,16,512]{2,1,0:T(8,128)(2,1)}), bf16[64,16,512]{2,1,0:T(8,128)(2,1)S(1)}, u32[]{:S(2)}, u32[]{:S(2)}) %all-to-all-start.2) | async-done | bytes 1048608 | tf_op jit(solution)/shard_map/gather/all_to_all | solution.py:296
  87.9 1.4 %join_part.1 = f32[256,2048]{1,0:T(8,128)} custom-call(bf16[64,16,512]{2,1,0:T(8,128)(2,1)S(1)} %all-to-all-done.2.pieces), custom_call_target="tpu_custom_call" | custom-call | tf_op jit(solution)/shard_map/join_part/pallas_call | solution.py:239
  (2 shorter events, 0.0 us)
Async XLA Ops:
  0.6 1.6 %copy-start.1 = (bf16[256,2432]{1,0:T(8,128)(2,1)S(1)}, bf16[256,2432]{1,0:T(8,128)(2,1)}, u32[]{:S(2)}) copy-start(bf16[256,2432]{1,0:T(8,128)(2,1)} %target.3) | copy-start | bytes 3735556
  0.6 8.7 %collective-permute-start = (bf16[1024,2432]{1,0:T(8,128)(2,1)}, bf16[1024,2432]{1,0:T(8,128)(2,1)}, u32[]{:S(2)}, u32[]{:S(2)}) collective-permute-start(bf16[1024,2432]{1,0:T(8,128)(2,1)} %weight.3), channel_id=1, source_target_pairs={{0,64},{64,0},{1,65},{65,1},{2,66},{66,2},{3,67},{67,3},{4,68},{68... | collective-permute-start | bytes 14942216 | tf_op jit(solution)/shard_map/swap_weight/ppermute | solution.py:27
  2.2 2.4 %copy-start = (bf16[1024,2432]{1,0:T(8,128)(2,1)S(1)}, bf16[1024,2432]{1,0:T(8,128)(2,1)}, u32[]{:S(2)}) copy-start(bf16[1024,2432]{1,0:T(8,128)(2,1)} %weight.3) | copy-start | bytes 14942212
  9.3 29.1 %slice-start = ((s8[4980736]{0:T(1024)(128)(4,1)}), s8[4194304]{0:T(1024)(128)(4,1)S(1)}, s32[]{:S(2)}) async-start(s8[4980736]{0:T(1024)(128)(4,1)} %bitcast.2), calls=%async_computation.3 | async-start | bytes 8388608
  9.3 29.1 %slice-start.1 = ((s8[4980736]{0:T(1024)(128)(4,1)}), s8[786432]{0:T(1024)(128)(4,1)S(1)}, s32[]{:S(2)}) async-start(s8[4980736]{0:T(1024)(128)(4,1)} %bitcast.2), calls=%async_computation.4 | async-start | bytes 1572864
  42.3 23.0 %all-to-all-start.1 = ((bf16[64,16,512]{2,1,0:T(8,128)(2,1)}), bf16[64,16,512]{2,1,0:T(8,128)(2,1)S(1)}, u32[]{:S(2)}, u32[]{:S(2)}) async-start(bf16[64,16,512]{2,1,0:T(8,128)(2,1)} %back_part.1), calls=%async_computation.1 | async-start | bytes 2097152 | tf_op jit(solution)/shard_map/scatter_sum/all_to_all | solution.py:293
  47.2 26.0 %collective-permute-start.2 = (bf16[256,2432]{1,0:T(8,128)(2,1)S(1)}, bf16[256,2432]{1,0:T(8,128)(2,1)}, u32[]{:S(2)}, u32[]{:S(2)}) collective-permute-start(bf16[256,2432]{1,0:T(8,128)(2,1)S(1)} %get-tuple-element.17.dlogits), channel_id=1, source_target_pairs={{0,64},{64,0},{1,65},{65,1},{2,66},{66,2},{3,67},{67,3},{4,68},{68... | collective-permute-start | bytes 3735560 | tf_op jit(solution)/shard_map/swap_dlogits/ppermute | solution.py:27
  65.5 1.0 %copy-start.2 = (bf16[64,16,512]{2,1,0:T(8,128)(2,1)}, bf16[64,16,512]{2,1,0:T(8,128)(2,1)S(1)}, u32[]{:S(2)}) copy-start(bf16[64,16,512]{2,1,0:T(8,128)(2,1)S(1)} %sum_part.1) | copy-start | bytes 3145732
  66.5 21.5 %all-to-all-start.2 = ((bf16[64,16,512]{2,1,0:T(8,128)(2,1)}), bf16[64,16,512]{2,1,0:T(8,128)(2,1)S(1)}, u32[]{:S(2)}, u32[]{:S(2)}) async-start(bf16[64,16,512]{2,1,0:T(8,128)(2,1)} %copy-done.2), calls=%async_computation.2 | async-start | bytes 2097152 | tf_op jit(solution)/shard_map/gather/all_to_all | solution.py:296
  71.1 2.0 %collective-permute-start.1 = (bf16[256,1024]{1,0:T(8,128)(2,1)S(1)}, bf16[256,1024]{1,0:T(8,128)(2,1)S(1)}, u32[]{:S(2)}, u32[]{:S(2)}) collective-permute-start(bf16[256,1024]{1,0:T(8,128)(2,1)S(1)} %get-tuple-element.20.theirs), channel_id=1, source_target_pairs={{0,64},{64,0},{1,65},{65,1},{2,66},{66,2},{3,67},{67,3},{4,68},{68... | collective-permute-start | bytes 1572872 | tf_op jit(solution)/shard_map/swap_hidden/ppermute | solution.py:27

commit v6 on v5

--- a/solution.py
+++ b/solution.py
@@ -11,7 +11,6 @@
 TOKENS_PIECE = 16
 COLS_PIECE = 512
 BLOCK = 640
-AHEAD = 2
 LOG2E = math.log2(math.e)
 F32, BF16 = jnp.float32, jnp.bfloat16
 VMEM = pl.BlockSpec(memory_space=pltpu.VMEM)
@@ -51,10 +50,18 @@
     return pl.cdiv(3 * tokens // 128, 8) * 8
 
 
-def own_kernel(mine, weight, target, acc, probs, stat):
+def load(source, target, sems):
+    copies = []
+    for j, (c, e) in enumerate(blocks(source.shape[1])):
+        part = pl.ds(c, e - c)
+        copies.append(pltpu.make_async_copy(source.at[:, part], target.at[:, part], sems.at[j]))
+        copies[-1].start()
+    return copies
+
+
+def own_kernel(mine, target, weight, acc, probs, stat, buffer, sems):
     vocab = target.shape[1]
-    for c, e in blocks(vocab):
-        acc[:, c:e] = dot(mine[...], weight[:, c:e], 1, 0)
+    copies = load(weight, buffer, sems)
     wide = target[...].astype(F32)
     peak = jnp.max(wide, axis=1, keepdims=True)
     terms = exp(wide - peak)
@@ -64,40 +71,38 @@
     mean = jnp.sum(terms * wide, axis=1, keepdims=True)
     lane = lax.broadcasted_iota(jnp.int32, stat.shape, 1)
     stat[...] = jnp.where(lane == 0, peak + jnp.log(total), mean)
-
-
-def own_part(mine, weight, target):
+    for copy, (c, e) in zip(copies, blocks(vocab)):
+        copy.wait()
+        acc[:, c:e] = dot(mine[...], buffer[:, c:e], 1, 0)
+
+
+def own_part(mine, target, weight):
     tokens, half = mine.shape
     vocab = target.shape[1]
     return pl.pallas_call(
         own_kernel,
-        in_specs=[VMEM] * 3,
-        out_specs=[VMEM] * 3,
+        in_specs=[VMEM] * 2 + [ANY],
+        out_specs=[VMEM] * 4,
         out_shape=[
             jax.ShapeDtypeStruct((tokens, vocab), F32),
             jax.ShapeDtypeStruct((tokens, vocab), F32),
             jax.ShapeDtypeStruct((tokens, 128), F32),
+            jax.ShapeDtypeStruct((half, vocab), BF16),
         ],
-        compiler_params=params(24),
+        scratch_shapes=[pltpu.SemaphoreType.DMA((len(blocks(vocab)),))],
+        compiler_params=params(16),
         cost_estimate=cost(2 * tokens * half * vocab, 2 * half * vocab),
         name="own_part",
-    )(mine, weight, target)
+    )(mine, target, weight)
 
 
 def draft_kernel(theirs, acc, probs, stat, weight, draft, out, buffer, sems):
     tokens, vocab = draft.shape
-    copies = []
-    for j, (c, e) in enumerate(blocks(vocab)):
-        part = pl.ds(c, e - c)
-        copies.append(pltpu.make_async_copy(weight.at[:, part], buffer.at[:, part], sems.at[j]))
-    for copy in copies[:AHEAD]:
-        copy.start()
+    copies = load(weight, buffer, sems)
     peak = jnp.full((tokens, 128), -jnp.inf, F32)
     cross = jnp.zeros((tokens, 128), F32)
     for j, (c, e) in enumerate(blocks(vocab)):
         copies[j].wait()
-        for copy in copies[j + AHEAD : j + AHEAD + 1]:
-            copy.start()
         value = acc[:, c:e] + dot(theirs[...], buffer[:, c:e], 1, 0)
         draft[:, c:e] = value
         for tile, weighed in zip(tiles(value), tiles(probs[:, c:e] * value)):
@@ -138,7 +143,7 @@
     )(theirs, acc, probs, stat, weight)
 
 
-def logits_kernel(factor, parts, draft, target, divergence, dlogits):
+def back_kernel(factor, row, parts, draft, target, weight, weight_o, divergence, dlogits, out):
     lines = draft.shape[0] // 128
     every = parts[...]
     top = jnp.max(every, axis=0)
@@ -152,52 +157,42 @@
     turned = jnp.concatenate([lse, jnp.zeros((128 - lse.shape[0], 128), F32)], axis=0).T
     lse_t = jnp.concatenate([turned[:, k : k + 1] for k in range(lines)], axis=0)
     lse_q = jnp.concatenate([turned[:, 2 * lines + k : 2 * lines + k + 1] for k in range(lines)], axis=0)
+
+    half = weight.shape[0]
+    per = half // COLS_PIECE
+    down = dlogits.shape[0] // TOKENS_PIECE
+    sums = [None] * (2 * per)
     for c, e in blocks(draft.shape[1]):
         probs_q = exp(draft[:, c:e] - lse_q)
         probs_t = exp(target[:, c:e].astype(F32) - lse_t)
-        dlogits[:, c:e] = ((probs_q - probs_t) * factor).astype(BF16)
-
-
-def logits_part(factor, parts, draft, target):
+        block = ((probs_q - probs_t) * factor).astype(BF16)
+        dlogits[:, c:e] = block
+        for j in range(2 * per):
+            rows = pl.ds(j % per * COLS_PIECE, COLS_PIECE)
+            term = dot(block, (weight, weight_o)[j // per][rows, c:e], 1, 1)
+            sums[j] = term if sums[j] is None else sums[j] + term
+    for j in range(2 * per):
+        place = lax.rem(row[0] * per + j, 2 * per)
+        out[pl.ds(place * down, down)] = sums[j].astype(BF16).reshape(down, TOKENS_PIECE, COLS_PIECE)
+
+
+def back_part(factor, row, parts, draft, target, weight, weight_o):
     tokens, vocab = draft.shape
-    return pl.pallas_call(
-        functools.partial(logits_kernel, factor),
-        in_specs=[VMEM] * 3,
-        out_specs=[VMEM] * 2,
+    half = weight.shape[0]
+    pieces = (tokens // TOKENS_PIECE) * (2 * half // COLS_PIECE)
+    return pl.pallas_call(
+        functools.partial(back_kernel, factor),
+        in_specs=[pl.BlockSpec(memory_space=pltpu.SMEM)] + [VMEM] * 5,
+        out_specs=[VMEM] * 3,
         out_shape=[
             jax.ShapeDtypeStruct((1, tokens), F32),
             jax.ShapeDtypeStruct((tokens, vocab), BF16),
+            jax.ShapeDtypeStruct((pieces, TOKENS_PIECE, COLS_PIECE), BF16),
         ],
-        compiler_params=params(16),
-        cost_estimate=cost(8 * tokens * vocab, 8 * tokens * vocab),
-        name="logits_part",
-    )(parts, draft, target)
-
-
-def back_kernel(row, dlogits, weight, weight_o, out):
-    half = weight.shape[0]
-    per = half // COLS_PIECE
-    down = dlogits.shape[0] // TOKENS_PIECE
-    for j in range(2 * per):
-        rows = pl.ds(j % per * COLS_PIECE, COLS_PIECE)
-        block = dot(dlogits[...], (weight, weight_o)[j // per][rows], 1, 1).astype(BF16)
-        place = lax.rem(row[0] * per + j, 2 * per)
-        out[pl.ds(place * down, down)] = block.reshape(down, TOKENS_PIECE, COLS_PIECE)
-
-
-def back_part(row, dlogits, weight, weight_o):
-    tokens, vocab = dlogits.shape
-    half = weight.shape[0]
-    pieces = (tokens // TOKENS_PIECE) * (2 * half // COLS_PIECE)
-    return pl.pallas_call(
-        back_kernel,
-        in_specs=[pl.BlockSpec(memory_space=pltpu.SMEM)] + [VMEM] * 3,
-        out_specs=VMEM,
-        out_shape=jax.ShapeDtypeStruct((pieces, TOKENS_PIECE, COLS_PIECE), BF16),
         compiler_params=params(16),
         cost_estimate=cost(4 * tokens * half * vocab, 4 * half * vocab),
         name="back_part",
-    )(row, dlogits, weight, weight_o)
+    )(row, parts, draft, target, weight, weight_o)
 
 
 def sum_kernel(terms, out):
@@ -278,24 +273,28 @@
         weight_o = swap(weight)
     mine = lax.dynamic_slice_in_dim(hidden, row * half, half, 1)
     theirs = lax.dynamic_slice_in_dim(hidden, (1 - row) * half, half, 1)
+
+    acc, probs, stat, weight_v = own_part(mine, target, weight)
+    draft, part, weight_o = draft_part(theirs, acc, probs, stat, weight_o)
+    theirs, part = lax.optimization_barrier((theirs, part))
     with jax.named_scope("swap_hidden"):
         mine_o = swap(theirs)
-
-    acc, probs, stat = own_part(mine, weight, target)
-    draft, part, weight_o = draft_part(theirs, acc, probs, stat, weight_o)
     with jax.named_scope("share_stats"):
         parts = lax.all_to_all(jnp.broadcast_to(part[None], (n,) + part.shape), "vocab", 0, 0)
-    divergence, dlogits = logits_part(vocab * n / 1024.0, parts, draft, target)
+    divergence, dlogits, pieces = back_part(
+        vocab * n / 1024.0, jnp.full((1,), row, jnp.int32), parts, draft, target, weight_v, weight_o
+    )
+    with jax.named_scope("scatter_sum"):
+        terms = lax.all_to_all(pieces, "vocab", 0, 0)
+    dlogits, terms = lax.optimization_barrier((dlogits, terms))
     with jax.named_scope("swap_dlogits"):
         dlogits_o = swap(dlogits)
-    pieces = back_part(jnp.full((1,), row, jnp.int32), dlogits, weight, weight_o)
-    with jax.named_scope("scatter_sum"):
-        terms = lax.all_to_all(pieces, "vocab", 0, 0)
     totals = sum_part(terms)
     with jax.named_scope("gather"):
         gathered = lax.all_to_all(totals, "vocab", 0, 0)
+    head_grad = head_part(mine, mine_o, dlogits, dlogits_o)
+    gathered, head_grad = lax.optimization_barrier((gathered, head_grad))
     hidden_grad = join_part(gathered, tokens, width)
-    head_grad = head_part(mine, mine_o, dlogits, dlogits_o)
     return (divergence.reshape(tokens), hidden_grad, head_grad)
 
 

time: 89.7 us -> 90.4 us (level)
  blocking collectives: 22.2 us -> 44.7 us
  waiting for transfers between devices: 28.8 us -> 12.1 us
  starting transfers between devices: 9.77 us -> 5.33 us
  local copies, waits for them, and re-layouts: 4.9 us -> 3.92 us
    all_to_all x0 -> x1, blocking collectives: none -> 22.5 us  [shards(): terms = lax.all_to_all(pieces, 'vocab', 0, 0)]
    all_to_all x1 -> x0, waiting for transfers between devices: 18 us -> none  [shards(): terms = lax.all_to_all(pieces, 'vocab', 0, 0)]
    all_to_all x1 -> x0, starting transfers between devices: 4.86 us -> none  [shards(): terms = lax.all_to_all(pieces, 'vocab', 0, 0)]
    all_to_all x1, waiting for transfers between devices: 6.51 us -> 9.41 us  [shards(): gathered = lax.all_to_all(totals, 'vocab', 0, 0)]
    ppermute x3, waiting for transfers between devices: 4.33 us -> 2.72 us  [swap(): return lax.ppermute(x, 'rows', SWAP)]
    pallas_call x1, Pallas kernels: 5.19 us -> 4.18 us  [draft_part(): pl.pallas_call(draft_kernel, in_specs=[VMEM] * 4 + [ANY], out_specs=[VMEM...]
    pallas_call x1, Pallas kernels: 0.24 us -> 1.23 us  [sum_part(): pl.pallas_call(sum_kernel, in_specs=[VMEM], out_specs=VMEM, out_shape=jax...]
    unnamed x10 -> x4, local copies, waits for them, and re-layouts: 3.53 us -> 2.55 us
  transfers between devices with their start and end apart: 5 -> 4, of which waited for: 4 -> 3; matrix products, arithmetic and copies ran while one was open for 2% -> 2% of each run, Pallas kernels for 12% -> 15%
where the time goes in v6:
time: 90.4 us; the launch traced here: 89.6 us
  blocking collectives  44.7 us (49%)
  Pallas kernels  22.8 us (25%)
  waiting for transfers between devices  12.1 us (13%)
  starting transfers between devices  5.33 us (6%)
  local copies, waits for them, and re-layouts  3.92 us (4%)
    all_to_all x1, blocking collectives, shards(): terms = lax.all_to_all(pieces, 'vocab', 0, 0)  22.5 us
    all_to_all x1, blocking collectives, shards(): lax.all_to_all(jnp.broadcast_to(part[None], (n,) + part.shape), 'vocab',...  22.2 us
    all_to_all x1, waiting for transfers between devices, shards(): gathered = lax.all_to_all(totals, 'vocab', 0, 0)  9.41 us
    pallas_call x1, Pallas kernels, head_part(): pl.pallas_call(head_kernel, grid=(half // step,), in_specs=[column, colum...  8.3 us
    all_to_all x1, starting transfers between devices, shards(): gathered = lax.all_to_all(totals, 'vocab', 0, 0)  4.65 us
    pallas_call x1, Pallas kernels, back_part(): pl.pallas_call(functools.partial(back_kernel, factor), in_specs=[pl.Block...  4.22 us
    pallas_call x1, Pallas kernels, draft_part(): pl.pallas_call(draft_kernel, in_specs=[VMEM] * 4 + [ANY], out_specs=[VMEM...  4.18 us
    pallas_call x1, Pallas kernels, own_part(): pl.pallas_call(own_kernel, in_specs=[VMEM] * 2 + [ANY], out_specs=[VMEM]...  3.51 us
  transfers between devices with their start and end apart: 4, of which 3 were waited for; matrix products, arithmetic and copies ran while one was open for 2% of the time, Pallas kernels for 15%

profile of v6, /device:TPU:0, one launch (start us, length us, event | category | flops | bytes accessed | tf_op | source)
XLA Modules:
  0.0 89.6 jit_solution(14666161279416280992)
XLA Ops:
  0.6 0.0 copy-start.1
  0.6 0.1 collective-permute-start
  0.7 1.4 %constant_dynamic-slice_fusion = (bf16[256,1024]{1,0:T(8,128)(2,1)S(1)}, bf16[256,1024]{1,0:T(8,128)(2,1)S(1)}) fusion(bf16[256,2048]{1,0:T(8,128)(2,1)} %param.3, s32[]{:T(128)S(6)} %select_n.7, s32[]{:T(128)S(6)} %select_n.6), kind=kLoop, calls=%fused_computation | loop fusion | bytes 2097160 | tf_op jit(solution)/shard_map/dynamic_slice | solution.py:274
  2.1 0.1 copy-done.1
  2.2 0.0 copy-start
  2.2 2.4 %copy-done = bf16[1024,2432]{1,0:T(8,128)(2,1)S(1)} copy-done((bf16[1024,2432]{1,0:T(8,128)(2,1)S(1)}, bf16[1024,2432]{1,0:T(8,128)(2,1)}, u32[]{:S(2)}) %copy-start) | copy-done | bytes 4980760
  4.7 3.5 %own_part.1 = (f32[256,2432]{1,0:T(8,128)S(1)}, f32[256,2432]{1,0:T(8,128)S(1)}, f32[256,128]{1,0:T(8,128)S(1)}, bf16[1024,2432]{1,0:T(8,128)(2,1)S(1)}) custom-call(bf16[256,1024]{1,0:T(8,128)(2,1)S(1)} %get-tuple-element.35.mine, bf16[256,2432]{1,0:T(8,128)(2,1)S(1)} %copy-done.1, bf16[1024,2432]{1,0:T(8,128)(2,1)S(1)} %copy-done), custom_call_target="tpu_custom_call" | custom-call | flops 1275068416 | bytes 4980736 | tf_op jit(solution)/shard_map/own_part/pallas_call | solution.py:82
  8.2 1.2 %collective-permute-done.weight = bf16[1024,2432]{1,0:T(8,128)(2,1)} collective-permute-done((bf16[1024,2432]{1,0:T(8,128)(2,1)}, bf16[1024,2432]{1,0:T(8,128)(2,1)}, u32[]{:S(2)}, u32[]{:S(2)}) %collective-permute-start) | collective-permute-done | bytes 4980768 | tf_op jit(solution)/shard_map/swap_weight/ppermute | solution.py:26
  9.3 4.2 %draft_part.1 = (f32[256,2432]{1,0:T(8,128)S(1)}, f32[8,128]{1,0:T(8,128)S(1)}, bf16[1024,2432]{1,0:T(8,128)(2,1)S(1)}) custom-call(bf16[256,1024]{1,0:T(8,128)(2,1)S(1)} %get-tuple-element.31.theirs, f32[256,2432]{1,0:T(8,128)S(1)} %get-tuple-element.19.acc, f32[256,2432]{1,0:T(8,128)S(1)} %get-tuple-element.20.probs, ...), custom_call_target="tpu_custom_call" | custom-call | flops 1275068416 | bytes 4980736 | tf_op jit(solution)/shard_map/draft_part/pallas_call | solution.py:130
  13.6 22.2 %all_to_all.15.parts = f32[64,8,128]{2,1,0:T(8,128)S(1)} all-to-all(f32[64,8,128]{2,1,0:T(8,128)S(1)} %broadcast_in_dim.10), channel_id=1, replica_groups=mesh['rows'=2,'vocab'=64] {'vocab'}, dimensions={0} | all-to-all | bytes 524288 | tf_op jit(solution)/shard_map/share_stats/all_to_all | solution.py:283
  35.8 4.2 %back_part.1 = (f32[1,256]{1,0:T(1,128)}, bf16[256,2432]{1,0:T(8,128)(2,1)S(1)}, bf16[64,16,512]{2,1,0:T(8,128)(2,1)S(1)}) custom-call(s32[1]{0:T(128)} %bitcast.row, f32[64,8,128]{2,1,0:T(8,128)S(1)} %all_to_all.15.parts, f32[256,2432]{1,0:T(8,128)S(1)} %get-tuple-element.24.draft, bf16[256,2432]{1,0:T(8,128)(2,1)S(1)} %copy-done.1, ...), custom_call_target="tpu_custom_call" | custom-call | flops 2550136832 | bytes 9961472 | tf_op jit(solution)/shard_map/back_part/pallas_call | solution.py:183
  40.0 22.5 %all_to_all.16.terms = bf16[64,16,512]{2,1,0:T(8,128)(2,1)S(1)} all-to-all(bf16[64,16,512]{2,1,0:T(8,128)(2,1)S(1)} %get-tuple-element.29), channel_id=1, replica_groups=mesh['rows'=2,'vocab'=64] {'vocab'}, dimensions={0} | all-to-all | bytes 2097152 | tf_op jit(solution)/shard_map/scatter_sum/all_to_all | solution.py:288
  62.5 0.0 collective-permute-start.2
  62.5 1.2 %sum_part.1 = bf16[64,16,512]{2,1,0:T(8,128)(2,1)} custom-call(bf16[64,16,512]{2,1,0:T(8,128)(2,1)S(1)} %all_to_all.16.terms), custom_call_target="tpu_custom_call" | custom-call | tf_op jit(solution)/shard_map/sum_part/pallas_call | solution.py:206
  63.7 4.7 %all-to-all-start.2 = ((bf16[64,16,512]{2,1,0:T(8,128)(2,1)}), bf16[64,16,512]{2,1,0:T(8,128)(2,1)S(1)}, u32[]{:S(2)}, u32[]{:S(2)}) async-start(bf16[64,16,512]{2,1,0:T(8,128)(2,1)} %sum_part.1), calls=%async_computation.2 | async-start | bytes 2097152 | tf_op jit(solution)/shard_map/gather/all_to_all | solution.py:294
  68.4 0.6 collective-permute-start.1
  69.0 1.5 %collective-permute-done.1.mine_o = bf16[256,1024]{1,0:T(8,128)(2,1)S(1)} collective-permute-done((bf16[256,1024]{1,0:T(8,128)(2,1)S(1)}, bf16[256,1024]{1,0:T(8,128)(2,1)S(1)}, u32[]{:S(2)}, u32[]{:S(2)}) %collective-permute-start.1) | collective-permute-done | bytes 524320 | tf_op jit(solution)/shard_map/swap_hidden/ppermute | solution.py:26
  70.5 0.0 collective-permute-done.2.dlogits_o
  70.5 8.3 %head_part.1 = f32[1024,2432]{1,0:T(8,128)} custom-call(bf16[256,1024]{1,0:T(8,128)(2,1)S(1)} %get-tuple-element.35.mine, bf16[256,1024]{1,0:T(8,128)(2,1)S(1)} %collective-permute-done.1.mine_o, bf16[256,2432]{1,0:T(8,128)(2,1)S(1)} %get-tuple-element.32.dlogits, bf16[256,2432]{1,0:T(8,128)(2,1)} %collective-permute-done.2.dlogits_o), custom_call_target="tpu_custom_call" | custom-call | flops 2550136832 | bytes 9961472 | tf_op jit(solution)/shard_map/head_part/pallas_call | solution.py:254
  78.8 9.4 %all-to-all-done.2.pieces = bf16[64,16,512]{2,1,0:T(8,128)(2,1)S(1)} async-done(((bf16[64,16,512]{2,1,0:T(8,128)(2,1)}), bf16[64,16,512]{2,1,0:T(8,128)(2,1)S(1)}, u32[]{:S(2)}, u32[]{:S(2)}) %all-to-all-start.2) | async-done | bytes 1048608 | tf_op jit(solution)/shard_map/gather/all_to_all | solution.py:294
  88.2 1.4 %join_part.1 = f32[256,2048]{1,0:T(8,128)} custom-call(bf16[64,16,512]{2,1,0:T(8,128)(2,1)S(1)} %all-to-all-done.2.pieces), custom_call_target="tpu_custom_call" | custom-call | tf_op jit(solution)/shard_map/join_part/pallas_call | solution.py:234
  (1 shorter events, 0.0 us)
Async XLA Ops:
  0.6 1.6 %copy-start.1 = (bf16[256,2432]{1,0:T(8,128)(2,1)S(1)}, bf16[256,2432]{1,0:T(8,128)(2,1)}, u32[]{:S(2)}) copy-start(bf16[256,2432]{1,0:T(8,128)(2,1)} %target.3) | copy-start | bytes 3735556
  0.6 8.7 %collective-permute-start = (bf16[1024,2432]{1,0:T(8,128)(2,1)}, bf16[1024,2432]{1,0:T(8,128)(2,1)}, u32[]{:S(2)}, u32[]{:S(2)}) collective-permute-start(bf16[1024,2432]{1,0:T(8,128)(2,1)} %weight.1), channel_id=1, source_target_pairs={{0,64},{64,0},{1,65},{65,1},{2,66},{66,2},{3,67},{67,3},{4,68},{68... | collective-permute-start | bytes 14942216 | tf_op jit(solution)/shard_map/swap_weight/ppermute | solution.py:26
  2.2 2.4 %copy-start = (bf16[1024,2432]{1,0:T(8,128)(2,1)S(1)}, bf16[1024,2432]{1,0:T(8,128)(2,1)}, u32[]{:S(2)}) copy-start(bf16[1024,2432]{1,0:T(8,128)(2,1)} %weight.1) | copy-start | bytes 14942212
  62.5 8.0 %collective-permute-start.2 = (bf16[256,2432]{1,0:T(8,128)(2,1)S(1)}, bf16[256,2432]{1,0:T(8,128)(2,1)}, u32[]{:S(2)}, u32[]{:S(2)}) collective-permute-start(bf16[256,2432]{1,0:T(8,128)(2,1)S(1)} %get-tuple-element.32.dlogits), channel_id=1, source_target_pairs={{0,64},{64,0},{1,65},{65,1},{2,66},{66,2},{3,67},{67,3},{4,68},{68... | collective-permute-start | bytes 3735560 | tf_op jit(solution)/shard_map/swap_dlogits/ppermute | solution.py:26
  63.7 24.5 %all-to-all-start.2 = ((bf16[64,16,512]{2,1,0:T(8,128)(2,1)}), bf16[64,16,512]{2,1,0:T(8,128)(2,1)S(1)}, u32[]{:S(2)}, u32[]{:S(2)}) async-start(bf16[64,16,512]{2,1,0:T(8,128)(2,1)} %sum_part.1), calls=%async_computation.2 | async-start | bytes 2097152 | tf_op jit(solution)/shard_map/gather/all_to_all | solution.py:294
  68.4 2.1 %collective-permute-start.1 = (bf16[256,1024]{1,0:T(8,128)(2,1)S(1)}, bf16[256,1024]{1,0:T(8,128)(2,1)S(1)}, u32[]{:S(2)}, u32[]{:S(2)}) collective-permute-start(bf16[256,1024]{1,0:T(8,128)(2,1)S(1)} %get-tuple-element.31.theirs), channel_id=1, source_target_pairs={{0,64},{64,0},{1,65},{65,1},{2,66},{66,2},{3,67},{67,3},{4,68},{68... | collective-permute-start | bytes 1572872 | tf_op jit(solution)/shard_map/swap_hidden/ppermute | solution.py:26

commit v7 on v6

--- a/solution.py
+++ b/solution.py
@@ -7,7 +7,14 @@
 from jax.experimental.pallas import tpu as pltpu
 from jax.sharding import PartitionSpec as P
 
+SIDE = 4
+PLANE = SIDE * SIDE
+CHIPS = SIDE * PLANE
 SWAP = ((0, 1), (1, 0))
+BOTH = ("rows", "vocab")
+PLANES = [[c * PLANE + i for i in range(PLANE)] for c in range(SIDE)] + [
+    [CHIPS + i * SIDE + c for i in range(PLANE)] for c in range(SIDE)
+]
 TOKENS_PIECE = 16
 COLS_PIECE = 512
 BLOCK = 640
@@ -24,6 +31,10 @@
 
 def swap(x):
     return lax.ppermute(x, "rows", SWAP)
+
+
+def shift(k):
+    return [(PLANES[r + c][i], PLANES[r + (c + k) % SIDE][i]) for r in (0, SIDE) for c in range(SIDE) for i in range(PLANE)]
 
 
 def params(mib):
@@ -171,9 +182,12 @@
             rows = pl.ds(j % per * COLS_PIECE, COLS_PIECE)
             term = dot(block, (weight, weight_o)[j // per][rows, c:e], 1, 1)
             sums[j] = term if sums[j] is None else sums[j] + term
+    along, across = jnp.where(row[0] == 0, 1, SIDE), jnp.where(row[0] == 0, PLANE, 1)
     for j in range(2 * per):
-        place = lax.rem(row[0] * per + j, 2 * per)
-        out[pl.ds(place * down, down)] = sums[j].astype(BF16).reshape(down, TOKENS_PIECE, COLS_PIECE)
+        first = lax.rem(row[0] * per + j, 2 * per) * across
+        total = sums[j].astype(BF16)
+        for i in range(down):
+            out[first + i * along] = total[i * TOKENS_PIECE : (i + 1) * TOKENS_PIECE]
 
 
 def back_part(factor, row, parts, draft, target, weight, weight_o):
@@ -207,39 +221,34 @@
         sum_kernel,
         in_specs=[VMEM],
         out_specs=VMEM,
-        out_shape=jax.ShapeDtypeStruct(terms.shape, BF16),
+        out_shape=jax.ShapeDtypeStruct((PLANE,) + terms.shape[1:], BF16),
         compiler_params=params(8),
         name="sum_part",
     )(terms)
 
 
-def join_kernel(pieces, out, stage, sems):
-    tokens, width = out.shape
-    down = tokens // TOKENS_PIECE
-    steps = sems.shape[0]
+def join_kernel(own, *rest):
+    *pieces, out, stage, sems = rest
     copies = []
-    for step in range(steps):
-        rows = pl.ds(step * tokens // steps, tokens // steps)
-        for i in range(step * down // steps, (step + 1) * down // steps):
-            for j in range(width // COLS_PIECE):
-                place = pl.ds(i * TOKENS_PIECE, TOKENS_PIECE), pl.ds(j * COLS_PIECE, COLS_PIECE)
-                stage[place] = pieces[j * down + i].astype(F32)
-        copies.append(pltpu.make_async_copy(stage.at[rows], out.at[rows], sems.at[step]))
+    for k, piece in enumerate(pieces):
+        stage[k] = piece[...].reshape(stage.shape[1:]).astype(F32)
+        column = pl.multiple_of(lax.rem(own[0] + SIDE - k, SIDE) * COLS_PIECE, COLS_PIECE)
+        copies.append(pltpu.make_async_copy(stage.at[k], out.at[:, pl.ds(column, COLS_PIECE)], sems.at[k]))
         copies[-1].start()
     for copy in copies:
         copy.wait()
 
 
-def join_part(pieces, tokens, width):
+def join_part(own, pieces, tokens, width):
     return pl.pallas_call(
         join_kernel,
-        in_specs=[VMEM],
-        out_specs=HBM,
+        in_specs=[pl.BlockSpec(memory_space=pltpu.SMEM)] + [VMEM] * SIDE,
+        out_specs=ANY,
         out_shape=jax.ShapeDtypeStruct((tokens, width), F32),
-        scratch_shapes=[pltpu.VMEM((tokens, width), F32), pltpu.SemaphoreType.DMA((4,))],
+        scratch_shapes=[pltpu.VMEM((SIDE, tokens, COLS_PIECE), F32), pltpu.SemaphoreType.DMA((SIDE,))],
         compiler_params=params(8),
         name="join_part",
-    )(pieces)
+    )(own, *pieces)
 
 
 def head_kernel(mine, mine_o, dlogits, dlogits_o, out):
@@ -276,9 +285,6 @@
 
     acc, probs, stat, weight_v = own_part(mine, target, weight)
     draft, part, weight_o = draft_part(theirs, acc, probs, stat, weight_o)
-    theirs, part = lax.optimization_barrier((theirs, part))
-    with jax.named_scope("swap_hidden"):
-        mine_o = swap(theirs)
     with jax.named_scope("share_stats"):
         parts = lax.all_to_all(jnp.broadcast_to(part[None], (n,) + part.shape), "vocab", 0, 0)
     divergence, dlogits, pieces = back_part(
@@ -286,15 +292,19 @@
     )
     with jax.named_scope("scatter_sum"):
         terms = lax.all_to_all(pieces, "vocab", 0, 0)
-    dlogits, terms = lax.optimization_barrier((dlogits, terms))
-    with jax.named_scope("swap_dlogits"):
-        dlogits_o = swap(dlogits)
     totals = sum_part(terms)
-    with jax.named_scope("gather"):
-        gathered = lax.all_to_all(totals, "vocab", 0, 0)
+    with jax.named_scope("gather_plane"):
+        plane = lax.all_to_all(totals, BOTH, 0, 0, axis_index_groups=PLANES)
+    dlogits, theirs, plane = lax.optimization_barrier((dlogits, theirs, plane))
+    with jax.named_scope("gather_planes"):
+        planes = [plane] + [lax.ppermute(plane, BOTH, shift(k)) for k in range(1, SIDE)]
+    with jax.named_scope("swap_back"):
+        mine_o, dlogits_o = swap(theirs), swap(dlogits)
     head_grad = head_part(mine, mine_o, dlogits, dlogits_o)
-    gathered, head_grad = lax.optimization_barrier((gathered, head_grad))
-    hidden_grad = join_part(gathered, tokens, width)
+    *planes, head_grad = lax.optimization_barrier((*planes, head_grad))
+    chip = lax.axis_index("vocab")
+    own = jnp.where(row == 0, chip // PLANE, chip % SIDE).astype(jnp.int32)
+    hidden_grad = join_part(own.reshape(1), planes, tokens, width)
     return (divergence.reshape(tokens), hidden_grad, head_grad)
 
 

time: 90.4 us -> 90.7 us (level)
  blocking collectives: 44.7 us -> 56.7 us
  waiting for transfers between devices: 12.1 us -> 2.35 us
  starting transfers between devices: 5.33 us -> 3.08 us
    all_to_all x0 -> x1, blocking collectives: none -> 12 us  [shards(): plane = lax.all_to_all(totals, BOTH, 0, 0, axis_index_groups=PLANES)]
    all_to_all x1 -> x0, waiting for transfers between devices: 9.41 us -> none  [shards(): gathered = lax.all_to_all(totals, 'vocab', 0, 0)]
    all_to_all x1 -> x0, starting transfers between devices: 4.65 us -> none  [shards(): gathered = lax.all_to_all(totals, 'vocab', 0, 0)]
    ppermute x0 -> x3, starting transfers between devices: none -> 2.49 us  [shards(): lax.ppermute(plane, BOTH, shift(k))]
    pallas_call x1, Pallas kernels: 1.38 us -> 2.57 us  [join_part(): pl.pallas_call(join_kernel, in_specs=[pl.BlockSpec(memory_space=pltpu.SME...]
    pallas_call x1, Pallas kernels: 1.23 us -> 0.17 us  [sum_part(): pl.pallas_call(sum_kernel, in_specs=[VMEM], out_specs=VMEM, out_shape=jax...]
  transfers between devices with their start and end apart: 4 -> 6, of which waited for: 3 -> 4; matrix products, arithmetic and copies ran while one was open for 2% -> 2% of each run, Pallas kernels for 15% -> 13%
where the time goes in v7:
time: 90.7 us; the launch traced here: 89.5 us
  blocking collectives  56.7 us (63%)
  Pallas kernels  22.8 us (25%)
  local copies, waits for them, and re-layouts  3.92 us (4%)
  starting transfers between devices  3.08 us (3%)
  waiting for transfers between devices  2.35 us (3%)
    all_to_all x1, blocking collectives, shards(): terms = lax.all_to_all(pieces, 'vocab', 0, 0)  22.5 us
    all_to_all x1, blocking collectives, shards(): lax.all_to_all(jnp.broadcast_to(part[None], (n,) + part.shape), 'vocab',...  22.2 us
    all_to_all x1, blocking collectives, shards(): plane = lax.all_to_all(totals, BOTH, 0, 0, axis_index_groups=PLANES)  12 us
    pallas_call x1, Pallas kernels, head_part(): pl.pallas_call(head_kernel, grid=(half // step,), in_specs=[column, colum...  8.14 us
    pallas_call x1, Pallas kernels, back_part(): pl.pallas_call(functools.partial(back_kernel, factor), in_specs=[pl.Block...  4.22 us
    pallas_call x1, Pallas kernels, draft_part(): pl.pallas_call(draft_kernel, in_specs=[VMEM] * 4 + [ANY], out_specs=[VMEM...  4.18 us
    pallas_call x1, Pallas kernels, own_part(): pl.pallas_call(own_kernel, in_specs=[VMEM] * 2 + [ANY], out_specs=[VMEM]...  3.51 us
    pallas_call x1, Pallas kernels, join_part(): pl.pallas_call(join_kernel, in_specs=[pl.BlockSpec(memory_space=pltpu.SME...  2.57 us
  transfers between devices with their start and end apart: 6, of which 4 were waited for; matrix products, arithmetic and copies ran while one was open for 2% of the time, Pallas kernels for 13%

profile of v7, /device:TPU:0, one launch (start us, length us, event | category | flops | bytes accessed | tf_op | source)
XLA Modules:
  0.0 89.5 jit_solution(11635804014184118559)
XLA Ops:
  0.6 0.0 copy-start.1
  0.6 0.1 collective-permute-start
  0.7 1.4 %constant_dynamic-slice_fusion = (bf16[256,1024]{1,0:T(8,128)(2,1)S(1)}, bf16[256,1024]{1,0:T(8,128)(2,1)S(1)}) fusion(bf16[256,2048]{1,0:T(8,128)(2,1)} %param.3, s32[]{:T(128)S(6)} %select_n.21, s32[]{:T(128)S(6)} %select_n.20), kind=kLoop, calls=%fused_computation | loop fusion | bytes 2097160 | tf_op jit(solution)/shard_map/dynamic_slice | solution.py:283
  2.1 0.1 copy-done.1
  2.2 0.0 copy-start
  2.2 2.4 %copy-done = bf16[1024,2432]{1,0:T(8,128)(2,1)S(1)} copy-done((bf16[1024,2432]{1,0:T(8,128)(2,1)S(1)}, bf16[1024,2432]{1,0:T(8,128)(2,1)}, u32[]{:S(2)}) %copy-start) | copy-done | bytes 4980760
  4.7 3.5 %own_part.1 = (f32[256,2432]{1,0:T(8,128)S(1)}, f32[256,2432]{1,0:T(8,128)S(1)}, f32[256,128]{1,0:T(8,128)S(1)}, bf16[1024,2432]{1,0:T(8,128)(2,1)S(1)}) custom-call(bf16[256,1024]{1,0:T(8,128)(2,1)S(1)} %get-tuple-element.39.mine, bf16[256,2432]{1,0:T(8,128)(2,1)S(1)} %copy-done.1, bf16[1024,2432]{1,0:T(8,128)(2,1)S(1)} %copy-done), custom_call_target="tpu_custom_call" | custom-call | flops 1275068416 | bytes 4980736 | tf_op jit(solution)/shard_map/own_part/pallas_call | solution.py:93
  8.2 1.2 %collective-permute-done.weight = bf16[1024,2432]{1,0:T(8,128)(2,1)} collective-permute-done((bf16[1024,2432]{1,0:T(8,128)(2,1)}, bf16[1024,2432]{1,0:T(8,128)(2,1)}, u32[]{:S(2)}, u32[]{:S(2)}) %collective-permute-start) | collective-permute-done | bytes 4980768 | tf_op jit(solution)/shard_map/swap_weight/ppermute | solution.py:33
  9.3 4.2 %draft_part.1 = (f32[256,2432]{1,0:T(8,128)S(1)}, f32[8,128]{1,0:T(8,128)S(1)}, bf16[1024,2432]{1,0:T(8,128)(2,1)S(1)}) custom-call(bf16[256,1024]{1,0:T(8,128)(2,1)S(1)} %get-tuple-element.32.theirs, f32[256,2432]{1,0:T(8,128)S(1)} %get-tuple-element.21.acc, f32[256,2432]{1,0:T(8,128)S(1)} %get-tuple-element.22.probs, ...), custom_call_target="tpu_custom_call" | custom-call | flops 1275068416 | bytes 4980736 | tf_op jit(solution)/shard_map/draft_part/pallas_call | solution.py:141
  13.6 22.2 %all_to_all.15.parts = f32[64,8,128]{2,1,0:T(8,128)S(1)} all-to-all(f32[64,8,128]{2,1,0:T(8,128)S(1)} %broadcast_in_dim.10), channel_id=1, replica_groups=mesh['rows'=2,'vocab'=64] {'vocab'}, dimensions={0} | all-to-all | bytes 524288 | tf_op jit(solution)/shard_map/share_stats/all_to_all | solution.py:289
  35.8 4.2 %back_part.1 = (f32[1,256]{1,0:T(1,128)}, bf16[256,2432]{1,0:T(8,128)(2,1)S(1)}, bf16[64,16,512]{2,1,0:T(8,128)(2,1)S(1)}) custom-call(s32[1]{0:T(128)} %bitcast.row, f32[64,8,128]{2,1,0:T(8,128)S(1)} %all_to_all.15.parts, f32[256,2432]{1,0:T(8,128)S(1)} %get-tuple-element.25.draft, bf16[256,2432]{1,0:T(8,128)(2,1)S(1)} %copy-done.1, ...), custom_call_target="tpu_custom_call" | custom-call | flops 2550136832 | bytes 9961472 | tf_op jit(solution)/shard_map/back_part/pallas_call | solution.py:197
  40.0 22.5 %all_to_all.16.terms = bf16[64,16,512]{2,1,0:T(8,128)(2,1)S(1)} all-to-all(bf16[64,16,512]{2,1,0:T(8,128)(2,1)S(1)} %get-tuple-element.30), channel_id=1, replica_groups=mesh['rows'=2,'vocab'=64] {'vocab'}, dimensions={0} | all-to-all | bytes 2097152 | tf_op jit(solution)/shard_map/scatter_sum/all_to_all | solution.py:294
  62.5 0.2 sum_part.1
  62.7 12.0 %all_to_all.17.rest_0_ = bf16[16,16,512]{2,1,0:T(8,128)(2,1)} all-to-all(bf16[16,16,512]{2,1,0:T(8,128)(2,1)S(1)} %sum_part.1), channel_id=1, replica_groups={{0,1,2,3,4,5,6,7,8,9,10,11,12,13,14,15},{16,17,18,19,20,21,22,23,24,25,..., dimensions={0} | all-to-all | bytes 524288 | tf_op jit(solution)/shard_map/gather_plane/all_to_all | solution.py:297
  74.6 0.0 collective-permute-start.5
  74.6 0.5 collective-permute-start.4
  75.1 0.8 collective-permute-start.3
  75.9 1.7 %collective-permute-start.2 = (bf16[16,16,512]{2,1,0:T(8,128)(2,1)}, bf16[16,16,512]{2,1,0:T(8,128)(2,1)}, u32[]{:S(2)}, u32[]{:S(2)}) collective-permute-start(bf16[16,16,512]{2,1,0:T(8,128)(2,1)} %all_to_all.17.rest_0_), channel_id=1, source_target_pairs={{0,32},{1,33},{2,34},{3,35},{4,36},{5,37},{6,38},{7,39},{8,40},{9,... | collective-permute-start | bytes 786440 | tf_op jit(solution)/shard_map/gather_planes/ppermute | solution.py:300
  77.6 0.0 collective-permute-start.1
  77.6 0.5 collective-permute-done.4.mine_o
  78.1 0.2 collective-permute-done.5.dlogits_o
  78.3 8.1 %head_part.1 = f32[1024,2432]{1,0:T(8,128)} custom-call(bf16[256,1024]{1,0:T(8,128)(2,1)S(1)} %get-tuple-element.39.mine, bf16[256,1024]{1,0:T(8,128)(2,1)} %collective-permute-done.4.mine_o, bf16[256,2432]{1,0:T(8,128)(2,1)S(1)} %get-tuple-element.33.dlogits, bf16[256,2432]{1,0:T(8,128)(2,1)S(1)} %collective-permute-done.5.dlogits_o), custom_call_target="tpu_custom_call" | custom-call | flops 2550136832 | bytes 9961472 | tf_op jit(solution)/shard_map/head_part/pallas_call | solution.py:263
  86.5 0.0 collective-permute-done.3.rest_3_
  86.5 0.0 collective-permute-done.2.rest_2_
  86.5 0.5 collective-permute-done.1.rest_1_
  86.9 2.6 %join_part.1 = f32[256,2048]{1,0:T(8,128)} custom-call(s32[1]{0:T(128)} %bitcast.2.own, bf16[16,16,512]{2,1,0:T(8,128)(2,1)} %all_to_all.17.rest_0_, bf16[16,16,512]{2,1,0:T(8,128)(2,1)} %collective-permute-done.1.rest_1_, bf16[16,16,512]{2,1,0:T(8,128)(2,1)} %collective-permute-done.2.rest_2_, bf16[16,16,512]{2,1,0:T(8,128)(2,1)} %collective-permute-done.3.rest_3_), custom_call_target="tpu_custom_call" | custom-call | tf_op jit(solution)/shard_map/join_part/pallas_call | solution.py:243
  (1 shorter events, 0.0 us)
Async XLA Ops:
  0.6 1.6 %copy-start.1 = (bf16[256,2432]{1,0:T(8,128)(2,1)S(1)}, bf16[256,2432]{1,0:T(8,128)(2,1)}, u32[]{:S(2)}) copy-start(bf16[256,2432]{1,0:T(8,128)(2,1)} %target.3) | copy-start | bytes 3735556
  0.6 8.7 %collective-permute-start = (bf16[1024,2432]{1,0:T(8,128)(2,1)}, bf16[1024,2432]{1,0:T(8,128)(2,1)}, u32[]{:S(2)}, u32[]{:S(2)}) collective-permute-start(bf16[1024,2432]{1,0:T(8,128)(2,1)} %weight.1), channel_id=1, source_target_pairs={{0,64},{64,0},{1,65},{65,1},{2,66},{66,2},{3,67},{67,3},{4,68},{68... | collective-permute-start | bytes 14942216 | tf_op jit(solution)/shard_map/swap_weight/ppermute | solution.py:33
  2.2 2.4 %copy-start = (bf16[1024,2432]{1,0:T(8,128)(2,1)S(1)}, bf16[1024,2432]{1,0:T(8,128)(2,1)}, u32[]{:S(2)}) copy-start(bf16[1024,2432]{1,0:T(8,128)(2,1)} %weight.1) | copy-start | bytes 14942212
  74.6 3.7 %collective-permute-start.5 = (bf16[256,2432]{1,0:T(8,128)(2,1)S(1)}, bf16[256,2432]{1,0:T(8,128)(2,1)S(1)}, u32[]{:S(2)}, u32[]{:S(2)}) collective-permute-start(bf16[256,2432]{1,0:T(8,128)(2,1)S(1)} %get-tuple-element.33.dlogits), channel_id=1, source_target_pairs={{0,64},{64,0},{1,65},{65,1},{2,66},{66,2},{3,67},{67,3},{4,68},{68... | collective-permute-start | bytes 3735560 | tf_op jit(solution)/shard_map/swap_back/ppermute | solution.py:33
  74.6 3.5 %collective-permute-start.4 = (bf16[256,1024]{1,0:T(8,128)(2,1)S(1)}, bf16[256,1024]{1,0:T(8,128)(2,1)}, u32[]{:S(2)}, u32[]{:S(2)}) collective-permute-start(bf16[256,1024]{1,0:T(8,128)(2,1)S(1)} %get-tuple-element.32.theirs), channel_id=1, source_target_pairs={{0,64},{64,0},{1,65},{65,1},{2,66},{66,2},{3,67},{67,3},{4,68},{68... | collective-permute-start | bytes 1572872 | tf_op jit(solution)/shard_map/swap_back/ppermute | solution.py:33
  75.1 11.3 %collective-permute-start.3 = (bf16[16,16,512]{2,1,0:T(8,128)(2,1)}, bf16[16,16,512]{2,1,0:T(8,128)(2,1)}, u32[]{:S(2)}, u32[]{:S(2)}) collective-permute-start(bf16[16,16,512]{2,1,0:T(8,128)(2,1)} %all_to_all.17.rest_0_), channel_id=1, source_target_pairs={{0,48},{1,49},{2,50},{3,51},{4,52},{5,53},{6,54},{7,55},{8,56},{9,... | collective-permute-start | bytes 786440 | tf_op jit(solution)/shard_map/gather_planes/ppermute | solution.py:300
  75.9 10.5 %collective-permute-start.2 = (bf16[16,16,512]{2,1,0:T(8,128)(2,1)}, bf16[16,16,512]{2,1,0:T(8,128)(2,1)}, u32[]{:S(2)}, u32[]{:S(2)}) collective-permute-start(bf16[16,16,512]{2,1,0:T(8,128)(2,1)} %all_to_all.17.rest_0_), channel_id=1, source_target_pairs={{0,32},{1,33},{2,34},{3,35},{4,36},{5,37},{6,38},{7,39},{8,40},{9,... | collective-permute-start | bytes 786440 | tf_op jit(solution)/shard_map/gather_planes/ppermute | solution.py:300
  77.6 9.3 %collective-permute-start.1 = (bf16[16,16,512]{2,1,0:T(8,128)(2,1)}, bf16[16,16,512]{2,1,0:T(8,128)(2,1)}, u32[]{:S(2)}, u32[]{:S(2)}) collective-permute-start(bf16[16,16,512]{2,1,0:T(8,128)(2,1)} %all_to_all.17.rest_0_), channel_id=1, source_target_pairs={{0,16},{1,17},{2,18},{3,19},{4,20},{5,21},{6,22},{7,23},{8,24},{9,... | collective-permute-start | bytes 786440 | tf_op jit(solution)/shard_map/gather_planes/ppermute | solution.py:300

commit v8 on v7

--- a/solution.py
+++ b/solution.py
@@ -228,12 +228,16 @@
 
 
 def join_kernel(own, *rest):
-    *pieces, out, stage, sems = rest
+    *pieces, out, held, stage, sems, out_sems = rest
+    loads = [pltpu.make_async_copy(piece, held.at[k], sems.at[k]) for k, piece in enumerate(pieces)]
+    for each in loads:
+        each.start()
     copies = []
-    for k, piece in enumerate(pieces):
-        stage[k] = piece[...].reshape(stage.shape[1:]).astype(F32)
+    for k, each in enumerate(loads):
+        each.wait()
+        stage[k] = held[k].reshape(stage.shape[1:]).astype(F32)
         column = pl.multiple_of(lax.rem(own[0] + SIDE - k, SIDE) * COLS_PIECE, COLS_PIECE)
-        copies.append(pltpu.make_async_copy(stage.at[k], out.at[:, pl.ds(column, COLS_PIECE)], sems.at[k]))
+        copies.append(pltpu.make_async_copy(stage.at[k], out.at[:, pl.ds(column, COLS_PIECE)], out_sems.at[k]))
         copies[-1].start()
     for copy in copies:
         copy.wait()
@@ -242,34 +246,59 @@
 def join_part(own, pieces, tokens, width):
     return pl.pallas_call(
         join_kernel,
-        in_specs=[pl.BlockSpec(memory_space=pltpu.SMEM)] + [VMEM] * SIDE,
+        in_specs=[pl.BlockSpec(memory_space=pltpu.SMEM)] + [ANY] * SIDE,
         out_specs=ANY,
         out_shape=jax.ShapeDtypeStruct((tokens, width), F32),
-        scratch_shapes=[pltpu.VMEM((SIDE, tokens, COLS_PIECE), F32), pltpu.SemaphoreType.DMA((SIDE,))],
+        scratch_shapes=[
+            pltpu.VMEM((SIDE, PLANE, TOKENS_PIECE, COLS_PIECE), BF16),
+            pltpu.VMEM((SIDE, tokens, COLS_PIECE), F32),
+            pltpu.SemaphoreType.DMA((SIDE,)),
+            pltpu.SemaphoreType.DMA((SIDE,)),
+        ],
         compiler_params=params(8),
         name="join_part",
     )(own, *pieces)
 
 
-def head_kernel(mine, mine_o, dlogits, dlogits_o, out):
-    out[...] = dot(mine[...], dlogits[...], 0, 0) + dot(mine_o[...], dlogits_o[...], 0, 0)
+def head_kernel(mine, dlogits, mine_o, dlogits_o, out, held, held_o, stage, sems, out_sems):
+    steps, step = stage.shape[:2]
+    loads = [pltpu.make_async_copy(*pair) for pair in ((mine_o, held, sems.at[0]), (dlogits_o, held_o, sems.at[1]))]
+    for each in loads:
+        each.start()
+    copies = []
+    for j in range(steps):
+        part = pl.ds(j * step, step)
+        value = dot(mine[:, part], dlogits[...], 0, 0)
+        if j == 0:
+            for each in loads:
+                each.wait()
+        stage[j] = value + dot(held[:, part], held_o[...], 0, 0)
+        copies.append(pltpu.make_async_copy(stage.at[j], out.at[part], out_sems.at[j]))
+        copies[-1].start()
+    for copy in copies:
+        copy.wait()
 
 
 def head_part(mine, mine_o, dlogits, dlogits_o):
     tokens, half = mine.shape
     vocab = dlogits.shape[1]
     step = 128
-    column = pl.BlockSpec((tokens, step), lambda j: (0, j))
     return pl.pallas_call(
         head_kernel,
-        grid=(half // step,),
-        in_specs=[column, column, VMEM, VMEM],
-        out_specs=pl.BlockSpec((step, vocab), lambda j: (j, 0)),
+        in_specs=[VMEM] * 2 + [ANY] * 2,
+        out_specs=ANY,
         out_shape=jax.ShapeDtypeStruct((half, vocab), F32),
-        compiler_params=params(16),
+        scratch_shapes=[
+            pltpu.VMEM((tokens, half), BF16),
+            pltpu.VMEM((tokens, vocab), BF16),
+            pltpu.VMEM((half // step, step, vocab), F32),
+            pltpu.SemaphoreType.DMA((2,)),
+            pltpu.SemaphoreType.DMA((half // step,)),
+        ],
+        compiler_params=params(24),
         cost_estimate=cost(4 * tokens * half * vocab, 4 * half * vocab),
         name="head_part",
-    )(mine, mine_o, dlogits, dlogits_o)
+    )(mine, dlogits, mine_o, dlogits_o)
 
 
 def shards(hidden, weight, target):
@@ -285,21 +314,25 @@
 
     acc, probs, stat, weight_v = own_part(mine, target, weight)
     draft, part, weight_o = draft_part(theirs, acc, probs, stat, weight_o)
+    theirs, part = lax.optimization_barrier((theirs, part))
+    with jax.named_scope("swap_hidden"):
+        mine_o = swap(theirs)
     with jax.named_scope("share_stats"):
         parts = lax.all_to_all(jnp.broadcast_to(part[None], (n,) + part.shape), "vocab", 0, 0)
     divergence, dlogits, pieces = back_part(
         vocab * n / 1024.0, jnp.full((1,), row, jnp.int32), parts, draft, target, weight_v, weight_o
     )
+    pieces, mine_o = lax.optimization_barrier((pieces, mine_o))
     with jax.named_scope("scatter_sum"):
         terms = lax.all_to_all(pieces, "vocab", 0, 0)
     totals = sum_part(terms)
     with jax.named_scope("gather_plane"):
         plane = lax.all_to_all(totals, BOTH, 0, 0, axis_index_groups=PLANES)
-    dlogits, theirs, plane = lax.optimization_barrier((dlogits, theirs, plane))
+    dlogits, plane = lax.optimization_barrier((dlogits, plane))
     with jax.named_scope("gather_planes"):
         planes = [plane] + [lax.ppermute(plane, BOTH, shift(k)) for k in range(1, SIDE)]
-    with jax.named_scope("swap_back"):
-        mine_o, dlogits_o = swap(theirs), swap(dlogits)
+    with jax.named_scope("swap_dlogits"):
+        dlogits_o = swap(dlogits)
     head_grad = head_part(mine, mine_o, dlogits, dlogits_o)
     *planes, head_grad = lax.optimization_barrier((*planes, head_grad))
     chip = lax.axis_index("vocab")

time: 90.7 us -> 89.3 us (0.985)
  Pallas kernels: 22.8 us -> 19.3 us
  waiting for transfers between devices: 2.35 us -> 4.17 us
  local copies, waits for them, and re-layouts: 3.92 us -> 4.97 us
    pallas_call x1, Pallas kernels: 8.14 us -> 4.87 us  [head_part(): pl.pallas_call(head_kernel, in_specs=[VMEM] * 2 + [ANY] * 2, out_specs=AN...]
    ppermute x3, waiting for transfers between devices: 0.48 us -> 2.92 us  [shards(): lax.ppermute(plane, BOTH, shift(k))]
    unnamed x4 -> x8, local copies, waits for them, and re-layouts: 2.55 us -> 3.6 us
  transfers between devices with their start and end apart: 6 -> 6, of which waited for: 4 -> 4; matrix products, arithmetic and copies ran while one was open for 2% -> 2% of each run, Pallas kernels for 13% -> 14%
where the time goes in v8:
time: 89.3 us; the launch traced here: 88.9 us
  blocking collectives  56.5 us (63%)
  Pallas kernels  19.3 us (22%)
  local copies, waits for them, and re-layouts  4.97 us (6%)
  waiting for transfers between devices  4.17 us (5%)
  starting transfers between devices  3.16 us (4%)
    all_to_all x1, blocking collectives, shards(): terms = lax.all_to_all(pieces, 'vocab', 0, 0)  22.8 us
    all_to_all x1, blocking collectives, shards(): lax.all_to_all(jnp.broadcast_to(part[None], (n,) + part.shape), 'vocab',...  22.4 us
    all_to_all x1, blocking collectives, shards(): plane = lax.all_to_all(totals, BOTH, 0, 0, axis_index_groups=PLANES)  11.3 us
    pallas_call x1, Pallas kernels, head_part(): pl.pallas_call(head_kernel, in_specs=[VMEM] * 2 + [ANY] * 2, out_specs=AN...  4.87 us
    pallas_call x1, Pallas kernels, back_part(): pl.pallas_call(functools.partial(back_kernel, factor), in_specs=[pl.Block...  4.21 us
    pallas_call x1, Pallas kernels, draft_part(): pl.pallas_call(draft_kernel, in_specs=[VMEM] * 4 + [ANY], out_specs=[VMEM...  4.19 us
    unnamed x8, local copies, waits for them, and re-layouts  3.6 us
    pallas_call x1, Pallas kernels, own_part(): pl.pallas_call(own_kernel, in_specs=[VMEM] * 2 + [ANY], out_specs=[VMEM]...  3.5 us
  transfers between devices with their start and end apart: 6, of which 4 were waited for; matrix products, arithmetic and copies ran while one was open for 2% of the time, Pallas kernels for 14%

profile of v8, /device:TPU:0, one launch (start us, length us, event | category | flops | bytes accessed | tf_op | source)
XLA Modules:
  0.0 88.9 jit_solution(17823894796384046249)
XLA Ops:
  0.6 0.0 copy-start.1
  0.6 0.1 collective-permute-start
  0.7 1.4 %constant_dynamic-slice_fusion = (bf16[256,1024]{1,0:T(8,128)(2,1)S(1)}, bf16[256,1024]{1,0:T(8,128)(2,1)S(1)}) fusion(bf16[256,2048]{1,0:T(8,128)(2,1)} %param.3, s32[]{:T(128)S(6)} %select_n.21, s32[]{:T(128)S(6)} %select_n.20), kind=kLoop, calls=%fused_computation | loop fusion | bytes 2097160 | tf_op jit(solution)/shard_map/dynamic_slice | solution.py:312
  2.1 0.1 copy-done.1
  2.2 0.0 copy-start
  2.2 2.4 %copy-done = bf16[1024,2432]{1,0:T(8,128)(2,1)S(1)} copy-done((bf16[1024,2432]{1,0:T(8,128)(2,1)S(1)}, bf16[1024,2432]{1,0:T(8,128)(2,1)}, u32[]{:S(2)}) %copy-start) | copy-done | bytes 4980760
  4.7 3.5 %own_part.1 = (f32[256,2432]{1,0:T(8,128)S(1)}, f32[256,2432]{1,0:T(8,128)S(1)}, f32[256,128]{1,0:T(8,128)S(1)}, bf16[1024,2432]{1,0:T(8,128)(2,1)S(1)}) custom-call(bf16[256,1024]{1,0:T(8,128)(2,1)S(1)} %get-tuple-element.45.mine, bf16[256,2432]{1,0:T(8,128)(2,1)S(1)} %copy-done.1, bf16[1024,2432]{1,0:T(8,128)(2,1)S(1)} %copy-done), custom_call_target="tpu_custom_call" | custom-call | flops 1275068416 | bytes 4980736 | tf_op jit(solution)/shard_map/own_part/pallas_call | solution.py:93
  8.2 1.2 %collective-permute-done.weight = bf16[1024,2432]{1,0:T(8,128)(2,1)} collective-permute-done((bf16[1024,2432]{1,0:T(8,128)(2,1)}, bf16[1024,2432]{1,0:T(8,128)(2,1)}, u32[]{:S(2)}, u32[]{:S(2)}) %collective-permute-start) | collective-permute-done | bytes 4980768 | tf_op jit(solution)/shard_map/swap_weight/ppermute | solution.py:33
  9.3 4.2 %draft_part.1 = (f32[256,2432]{1,0:T(8,128)S(1)}, f32[8,128]{1,0:T(8,128)S(1)}, bf16[1024,2432]{1,0:T(8,128)(2,1)S(1)}) custom-call(bf16[256,1024]{1,0:T(8,128)(2,1)S(1)} %get-tuple-element.35.theirs, f32[256,2432]{1,0:T(8,128)S(1)} %get-tuple-element.24.acc, f32[256,2432]{1,0:T(8,128)S(1)} %get-tuple-element.25.probs, ...), custom_call_target="tpu_custom_call" | custom-call | flops 1275068416 | bytes 4980736 | tf_op jit(solution)/shard_map/draft_part/pallas_call | solution.py:141
  13.5 0.2 collective-permute-start.1
  13.8 22.4 %all_to_all.15.parts = f32[64,8,128]{2,1,0:T(8,128)S(1)} all-to-all(f32[64,8,128]{2,1,0:T(8,128)S(1)} %broadcast_in_dim.10), channel_id=1, replica_groups=mesh['rows'=2,'vocab'=64] {'vocab'}, dimensions={0} | all-to-all | bytes 524288 | tf_op jit(solution)/shard_map/share_stats/all_to_all | solution.py:321
  36.2 4.2 %back_part.1 = (f32[1,256]{1,0:T(1,128)}, bf16[256,2432]{1,0:T(8,128)(2,1)S(1)}, bf16[64,16,512]{2,1,0:T(8,128)(2,1)S(1)}) custom-call(s32[1]{0:T(128)} %bitcast.row, f32[64,8,128]{2,1,0:T(8,128)S(1)} %all_to_all.15.parts, f32[256,2432]{1,0:T(8,128)S(1)} %get-tuple-element.29.draft, bf16[256,2432]{1,0:T(8,128)(2,1)S(1)} %copy-done.1, ...), custom_call_target="tpu_custom_call" | custom-call | flops 2550136832 | bytes 9961472 | tf_op jit(solution)/shard_map/back_part/pallas_call | solution.py:197
  40.4 0.0 collective-permute-done.1.mine_o
  40.4 0.0 copy-start.2
  40.4 22.8 %all_to_all.16.terms = bf16[64,16,512]{2,1,0:T(8,128)(2,1)S(1)} all-to-all(bf16[64,16,512]{2,1,0:T(8,128)(2,1)S(1)} %get-tuple-element.36), channel_id=1, replica_groups=mesh['rows'=2,'vocab'=64] {'vocab'}, dimensions={0} | all-to-all | bytes 2097152 | tf_op jit(solution)/shard_map/scatter_sum/all_to_all | solution.py:327
  63.2 0.2 sum_part.1
  63.4 11.3 %all_to_all.17.rest_0_ = bf16[16,16,512]{2,1,0:T(8,128)(2,1)S(1)} all-to-all(bf16[16,16,512]{2,1,0:T(8,128)(2,1)S(1)} %sum_part.1), channel_id=1, replica_groups={{0,1,2,3,4,5,6,7,8,9,10,11,12,13,14,15},{16,17,18,19,20,21,22,23,24,25,..., dimensions={0} | all-to-all | bytes 524288 | tf_op jit(solution)/shard_map/gather_plane/all_to_all | solution.py:330
  74.7 0.0 collective-permute-start.5
  74.7 1.0 %collective-permute-start.4 = (bf16[16,16,512]{2,1,0:T(8,128)(2,1)S(1)}, bf16[16,16,512]{2,1,0:T(8,128)(2,1)S(1)}, u32[]{:S(2)}, u32[]{:S(2)}) collective-permute-start(bf16[16,16,512]{2,1,0:T(8,128)(2,1)S(1)} %all_to_all.17.rest_0_), channel_id=1, source_target_pairs={{0,48},{1,49},{2,50},{3,51},{4,52},{5,53},{6,54},{7,55},{8,56},{9,... | collective-permute-start | bytes 786440 | tf_op jit(solution)/shard_map/gather_planes/ppermute | solution.py:333
  75.7 0.0 copy-done.2
  75.7 1.7 %collective-permute-start.3 = (bf16[16,16,512]{2,1,0:T(8,128)(2,1)S(1)}, bf16[16,16,512]{2,1,0:T(8,128)(2,1)}, u32[]{:S(2)}, u32[]{:S(2)}) collective-permute-start(bf16[16,16,512]{2,1,0:T(8,128)(2,1)S(1)} %all_to_all.17.rest_0_), channel_id=1, source_target_pairs={{0,32},{1,33},{2,34},{3,35},{4,36},{5,37},{6,38},{7,39},{8,40},{9,... | collective-permute-start | bytes 786440 | tf_op jit(solution)/shard_map/gather_planes/ppermute | solution.py:333
  77.3 0.2 collective-permute-start.2
  77.5 0.1 collective-permute-done.5.dlogits_o
  77.6 0.0 copy-start.3
  77.6 1.0 %copy-done.3 = bf16[256,1024]{1,0:T(8,128)(2,1)S(1)} copy-done((bf16[256,1024]{1,0:T(8,128)(2,1)S(1)}, bf16[256,1024]{1,0:T(8,128)(2,1)}, u32[]{:S(2)}) %copy-start.3) | copy-done | bytes 524312
  78.6 4.9 %head_part.1 = f32[1024,2432]{1,0:T(8,128)} custom-call(bf16[256,1024]{1,0:T(8,128)(2,1)S(1)} %get-tuple-element.45.mine, bf16[256,2432]{1,0:T(8,128)(2,1)S(1)} %get-tuple-element.38.dlogits, bf16[256,1024]{1,0:T(8,128)(2,1)S(1)} %copy-done.3, bf16[256,2432]{1,0:T(8,128)(2,1)S(1)} %collective-permute-done.5.dlogits_o), custom_call_target="tpu_custom_call" | custom-call | flops 2550136832 | bytes 9961472 | tf_op jit(solution)/shard_map/head_part/pallas_call | solution.py:286
  83.5 0.0 collective-permute-done.4.rest_3_
  83.5 0.2 collective-permute-done.3.rest_2_
  83.7 2.7 %collective-permute-done.2.rest_1_ = bf16[16,16,512]{2,1,0:T(8,128)(2,1)} collective-permute-done((bf16[16,16,512]{2,1,0:T(8,128)(2,1)S(1)}, bf16[16,16,512]{2,1,0:T(8,128)(2,1)}, u32[]{:S(2)}, u32[]{:S(2)}) %collective-permute-start.2) | collective-permute-done | bytes 262176 | tf_op jit(solution)/shard_map/gather_planes/ppermute | solution.py:333
  86.4 2.3 %join_part.1 = f32[256,2048]{1,0:T(8,128)} custom-call(s32[1]{0:T(128)} %bitcast.2.own, bf16[16,16,512]{2,1,0:T(8,128)(2,1)S(1)} %all_to_all.17.rest_0_, bf16[16,16,512]{2,1,0:T(8,128)(2,1)} %collective-permute-done.2.rest_1_, bf16[16,16,512]{2,1,0:T(8,128)(2,1)} %collective-permute-done.3.rest_2_, bf16[16,16,512]{2,1,0:T(8,128)(2,1)S(1)} %collective-permute-done.4.rest_3_), custom_call_target="tpu_custom_call" | custom-call | tf_op jit(solution)/shard_map/join_part/pallas_call | solution.py:247
  (1 shorter events, 0.0 us)
Async XLA Ops:
  0.6 1.6 %copy-start.1 = (bf16[256,2432]{1,0:T(8,128)(2,1)S(1)}, bf16[256,2432]{1,0:T(8,128)(2,1)}, u32[]{:S(2)}) copy-start(bf16[256,2432]{1,0:T(8,128)(2,1)} %target.3) | copy-start | bytes 3735556
  0.6 8.7 %collective-permute-start = (bf16[1024,2432]{1,0:T(8,128)(2,1)}, bf16[1024,2432]{1,0:T(8,128)(2,1)}, u32[]{:S(2)}, u32[]{:S(2)}) collective-permute-start(bf16[1024,2432]{1,0:T(8,128)(2,1)} %weight.1), channel_id=1, source_target_pairs={{0,64},{64,0},{1,65},{65,1},{2,66},{66,2},{3,67},{67,3},{4,68},{68... | collective-permute-start | bytes 14942216 | tf_op jit(solution)/shard_map/swap_weight/ppermute | solution.py:33
  2.2 2.4 %copy-start = (bf16[1024,2432]{1,0:T(8,128)(2,1)S(1)}, bf16[1024,2432]{1,0:T(8,128)(2,1)}, u32[]{:S(2)}) copy-start(bf16[1024,2432]{1,0:T(8,128)(2,1)} %weight.1) | copy-start | bytes 14942212
  13.5 26.9 %collective-permute-start.1 = (bf16[256,1024]{1,0:T(8,128)(2,1)S(1)}, bf16[256,1024]{1,0:T(8,128)(2,1)S(1)}, u32[]{:S(2)}, u32[]{:S(2)}) collective-permute-start(bf16[256,1024]{1,0:T(8,128)(2,1)S(1)} %get-tuple-element.35.theirs), channel_id=1, source_target_pairs={{0,64},{64,0},{1,65},{65,1},{2,66},{66,2},{3,67},{67,3},{4,68},{68... | collective-permute-start | bytes 1572872 | tf_op jit(solution)/shard_map/swap_hidden/ppermute | solution.py:33
  40.4 35.2 %copy-start.2 = (bf16[256,1024]{1,0:T(8,128)(2,1)}, bf16[256,1024]{1,0:T(8,128)(2,1)S(1)}, u32[]{:S(2)}) copy-start(bf16[256,1024]{1,0:T(8,128)(2,1)S(1)} %collective-permute-done.1.mine_o) | copy-start | bytes 1572868
  74.7 2.9 %collective-permute-start.5 = (bf16[256,2432]{1,0:T(8,128)(2,1)S(1)}, bf16[256,2432]{1,0:T(8,128)(2,1)S(1)}, u32[]{:S(2)}, u32[]{:S(2)}) collective-permute-start(bf16[256,2432]{1,0:T(8,128)(2,1)S(1)} %get-tuple-element.38.dlogits), channel_id=1, source_target_pairs={{0,64},{64,0},{1,65},{65,1},{2,66},{66,2},{3,67},{67,3},{4,68},{68... | collective-permute-start | bytes 3735560 | tf_op jit(solution)/shard_map/swap_dlogits/ppermute | solution.py:33
  74.7 8.9 %collective-permute-start.4 = (bf16[16,16,512]{2,1,0:T(8,128)(2,1)S(1)}, bf16[16,16,512]{2,1,0:T(8,128)(2,1)S(1)}, u32[]{:S(2)}, u32[]{:S(2)}) collective-permute-start(bf16[16,16,512]{2,1,0:T(8,128)(2,1)S(1)} %all_to_all.17.rest_0_), channel_id=1, source_target_pairs={{0,48},{1,49},{2,50},{3,51},{4,52},{5,53},{6,54},{7,55},{8,56},{9,... | collective-permute-start | bytes 786440 | tf_op jit(solution)/shard_map/gather_planes/ppermute | solution.py:333
  75.7 8.1 %collective-permute-start.3 = (bf16[16,16,512]{2,1,0:T(8,128)(2,1)S(1)}, bf16[16,16,512]{2,1,0:T(8,128)(2,1)}, u32[]{:S(2)}, u32[]{:S(2)}) collective-permute-start(bf16[16,16,512]{2,1,0:T(8,128)(2,1)S(1)} %all_to_all.17.rest_0_), channel_id=1, source_target_pairs={{0,32},{1,33},{2,34},{3,35},{4,36},{5,37},{6,38},{7,39},{8,40},{9,... | collective-permute-start | bytes 786440 | tf_op jit(solution)/shard_map/gather_planes/ppermute | solution.py:333
  77.3 9.1 %collective-permute-start.2 = (bf16[16,16,512]{2,1,0:T(8,128)(2,1)S(1)}, bf16[16,16,512]{2,1,0:T(8,128)(2,1)}, u32[]{:S(2)}, u32[]{:S(2)}) collective-permute-start(bf16[16,16,512]{2,1,0:T(8,128)(2,1)S(1)} %all_to_all.17.rest_0_), channel_id=1, source_target_pairs={{0,16},{1,17},{2,18},{3,19},{4,20},{5,21},{6,22},{7,23},{8,24},{9,... | collective-permute-start | bytes 786440 | tf_op jit(solution)/shard_map/gather_planes/ppermute | solution.py:333
  77.6 1.0 %copy-start.3 = (bf16[256,1024]{1,0:T(8,128)(2,1)S(1)}, bf16[256,1024]{1,0:T(8,128)(2,1)}, u32[]{:S(2)}) copy-start(bf16[256,1024]{1,0:T(8,128)(2,1)} %copy-done.2) | copy-start | bytes 1572868

commit v9 on v6

--- a/solution.py
+++ b/solution.py
@@ -40,6 +40,11 @@
 
 def blocks(n):
     return [(c, min(c + BLOCK, n)) for c in range(0, n, BLOCK)]
+
+
+def thirds(n):
+    step = pl.cdiv(n // 128, 3) * 128
+    return [(c, min(c + step, n)) for c in range(0, n, step)]
 
 
 def tiles(x):
@@ -143,7 +148,7 @@
     )(theirs, acc, probs, stat, weight)
 
 
-def back_kernel(factor, row, parts, draft, target, weight, weight_o, divergence, dlogits, out):
+def back_kernel(factor, row, parts, draft, target, weight, weight_o, divergence, out, *dlogits):
     lines = draft.shape[0] // 128
     every = parts[...]
     top = jnp.max(every, axis=0)
@@ -160,13 +165,13 @@
 
     half = weight.shape[0]
     per = half // COLS_PIECE
-    down = dlogits.shape[0] // TOKENS_PIECE
+    down = draft.shape[0] // TOKENS_PIECE
     sums = [None] * (2 * per)
-    for c, e in blocks(draft.shape[1]):
+    for kept, (c, e) in zip(dlogits, thirds(draft.shape[1])):
         probs_q = exp(draft[:, c:e] - lse_q)
         probs_t = exp(target[:, c:e].astype(F32) - lse_t)
         block = ((probs_q - probs_t) * factor).astype(BF16)
-        dlogits[:, c:e] = block
+        kept[...] = block
         for j in range(2 * per):
             rows = pl.ds(j % per * COLS_PIECE, COLS_PIECE)
             term = dot(block, (weight, weight_o)[j // per][rows, c:e], 1, 1)
@@ -183,12 +188,12 @@
     return pl.pallas_call(
         functools.partial(back_kernel, factor),
         in_specs=[pl.BlockSpec(memory_space=pltpu.SMEM)] + [VMEM] * 5,
-        out_specs=[VMEM] * 3,
+        out_specs=[VMEM] * 5,
         out_shape=[
             jax.ShapeDtypeStruct((1, tokens), F32),
-            jax.ShapeDtypeStruct((tokens, vocab), BF16),
             jax.ShapeDtypeStruct((pieces, TOKENS_PIECE, COLS_PIECE), BF16),
-        ],
+        ]
+        + [jax.ShapeDtypeStruct((tokens, e - c), BF16) for c, e in thirds(vocab)],
         compiler_params=params(16),
         cost_estimate=cost(4 * tokens * half * vocab, 4 * half * vocab),
         name="back_part",
@@ -234,7 +239,7 @@
     return pl.pallas_call(
         join_kernel,
         in_specs=[VMEM],
-        out_specs=HBM,
+        out_specs=ANY,
         out_shape=jax.ShapeDtypeStruct((tokens, width), F32),
         scratch_shapes=[pltpu.VMEM((tokens, width), F32), pltpu.SemaphoreType.DMA((4,))],
         compiler_params=params(8),
@@ -242,25 +247,47 @@
     )(pieces)
 
 
-def head_kernel(mine, mine_o, dlogits, dlogits_o, out):
-    out[...] = dot(mine[...], dlogits[...], 0, 0) + dot(mine_o[...], dlogits_o[...], 0, 0)
+def head_kernel(mine, *rest):
+    dlogits, (mine_o, *dlogits_o), (out, held, *held_o, stage, sems, out_sems) = rest[:3], rest[3:7], rest[7:]
+    steps, step = stage.shape[:2]
+    pairs = zip((mine_o, *dlogits_o), (held, *held_o))
+    loads = [pltpu.make_async_copy(*pair, sems.at[i]) for i, pair in enumerate(pairs)]
+    for each in loads:
+        each.start()
+    copies = []
+    for j in range(steps):
+        part = pl.ds(j * step, step)
+        for i, (c, e) in enumerate(thirds(out.shape[1])):
+            value = dot(mine[:, part], dlogits[i][...], 0, 0)
+            if j == 0:
+                for each in (loads[:2] if i == 0 else loads[i + 1 : i + 2]):
+                    each.wait()
+            stage[j, :, c:e] = value + dot(held[:, part], held_o[i][...], 0, 0)
+        copies.append(pltpu.make_async_copy(stage.at[j], out.at[part], out_sems.at[j]))
+        copies[-1].start()
+    for copy in copies:
+        copy.wait()
 
 
 def head_part(mine, mine_o, dlogits, dlogits_o):
     tokens, half = mine.shape
-    vocab = dlogits.shape[1]
+    vocab = sum(x.shape[1] for x in dlogits)
     step = 128
-    column = pl.BlockSpec((tokens, step), lambda j: (0, j))
     return pl.pallas_call(
         head_kernel,
-        grid=(half // step,),
-        in_specs=[column, column, VMEM, VMEM],
-        out_specs=pl.BlockSpec((step, vocab), lambda j: (j, 0)),
+        in_specs=[VMEM] * 4 + [ANY] * 4,
+        out_specs=ANY,
         out_shape=jax.ShapeDtypeStruct((half, vocab), F32),
-        compiler_params=params(16),
+        scratch_shapes=[pltpu.VMEM(x.shape, BF16) for x in (mine_o, *dlogits_o)]
+        + [
+            pltpu.VMEM((half // step, step, vocab), F32),
+            pltpu.SemaphoreType.DMA((4,)),
+            pltpu.SemaphoreType.DMA((half // step,)),
+        ],
+        compiler_params=params(24),
         cost_estimate=cost(4 * tokens * half * vocab, 4 * half * vocab),
         name="head_part",
-    )(mine, mine_o, dlogits, dlogits_o)
+    )(mine, *dlogits, mine_o, *dlogits_o)
 
 
 def shards(hidden, weight, target):
@@ -276,24 +303,20 @@
 
     acc, probs, stat, weight_v = own_part(mine, target, weight)
     draft, part, weight_o = draft_part(theirs, acc, probs, stat, weight_o)
-    theirs, part = lax.optimization_barrier((theirs, part))
-    with jax.named_scope("swap_hidden"):
-        mine_o = swap(theirs)
     with jax.named_scope("share_stats"):
         parts = lax.all_to_all(jnp.broadcast_to(part[None], (n,) + part.shape), "vocab", 0, 0)
-    divergence, dlogits, pieces = back_part(
+    divergence, pieces, *dlogits = back_part(
         vocab * n / 1024.0, jnp.full((1,), row, jnp.int32), parts, draft, target, weight_v, weight_o
     )
     with jax.named_scope("scatter_sum"):
         terms = lax.all_to_all(pieces, "vocab", 0, 0)
-    dlogits, terms = lax.optimization_barrier((dlogits, terms))
-    with jax.named_scope("swap_dlogits"):
-        dlogits_o = swap(dlogits)
+    with jax.named_scope("swap_back"):
+        mine_o, dlogits_o = swap(theirs), [swap(x) for x in dlogits]
+    head_grad = head_part(mine, mine_o, dlogits, dlogits_o)
+    terms, head_grad = lax.optimization_barrier((terms, head_grad))
     totals = sum_part(terms)
     with jax.named_scope("gather"):
         gathered = lax.all_to_all(totals, "vocab", 0, 0)
-    head_grad = head_part(mine, mine_o, dlogits, dlogits_o)
-    gathered, head_grad = lax.optimization_barrier((gathered, head_grad))
     hidden_grad = join_part(gathered, tokens, width)
     return (divergence.reshape(tokens), hidden_grad, head_grad)
 

time: 90.4 us -> 87.5 us (0.968)
  Pallas kernels: 22.8 us -> 19.7 us
  local copies, waits for them, and re-layouts: 3.92 us -> 5 us
    pallas_call x2, Pallas kernels: 9.68 us -> 7.07 us  [the longest x1 5.69 us: head_part(): pl.pallas_call(head_kernel, in_specs=[VMEM] * 4 + [ANY] * 4, out_specs=AN...]
    unnamed x4 -> x6, local copies, waits for them, and re-layouts: 2.55 us -> 3.7 us
    all_to_all x1, blocking collectives: 22.5 us -> 21.5 us  [shards(): gathered = lax.all_to_all(totals, 'vocab', 0, 0)]
    pallas_call x1, Pallas kernels: 1.23 us -> 0.24 us  [sum_part(): pl.pallas_call(sum_kernel, in_specs=[VMEM], out_specs=VMEM, out_shape=jax...]
    ppermute x3 -> x5, waiting for transfers between devices: 2.72 us -> 2.78 us  [swap(): return lax.ppermute(x, 'rows', SWAP)]
  transfers between devices with their start and end apart: 4 -> 6, of which waited for: 3 -> 4; matrix products, arithmetic and copies ran while one was open for 2% -> 1% of each run, Pallas kernels for 15% -> 11%
where the time goes in v9:
time: 87.5 us; the launch traced here: 87.1 us
  blocking collectives  44 us (50%)
  Pallas kernels  19.7 us (23%)
  waiting for transfers between devices  11.5 us (13%)
  starting transfers between devices  6.04 us (7%)
  local copies, waits for them, and re-layouts  5 us (6%)
  between operations  0.88 us (1%)
    all_to_all x1, blocking collectives, shards(): lax.all_to_all(jnp.broadcast_to(part[None], (n,) + part.shape), 'vocab',...  22.5 us
    all_to_all x1, blocking collectives, shards(): gathered = lax.all_to_all(totals, 'vocab', 0, 0)  21.5 us
    all_to_all x1, waiting for transfers between devices, shards(): terms = lax.all_to_all(pieces, 'vocab', 0, 0)  8.73 us
    pallas_call x1, Pallas kernels, head_part(): pl.pallas_call(head_kernel, in_specs=[VMEM] * 4 + [ANY] * 4, out_specs=AN...  5.69 us
    all_to_all x1, starting transfers between devices, shards(): terms = lax.all_to_all(pieces, 'vocab', 0, 0)  4.86 us
    pallas_call x1, Pallas kernels, back_part(): pl.pallas_call(functools.partial(back_kernel, factor), in_specs=[pl.Block...  4.62 us
    pallas_call x1, Pallas kernels, draft_part(): pl.pallas_call(draft_kernel, in_specs=[VMEM] * 4 + [ANY], out_specs=[VMEM...  4.29 us
    unnamed x6, local copies, waits for them, and re-layouts  3.7 us
  transfers between devices with their start and end apart: 6, of which 4 were waited for; matrix products, arithmetic and copies ran while one was open for 1% of the time, Pallas kernels for 11%

profile of v9, /device:TPU:0, one launch (start us, length us, event | category | flops | bytes accessed | tf_op | source)
XLA Modules:
  0.0 87.1 jit_solution(1515584727364816690)
XLA Ops:
  0.6 0.1 collective-permute-start
  0.7 1.3 %constant_dynamic-slice_fusion = (bf16[256,1024]{1,0:T(8,128)(2,1)S(1)}, bf16[256,1024]{1,0:T(8,128)(2,1)S(1)}) fusion(bf16[256,2048]{1,0:T(8,128)(2,1)} %param.3, s32[]{:T(128)S(6)} %select_n.7, s32[]{:T(128)S(6)} %select_n.6), kind=kLoop, calls=%fused_computation | loop fusion | bytes 2097160 | tf_op jit(solution)/shard_map/dynamic_slice | solution.py:301
  2.0 0.0 copy-start
  2.0 2.4 %copy-done = bf16[1024,2432]{1,0:T(8,128)(2,1)S(1)} copy-done((bf16[1024,2432]{1,0:T(8,128)(2,1)S(1)}, bf16[1024,2432]{1,0:T(8,128)(2,1)}, u32[]{:S(2)}) %copy-start) | copy-done | bytes 4980760
  4.4 0.0 copy-start.1
  4.4 1.3 %copy-done.1 = bf16[256,2432]{1,0:T(8,128)(2,1)S(1)} copy-done((bf16[256,2432]{1,0:T(8,128)(2,1)S(1)}, bf16[256,2432]{1,0:T(8,128)(2,1)}, u32[]{:S(2)}) %copy-start.1) | copy-done | bytes 1245208
  5.7 3.5 %own_part.1 = (f32[256,2432]{1,0:T(8,128)S(1)}, f32[256,2432]{1,0:T(8,128)S(1)}, f32[256,128]{1,0:T(8,128)S(1)}, bf16[1024,2432]{1,0:T(8,128)(2,1)S(1)}) custom-call(bf16[256,1024]{1,0:T(8,128)(2,1)S(1)} %get-tuple-element.31.mine, bf16[256,2432]{1,0:T(8,128)(2,1)S(1)} %copy-done.1, bf16[1024,2432]{1,0:T(8,128)(2,1)S(1)} %copy-done), custom_call_target="tpu_custom_call" | custom-call | flops 1275068416 | bytes 4980736 | tf_op jit(solution)/shard_map/own_part/pallas_call | solution.py:87
  9.2 0.1 collective-permute-done.weight
  9.3 0.0 copy-start.2
  9.3 4.3 %draft_part.1 = (f32[256,2432]{1,0:T(8,128)S(1)}, f32[8,128]{1,0:T(8,128)S(1)}, bf16[1024,2432]{1,0:T(8,128)(2,1)S(1)}) custom-call(bf16[256,1024]{1,0:T(8,128)(2,1)S(1)} %get-tuple-element.32.theirs, f32[256,2432]{1,0:T(8,128)S(1)} %get-tuple-element.17.acc, f32[256,2432]{1,0:T(8,128)S(1)} %get-tuple-element.18.probs, ...), custom_call_target="tpu_custom_call" | custom-call | flops 1275068416 | bytes 4980736 | tf_op jit(solution)/shard_map/draft_part/pallas_call | solution.py:135
  13.7 22.5 %all_to_all.15.parts = f32[64,8,128]{2,1,0:T(8,128)S(1)} all-to-all(f32[64,8,128]{2,1,0:T(8,128)S(1)} %broadcast_in_dim.10), channel_id=1, replica_groups=mesh['rows'=2,'vocab'=64] {'vocab'}, dimensions={0} | all-to-all | bytes 524288 | tf_op jit(solution)/shard_map/share_stats/all_to_all | solution.py:307
  36.1 0.0 copy-done.2
  36.1 4.6 %back_part.1 = (f32[1,256]{1,0:T(1,128)}, bf16[64,16,512]{2,1,0:T(8,128)(2,1)}, bf16[256,896]{1,0:T(8,128)(2,1)S(1)}, bf16[256,896]{1,0:T(8,128)(2,1)S(1)}, bf16[256,640]{1,0:T(8,128)(2,1)S(1)}) custom-call(s32[1]{0:T(128)} %bitcast.row, f32[64,8,128]{2,1,0:T(8,128)S(1)} %all_to_all.15.parts, f32[256,2432]{1,0:T(8,128)S(1)} %get-tuple-element.21.draft, ...), custom_call_target="tpu_custom_call" | custom-call | flops 2550136832 | bytes 9961472 | tf_op jit(solution)/shard_map/back_part/pallas_call | solution.py:188
  40.8 4.9 %all-to-all-start.1 = ((bf16[64,16,512]{2,1,0:T(8,128)(2,1)}), bf16[64,16,512]{2,1,0:T(8,128)(2,1)S(1)}, u32[]{:S(2)}, u32[]{:S(2)}) async-start(bf16[64,16,512]{2,1,0:T(8,128)(2,1)} %get-tuple-element.25), calls=%async_computation.1 | async-start | bytes 2097152 | tf_op jit(solution)/shard_map/scatter_sum/all_to_all | solution.py:312
  45.6 0.1 collective-permute-start.1
  45.7 0.5 collective-permute-start.2
  46.2 0.1 collective-permute-start.3
  46.3 0.4 collective-permute-start.4
  46.7 0.9 %collective-permute-done.1.rest_3_ = bf16[256,1024]{1,0:T(8,128)(2,1)S(1)} collective-permute-done((bf16[256,1024]{1,0:T(8,128)(2,1)S(1)}, bf16[256,1024]{1,0:T(8,128)(2,1)S(1)}, u32[]{:S(2)}, u32[]{:S(2)}) %collective-permute-start.1) | collective-permute-done | bytes 524320 | tf_op jit(solution)/shard_map/swap_back/ppermute | solution.py:26
  47.6 1.8 %collective-permute-done.4.rest_6_ = bf16[256,640]{1,0:T(8,128)(2,1)S(1)} collective-permute-done((bf16[256,640]{1,0:T(8,128)(2,1)S(1)}, bf16[256,640]{1,0:T(8,128)(2,1)S(1)}, u32[]{:S(2)}, u32[]{:S(2)}) %collective-permute-start.4) | collective-permute-done | bytes 327712 | tf_op jit(solution)/shard_map/swap_back/ppermute | solution.py:26
  49.4 0.0 collective-permute-done.2.rest_4_
  49.4 0.0 collective-permute-done.3.rest_5_
  49.4 5.7 %head_part.1 = f32[1024,2432]{1,0:T(8,128)} custom-call(bf16[256,1024]{1,0:T(8,128)(2,1)S(1)} %get-tuple-element.31.mine, bf16[256,896]{1,0:T(8,128)(2,1)S(1)} %get-tuple-element.26.rest_0_, bf16[256,896]{1,0:T(8,128)(2,1)S(1)} %get-tuple-element.27.rest_1_, bf16[256,640]{1,0:T(8,128)(2,1)S(1)} %get-tuple-element.28.rest_2_, ...), custom_call_target="tpu_custom_call" | custom-call | flops 2550136832 | bytes 9961472 | tf_op jit(solution)/shard_map/head_part/pallas_call | solution.py:276
  55.1 8.7 %all-to-all-done.1.terms = bf16[64,16,512]{2,1,0:T(8,128)(2,1)S(1)} async-done(((bf16[64,16,512]{2,1,0:T(8,128)(2,1)}), bf16[64,16,512]{2,1,0:T(8,128)(2,1)S(1)}, u32[]{:S(2)}, u32[]{:S(2)}) %all-to-all-start.1) | async-done | bytes 1048608 | tf_op jit(solution)/shard_map/scatter_sum/all_to_all | solution.py:312
  63.8 0.2 sum_part.1
  64.1 21.5 %all_to_all.16.pieces = bf16[64,16,512]{2,1,0:T(8,128)(2,1)S(1)} all-to-all(bf16[64,16,512]{2,1,0:T(8,128)(2,1)S(1)} %sum_part.1), channel_id=1, replica_groups=mesh['rows'=2,'vocab'=64] {'vocab'}, dimensions={0} | all-to-all | bytes 2097152 | tf_op jit(solution)/shard_map/gather/all_to_all | solution.py:319
  85.6 1.4 %join_part.1 = f32[256,2048]{1,0:T(8,128)} custom-call(bf16[64,16,512]{2,1,0:T(8,128)(2,1)S(1)} %all_to_all.16.pieces), custom_call_target="tpu_custom_call" | custom-call | tf_op jit(solution)/shard_map/join_part/pallas_call | solution.py:239
  (1 shorter events, 0.0 us)
Async XLA Ops:
  0.6 8.7 %collective-permute-start = (bf16[1024,2432]{1,0:T(8,128)(2,1)}, bf16[1024,2432]{1,0:T(8,128)(2,1)}, u32[]{:S(2)}, u32[]{:S(2)}) collective-permute-start(bf16[1024,2432]{1,0:T(8,128)(2,1)} %weight.1), channel_id=1, source_target_pairs={{0,64},{64,0},{1,65},{65,1},{2,66},{66,2},{3,67},{67,3},{4,68},{68... | collective-permute-start | bytes 14942216 | tf_op jit(solution)/shard_map/swap_weight/ppermute | solution.py:26
  2.0 2.4 %copy-start = (bf16[1024,2432]{1,0:T(8,128)(2,1)S(1)}, bf16[1024,2432]{1,0:T(8,128)(2,1)}, u32[]{:S(2)}) copy-start(bf16[1024,2432]{1,0:T(8,128)(2,1)} %weight.1) | copy-start | bytes 14942212
  4.4 1.3 %copy-start.1 = (bf16[256,2432]{1,0:T(8,128)(2,1)S(1)}, bf16[256,2432]{1,0:T(8,128)(2,1)}, u32[]{:S(2)}) copy-start(bf16[256,2432]{1,0:T(8,128)(2,1)} %target.3) | copy-start | bytes 3735556
  9.3 26.8 %copy-start.2 = (bf16[256,2432]{1,0:T(8,128)(2,1)S(1)}, bf16[256,2432]{1,0:T(8,128)(2,1)}, u32[]{:S(2)}) copy-start(bf16[256,2432]{1,0:T(8,128)(2,1)} %target.3) | copy-start | bytes 3735556
  40.8 23.1 %all-to-all-start.1 = ((bf16[64,16,512]{2,1,0:T(8,128)(2,1)}), bf16[64,16,512]{2,1,0:T(8,128)(2,1)S(1)}, u32[]{:S(2)}, u32[]{:S(2)}) async-start(bf16[64,16,512]{2,1,0:T(8,128)(2,1)} %get-tuple-element.25), calls=%async_computation.1 | async-start | bytes 2097152 | tf_op jit(solution)/shard_map/scatter_sum/all_to_all | solution.py:312
  45.6 2.0 %collective-permute-start.1 = (bf16[256,1024]{1,0:T(8,128)(2,1)S(1)}, bf16[256,1024]{1,0:T(8,128)(2,1)S(1)}, u32[]{:S(2)}, u32[]{:S(2)}) collective-permute-start(bf16[256,1024]{1,0:T(8,128)(2,1)S(1)} %get-tuple-element.32.theirs), channel_id=1, source_target_pairs={{0,64},{64,0},{1,65},{65,1},{2,66},{66,2},{3,67},{67,3},{4,68},{68... | collective-permute-start | bytes 1572872 | tf_op jit(solution)/shard_map/swap_back/ppermute | solution.py:26
  45.7 3.7 %collective-permute-start.2 = (bf16[256,896]{1,0:T(8,128)(2,1)S(1)}, bf16[256,896]{1,0:T(8,128)(2,1)S(1)}, u32[]{:S(2)}, u32[]{:S(2)}) collective-permute-start(bf16[256,896]{1,0:T(8,128)(2,1)S(1)} %get-tuple-element.26.rest_0_), channel_id=1, source_target_pairs={{0,64},{64,0},{1,65},{65,1},{2,66},{66,2},{3,67},{67,3},{4,68},{68... | collective-permute-start | bytes 1376264 | tf_op jit(solution)/shard_map/swap_back/ppermute | solution.py:26
  46.2 3.2 %collective-permute-start.3 = (bf16[256,896]{1,0:T(8,128)(2,1)S(1)}, bf16[256,896]{1,0:T(8,128)(2,1)S(1)}, u32[]{:S(2)}, u32[]{:S(2)}) collective-permute-start(bf16[256,896]{1,0:T(8,128)(2,1)S(1)} %get-tuple-element.27.rest_1_), channel_id=1, source_target_pairs={{0,64},{64,0},{1,65},{65,1},{2,66},{66,2},{3,67},{67,3},{4,68},{68... | collective-permute-start | bytes 1376264 | tf_op jit(solution)/shard_map/swap_back/ppermute | solution.py:26
  46.3 3.1 %collective-permute-start.4 = (bf16[256,640]{1,0:T(8,128)(2,1)S(1)}, bf16[256,640]{1,0:T(8,128)(2,1)S(1)}, u32[]{:S(2)}, u32[]{:S(2)}) collective-permute-start(bf16[256,640]{1,0:T(8,128)(2,1)S(1)} %get-tuple-element.28.rest_2_), channel_id=1, source_target_pairs={{0,64},{64,0},{1,65},{65,1},{2,66},{66,2},{3,67},{67,3},{4,68},{68... | collective-permute-start | bytes 983048 | tf_op jit(solution)/shard_map/swap_back/ppermute | solution.py:26

commit v10 on v9

--- a/solution.py
+++ b/solution.py
@@ -10,11 +10,12 @@
 SWAP = ((0, 1), (1, 0))
 TOKENS_PIECE = 16
 COLS_PIECE = 512
+PARTS = 4
 BLOCK = 640
 LOG2E = math.log2(math.e)
 F32, BF16 = jnp.float32, jnp.bfloat16
 VMEM = pl.BlockSpec(memory_space=pltpu.VMEM)
-HBM = pl.BlockSpec(memory_space=pltpu.HBM)
+SMEM = pl.BlockSpec(memory_space=pltpu.SMEM)
 ANY = pl.BlockSpec(memory_space=pl.ANY)
 
 
@@ -55,18 +56,39 @@
     return pl.cdiv(3 * tokens // 128, 8) * 8
 
 
-def load(source, target, sems):
+def own_half(x, row, half):
+    return x[:, pl.ds(pl.multiple_of(row[0] * half, 128), half)]
+
+
+def cross_kernel(start, row, hidden_o, weight, out):
+    half = weight.shape[0]
+    out[...] = dot(own_half(hidden_o, row, half), weight[:, start : start + out.shape[1]], 1, 0)
+
+
+def cross_part(row, hidden_o, weight, start, stop):
+    tokens, half = hidden_o.shape[0], weight.shape[0]
+    return pl.pallas_call(
+        functools.partial(cross_kernel, start),
+        in_specs=[SMEM] + [VMEM] * 2,
+        out_specs=VMEM,
+        out_shape=jax.ShapeDtypeStruct((tokens, stop - start), F32),
+        compiler_params=params(8),
+        cost_estimate=cost(2 * tokens * half * (stop - start), 2 * half * (stop - start)),
+        name="cross_part",
+    )(row, hidden_o, weight)
+
+
+def own_kernel(row, hidden, target, weight, acc, probs, stat, *rest):
+    *parts, sems = rest
+    half, vocab = weight.shape
+    rows = parts[0].shape[0]
     copies = []
-    for j, (c, e) in enumerate(blocks(source.shape[1])):
-        part = pl.ds(c, e - c)
-        copies.append(pltpu.make_async_copy(source.at[:, part], target.at[:, part], sems.at[j]))
+    for k, part in enumerate(parts):
+        copies.append(pltpu.make_async_copy(weight.at[pl.ds(k * rows, rows)], part, sems.at[k]))
         copies[-1].start()
-    return copies
-
-
-def own_kernel(mine, target, weight, acc, probs, stat, buffer, sems):
-    vocab = target.shape[1]
-    copies = load(weight, buffer, sems)
+    mine = own_half(hidden, row, half)
+    for c, e in blocks(vocab):
+        acc[:, c:e] = dot(mine, weight[:, c:e], 1, 0)
     wide = target[...].astype(F32)
     peak = jnp.max(wide, axis=1, keepdims=True)
     terms = exp(wide - peak)
@@ -76,43 +98,41 @@
     mean = jnp.sum(terms * wide, axis=1, keepdims=True)
     lane = lax.broadcasted_iota(jnp.int32, stat.shape, 1)
     stat[...] = jnp.where(lane == 0, peak + jnp.log(total), mean)
-    for copy, (c, e) in zip(copies, blocks(vocab)):
+    for copy in copies:
         copy.wait()
-        acc[:, c:e] = dot(mine[...], buffer[:, c:e], 1, 0)
-
-
-def own_part(mine, target, weight):
-    tokens, half = mine.shape
-    vocab = target.shape[1]
+
+
+def own_part(row, hidden, target, weight):
+    tokens = hidden.shape[0]
+    half, vocab = weight.shape
     return pl.pallas_call(
         own_kernel,
-        in_specs=[VMEM] * 2 + [ANY],
-        out_specs=[VMEM] * 4,
+        in_specs=[SMEM] + [VMEM] * 3,
+        out_specs=[VMEM] * (3 + PARTS),
         out_shape=[
             jax.ShapeDtypeStruct((tokens, vocab), F32),
             jax.ShapeDtypeStruct((tokens, vocab), F32),
             jax.ShapeDtypeStruct((tokens, 128), F32),
-            jax.ShapeDtypeStruct((half, vocab), BF16),
-        ],
-        scratch_shapes=[pltpu.SemaphoreType.DMA((len(blocks(vocab)),))],
-        compiler_params=params(16),
+        ]
+        + [jax.ShapeDtypeStruct((half // PARTS, vocab), BF16)] * PARTS,
+        scratch_shapes=[pltpu.SemaphoreType.DMA((PARTS,))],
+        compiler_params=params(8),
         cost_estimate=cost(2 * tokens * half * vocab, 2 * half * vocab),
         name="own_part",
-    )(mine, target, weight)
-
-
-def draft_kernel(theirs, acc, probs, stat, weight, draft, out, buffer, sems):
+    )(row, hidden, target, weight)
+
+
+def draft_kernel(acc, probs, stat, first, second, draft, out):
     tokens, vocab = draft.shape
-    copies = load(weight, buffer, sems)
     peak = jnp.full((tokens, 128), -jnp.inf, F32)
     cross = jnp.zeros((tokens, 128), F32)
-    for j, (c, e) in enumerate(blocks(vocab)):
-        copies[j].wait()
-        value = acc[:, c:e] + dot(theirs[...], buffer[:, c:e], 1, 0)
-        draft[:, c:e] = value
-        for tile, weighed in zip(tiles(value), tiles(probs[:, c:e] * value)):
-            peak = jnp.maximum(peak, tile)
-            cross = cross + weighed
+    split = first.shape[1]
+    for c in range(0, vocab, 128):
+        other = first[:, c : c + 128] if c < split else second[:, c - split : c - split + 128]
+        value = acc[:, c : c + 128] + other
+        draft[:, c : c + 128] = value
+        peak = jnp.maximum(peak, value)
+        cross = cross + probs[:, c : c + 128] * value
     top = jnp.max(peak, axis=1, keepdims=True)
     total = jnp.zeros((tokens, 128), F32)
     for tile in tiles(draft[...]):
@@ -128,27 +148,24 @@
             out[at : at + 1] = rows[i : i + 1, k * 128 : (k + 1) * 128]
 
 
-def draft_part(theirs, acc, probs, stat, weight):
-    tokens, half = theirs.shape
-    vocab = acc.shape[1]
-    steps = len(blocks(vocab))
+def draft_part(acc, probs, stat, first, second):
+    tokens, vocab = acc.shape
     return pl.pallas_call(
         draft_kernel,
-        in_specs=[VMEM] * 4 + [ANY],
-        out_specs=[VMEM] * 3,
+        in_specs=[VMEM] * 5,
+        out_specs=[VMEM] * 2,
         out_shape=[
             jax.ShapeDtypeStruct((tokens, vocab), F32),
             jax.ShapeDtypeStruct((stat_rows(tokens), 128), F32),
-            jax.ShapeDtypeStruct((half, vocab), BF16),
         ],
-        scratch_shapes=[pltpu.SemaphoreType.DMA((steps,))],
-        compiler_params=params(20),
-        cost_estimate=cost(2 * tokens * half * vocab, 2 * half * vocab),
+        compiler_params=params(8),
+        cost_estimate=cost(16 * tokens * vocab, 16 * tokens * vocab),
         name="draft_part",
-    )(theirs, acc, probs, stat, weight)
-
-
-def back_kernel(factor, row, parts, draft, target, weight, weight_o, divergence, out, *dlogits):
+    )(acc, probs, stat, first, second)
+
+
+def back_kernel(factor, row, parts, draft, target, *rest):
+    weights, (divergence, out, *dlogits) = rest[: 2 * PARTS], rest[2 * PARTS :]
     lines = draft.shape[0] // 128
     every = parts[...]
     top = jnp.max(every, axis=0)
@@ -163,31 +180,32 @@
     lse_t = jnp.concatenate([turned[:, k : k + 1] for k in range(lines)], axis=0)
     lse_q = jnp.concatenate([turned[:, 2 * lines + k : 2 * lines + k + 1] for k in range(lines)], axis=0)
 
-    half = weight.shape[0]
-    per = half // COLS_PIECE
+    wide = weights[0].shape[0]
+    fold = COLS_PIECE // wide
+    pieces = 2 * PARTS // fold
     down = draft.shape[0] // TOKENS_PIECE
-    sums = [None] * (2 * per)
+    sums = [None] * (2 * PARTS)
     for kept, (c, e) in zip(dlogits, thirds(draft.shape[1])):
         probs_q = exp(draft[:, c:e] - lse_q)
         probs_t = exp(target[:, c:e].astype(F32) - lse_t)
         block = ((probs_q - probs_t) * factor).astype(BF16)
         kept[...] = block
-        for j in range(2 * per):
-            rows = pl.ds(j % per * COLS_PIECE, COLS_PIECE)
-            term = dot(block, (weight, weight_o)[j // per][rows, c:e], 1, 1)
+        for j, weight in enumerate(weights):
+            term = dot(block, weight[:, c:e], 1, 1)
             sums[j] = term if sums[j] is None else sums[j] + term
-    for j in range(2 * per):
-        place = lax.rem(row[0] * per + j, 2 * per)
-        out[pl.ds(place * down, down)] = sums[j].astype(BF16).reshape(down, TOKENS_PIECE, COLS_PIECE)
-
-
-def back_part(factor, row, parts, draft, target, weight, weight_o):
+    for j, total in enumerate(sums):
+        place = lax.rem(row[0] * (pieces // 2) + j // fold, pieces) * down
+        columns = slice(j % fold * wide, (j % fold + 1) * wide)
+        out[pl.ds(place, down), :, columns] = total.astype(BF16).reshape(down, TOKENS_PIECE, wide)
+
+
+def back_part(factor, row, parts, draft, target, weights):
     tokens, vocab = draft.shape
-    half = weight.shape[0]
+    half = PARTS * weights[0].shape[0]
     pieces = (tokens // TOKENS_PIECE) * (2 * half // COLS_PIECE)
     return pl.pallas_call(
         functools.partial(back_kernel, factor),
-        in_specs=[pl.BlockSpec(memory_space=pltpu.SMEM)] + [VMEM] * 5,
+        in_specs=[SMEM] + [VMEM] * (3 + 2 * PARTS),
         out_specs=[VMEM] * 5,
         out_shape=[
             jax.ShapeDtypeStruct((1, tokens), F32),
@@ -197,7 +215,7 @@
         compiler_params=params(16),
         cost_estimate=cost(4 * tokens * half * vocab, 4 * half * vocab),
         name="back_part",
-    )(row, parts, draft, target, weight, weight_o)
+    )(row, parts, draft, target, *weights)
 
 
 def sum_kernel(terms, out):
@@ -292,25 +310,33 @@
 
 def shards(hidden, weight, target):
     n = lax.axis_size("vocab")
-    row = lax.axis_index("rows")
+    row = jnp.full((1,), lax.axis_index("rows"), jnp.int32)
     tokens, width = hidden.shape
     half, vocab = weight.shape
 
+    with jax.named_scope("swap_hidden"):
+        hidden_o = swap(hidden)
+    split = 2 * BLOCK
+    first = cross_part(row, hidden_o, weight, 0, split)
+    second = cross_part(row, hidden_o, weight, split, vocab)
+    with jax.named_scope("swap_draft"):
+        first, second = swap(first), swap(second)
+    acc, probs, stat, *weights = own_part(row, hidden, target, weight)
+    hidden, acc = lax.optimization_barrier((hidden, acc))
+    mine = lax.dynamic_slice_in_dim(hidden, row[0] * half, half, 1)
+    theirs = lax.dynamic_slice_in_dim(hidden, (1 - row[0]) * half, half, 1)
+    first, second, acc, *weights = lax.optimization_barrier((first, second, acc, *weights))
     with jax.named_scope("swap_weight"):
-        weight_o = swap(weight)
-    mine = lax.dynamic_slice_in_dim(hidden, row * half, half, 1)
-    theirs = lax.dynamic_slice_in_dim(hidden, (1 - row) * half, half, 1)
-
-    acc, probs, stat, weight_v = own_part(mine, target, weight)
-    draft, part, weight_o = draft_part(theirs, acc, probs, stat, weight_o)
+        weights_o = [swap(x) for x in weights]
+    draft, part = draft_part(acc, probs, stat, first, second)
     with jax.named_scope("share_stats"):
         parts = lax.all_to_all(jnp.broadcast_to(part[None], (n,) + part.shape), "vocab", 0, 0)
     divergence, pieces, *dlogits = back_part(
-        vocab * n / 1024.0, jnp.full((1,), row, jnp.int32), parts, draft, target, weight_v, weight_o
+        vocab * n / 1024.0, row, parts, draft, target, [*weights, *weights_o]
     )
     with jax.named_scope("scatter_sum"):
         terms = lax.all_to_all(pieces, "vocab", 0, 0)
-    with jax.named_scope("swap_back"):
+    with jax.named_scope("swap_dlogits"):
         mine_o, dlogits_o = swap(theirs), [swap(x) for x in dlogits]
     head_grad = head_part(mine, mine_o, dlogits, dlogits_o)
     terms, head_grad = lax.optimization_barrier((terms, head_grad))

time: 87.5 us -> 89.2 us (1.019)
  waiting for transfers between devices: 11.5 us -> 14.2 us
  starting transfers between devices: 6.04 us -> 7.81 us
  Pallas kernels: 19.7 us -> 18.4 us
  local copies, waits for them, and re-layouts: 5 us -> 3.87 us
    ppermute x5 -> x11, waiting for transfers between devices: 2.78 us -> 5.54 us  [swap(): return lax.ppermute(x, 'rows', SWAP)]
    ppermute x5 -> x11, starting transfers between devices: 1.18 us -> 2.95 us  [swap(): return lax.ppermute(x, 'rows', SWAP)]
    pallas_call x3 -> x5, Pallas kernels: 12.4 us -> 11 us  [the longest x1 4.63 us: back_part(): pl.pallas_call(functools.partial(back_kernel, factor), in_specs=[SMEM] +...]
    dynamic_slice x1, local copies, waits for them, and re-layouts: 1.27 us -> 0.08 us  [shards(): theirs = lax.dynamic_slice_in_dim(hidden, (1 - row[0]) * half, half, 1)]
    unnamed x6 -> x8, local copies, waits for them, and re-layouts: 3.7 us -> 3.75 us
  transfers between devices with their start and end apart: 6 -> 12, of which waited for: 4 -> 4; matrix products, arithmetic and copies ran while one was open for 1% -> 0% of each run, Pallas kernels for 11% -> 13%
where the time goes in v10:
time: 89.2 us; the launch traced here: 88.9 us
  blocking collectives  43.8 us (49%)
  Pallas kernels  18.4 us (21%)
  waiting for transfers between devices  14.2 us (16%)
  starting transfers between devices  7.81 us (9%)
  local copies, waits for them, and re-layouts  3.87 us (4%)
  between operations  0.93 us (1%)
    all_to_all x1, blocking collectives, shards(): lax.all_to_all(jnp.broadcast_to(part[None], (n,) + part.shape), 'vocab',...  22.3 us
    all_to_all x1, blocking collectives, shards(): gathered = lax.all_to_all(totals, 'vocab', 0, 0)  21.5 us
    all_to_all x1, waiting for transfers between devices, shards(): terms = lax.all_to_all(pieces, 'vocab', 0, 0)  8.62 us
    pallas_call x1, Pallas kernels, head_part(): pl.pallas_call(head_kernel, in_specs=[VMEM] * 4 + [ANY] * 4, out_specs=AN...  5.69 us
    ppermute x11, waiting for transfers between devices, swap(): return lax.ppermute(x, 'rows', SWAP)  5.54 us
    all_to_all x1, starting transfers between devices, shards(): terms = lax.all_to_all(pieces, 'vocab', 0, 0)  4.86 us
    pallas_call x1, Pallas kernels, back_part(): pl.pallas_call(functools.partial(back_kernel, factor), in_specs=[SMEM] +...  4.63 us
    unnamed x8, local copies, waits for them, and re-layouts  3.75 us
  transfers between devices with their start and end apart: 12, of which 4 were waited for; matrix products, arithmetic and copies ran while one was open for 0% of the time, Pallas kernels for 13%

profile of v10, /device:TPU:0, one launch (start us, length us, event | category | flops | bytes accessed | tf_op | source)
XLA Modules:
  0.0 88.9 jit_solution(14496366238967306857)
XLA Ops:
  0.6 0.1 collective-permute-start
  0.7 2.9 %collective-permute-done.hidden_o = bf16[256,2048]{1,0:T(8,128)(2,1)S(1)} collective-permute-done((bf16[256,2048]{1,0:T(8,128)(2,1)}, bf16[256,2048]{1,0:T(8,128)(2,1)S(1)}, u32[]{:S(2)}, u32[]{:S(2)}) %collective-permute-start) | collective-permute-done | bytes 1048608 | tf_op jit(solution)/shard_map/swap_hidden/ppermute | solution.py:27
  3.6 0.0 copy-start
  3.6 2.4 %copy-done = bf16[1024,2432]{1,0:T(8,128)(2,1)S(1)} copy-done((bf16[1024,2432]{1,0:T(8,128)(2,1)S(1)}, bf16[1024,2432]{1,0:T(8,128)(2,1)}, u32[]{:S(2)}) %copy-start) | copy-done | bytes 4980760
  6.0 0.0 copy-start.3
  6.0 0.9 cross_part.2
  6.9 0.0 copy-start.2
  6.9 0.2 collective-permute-start.1
  7.1 0.0 copy-start.1
  7.1 0.9 cross_part.3
  7.9 0.5 collective-permute-start.2
  8.4 0.0 copy-done.3
  8.4 0.0 copy-done.2
  8.4 1.3 %copy-done.1 = bf16[1024,2432]{1,0:T(8,128)(2,1)S(1)} copy-done((bf16[1024,2432]{1,0:T(8,128)(2,1)S(1)}, bf16[1024,2432]{1,0:T(8,128)(2,1)}, u32[]{:S(2)}) %copy-start.1) | copy-done | bytes 4980760
  9.7 3.6 %own_part.1 = (f32[256,2432]{1,0:T(8,128)S(1)}, f32[256,2432]{1,0:T(8,128)S(1)}, f32[256,128]{1,0:T(8,128)S(1)}, bf16[256,2432]{1,0:T(8,128)(2,1)S(1)}, bf16[256...) custom-call(s32[1]{0:T(128)} %bitcast.row, bf16[256,2048]{1,0:T(8,128)(2,1)S(1)} %copy-done.3, ...), custom_call_target="tpu_custom_call" | custom-call | flops 1275068416 | bytes 4980736 | tf_op jit(solution)/shard_map/own_part/pallas_call | solution.py:108
  13.4 0.0 collective-permute-done.2.second
  13.4 0.0 collective-permute-done.1.first
  13.4 0.3 collective-permute-start.3
  13.7 0.3 collective-permute-start.4
  14.0 0.2 collective-permute-start.5
  14.2 0.3 collective-permute-start.6
  14.5 1.1 %draft_part.1 = (f32[256,2432]{1,0:T(8,128)S(1)}, f32[8,128]{1,0:T(8,128)S(1)}) custom-call(f32[256,2432]{1,0:T(8,128)S(1)} %get-tuple-element.34.acc, f32[256,2432]{1,0:T(8,128)S(1)} %get-tuple-element.35.probs, f32[256,128]{1,0:T(8,128)S(1)} %get-tuple-element.36.stat, f32[256,1280]{1,0:T(8,128)S(1)} %collective-permute-done.1.first, ...), custom_call_target="tpu_custom_call" | custom-call | flops 9961472 | bytes 9961472 | tf_op jit(solution)/shard_map/draft_part/pallas_call | solution.py:153
  15.6 22.3 %all_to_all.15.parts = f32[64,8,128]{2,1,0:T(8,128)S(1)} all-to-all(f32[64,8,128]{2,1,0:T(8,128)S(1)} %broadcast_in_dim.10), channel_id=1, replica_groups=mesh['rows'=2,'vocab'=64] {'vocab'}, dimensions={0} | all-to-all | bytes 524288 | tf_op jit(solution)/shard_map/share_stats/all_to_all | solution.py:333
  37.9 0.0 collective-permute-done.3.rest_4_
  37.9 0.0 collective-permute-done.4.rest_5_
  37.9 0.0 collective-permute-done.5.rest_6_
  37.9 0.0 collective-permute-done.6.rest_7_
  37.9 4.6 %back_part.1 = (f32[1,256]{1,0:T(1,128)}, bf16[64,16,512]{2,1,0:T(8,128)(2,1)}, bf16[256,896]{1,0:T(8,128)(2,1)S(1)}, bf16[256,896]{1,0:T(8,128)(2,1)S(1)}, bf16[256,640]{1,0:T(8,128)(2,1)S(1)}) custom-call(s32[1]{0:T(128)} %bitcast.row, f32[64,8,128]{2,1,0:T(8,128)S(1)} %all_to_all.15.parts, f32[256,2432]{1,0:T(8,128)S(1)} %get-tuple-element.40.draft, ...), custom_call_target="tpu_custom_call" | custom-call | flops 2550136832 | bytes 9961472 | tf_op jit(solution)/shard_map/back_part/pallas_call | solution.py:206
  42.6 4.9 %all-to-all-start.1 = ((bf16[64,16,512]{2,1,0:T(8,128)(2,1)}), bf16[64,16,512]{2,1,0:T(8,128)(2,1)S(1)}, u32[]{:S(2)}, u32[]{:S(2)}) async-start(bf16[64,16,512]{2,1,0:T(8,128)(2,1)} %get-tuple-element.46), calls=%async_computation.1 | async-start | bytes 2097152 | tf_op jit(solution)/shard_map/scatter_sum/all_to_all | solution.py:338
  47.4 0.1 constant_dynamic-slice_fusion
  47.5 0.1 collective-permute-start.7
  47.6 0.5 collective-permute-start.8
  48.1 0.1 collective-permute-start.9
  48.2 0.4 collective-permute-start.10
  48.6 0.9 collective-permute-done.7.rest_3_
  49.5 1.8 %collective-permute-done.10.rest_6_ = bf16[256,640]{1,0:T(8,128)(2,1)S(1)} collective-permute-done((bf16[256,640]{1,0:T(8,128)(2,1)S(1)}, bf16[256,640]{1,0:T(8,128)(2,1)S(1)}, u32[]{:S(2)}, u32[]{:S(2)}) %collective-permute-start.10) | collective-permute-done | bytes 327712 | tf_op jit(solution)/shard_map/swap_dlogits/ppermute | solution.py:27
  51.3 0.0 collective-permute-done.8.rest_4_
  51.3 0.0 collective-permute-done.9.rest_5_
  51.3 5.7 %head_part.1 = f32[1024,2432]{1,0:T(8,128)} custom-call(bf16[256,1024]{1,0:T(8,128)(2,1)S(1)} %get-tuple-element.54.mine, bf16[256,896]{1,0:T(8,128)(2,1)S(1)} %get-tuple-element.48.rest_0_, bf16[256,896]{1,0:T(8,128)(2,1)S(1)} %get-tuple-element.49.rest_1_, bf16[256,640]{1,0:T(8,128)(2,1)S(1)} %get-tuple-element.50.rest_2_, ...), custom_call_target="tpu_custom_call" | custom-call | flops 2550136832 | bytes 9961472 | tf_op jit(solution)/shard_map/head_part/pallas_call | solution.py:294
  57.0 8.6 %all-to-all-done.1.terms = bf16[64,16,512]{2,1,0:T(8,128)(2,1)S(1)} async-done(((bf16[64,16,512]{2,1,0:T(8,128)(2,1)}), bf16[64,16,512]{2,1,0:T(8,128)(2,1)S(1)}, u32[]{:S(2)}, u32[]{:S(2)}) %all-to-all-start.1) | async-done | bytes 1048608 | tf_op jit(solution)/shard_map/scatter_sum/all_to_all | solution.py:338
  65.6 0.2 sum_part.1
  65.9 21.5 %all_to_all.16.pieces = bf16[64,16,512]{2,1,0:T(8,128)(2,1)S(1)} all-to-all(bf16[64,16,512]{2,1,0:T(8,128)(2,1)S(1)} %sum_part.1), channel_id=1, replica_groups=mesh['rows'=2,'vocab'=64] {'vocab'}, dimensions={0} | all-to-all | bytes 2097152 | tf_op jit(solution)/shard_map/gather/all_to_all | solution.py:345
  87.4 1.4 %join_part.1 = f32[256,2048]{1,0:T(8,128)} custom-call(bf16[64,16,512]{2,1,0:T(8,128)(2,1)S(1)} %all_to_all.16.pieces), custom_call_target="tpu_custom_call" | custom-call | tf_op jit(solution)/shard_map/join_part/pallas_call | solution.py:257
  (1 shorter events, 0.0 us)
Async XLA Ops:
  0.6 3.0 %collective-permute-start = (bf16[256,2048]{1,0:T(8,128)(2,1)}, bf16[256,2048]{1,0:T(8,128)(2,1)S(1)}, u32[]{:S(2)}, u32[]{:S(2)}) collective-permute-start(bf16[256,2048]{1,0:T(8,128)(2,1)} %hidden.1), channel_id=1, source_target_pairs={{0,64},{64,0},{1,65},{65,1},{2,66},{66,2},{3,67},{67,3},{4,68},{68... | collective-permute-start | bytes 3145736 | tf_op jit(solution)/shard_map/swap_hidden/ppermute | solution.py:27
  3.6 2.4 %copy-start = (bf16[1024,2432]{1,0:T(8,128)(2,1)S(1)}, bf16[1024,2432]{1,0:T(8,128)(2,1)}, u32[]{:S(2)}) copy-start(bf16[1024,2432]{1,0:T(8,128)(2,1)} %weight.5) | copy-start | bytes 14942212
  6.0 2.4 %copy-start.3 = (bf16[256,2048]{1,0:T(8,128)(2,1)S(1)}, bf16[256,2048]{1,0:T(8,128)(2,1)}, u32[]{:S(2)}) copy-start(bf16[256,2048]{1,0:T(8,128)(2,1)} %hidden.1) | copy-start | bytes 3145732
  6.9 1.5 %copy-start.2 = (bf16[256,2432]{1,0:T(8,128)(2,1)S(1)}, bf16[256,2432]{1,0:T(8,128)(2,1)}, u32[]{:S(2)}) copy-start(bf16[256,2432]{1,0:T(8,128)(2,1)} %target.3) | copy-start | bytes 3735556
  6.9 6.5 %collective-permute-start.1 = (f32[256,1280]{1,0:T(8,128)S(1)}, f32[256,1280]{1,0:T(8,128)S(1)}, u32[]{:S(2)}, u32[]{:S(2)}) collective-permute-start(f32[256,1280]{1,0:T(8,128)S(1)} %cross_part.2), channel_id=1, source_target_pairs={{0,64},{64,0},{1,65},{65,1},{2,66},{66,2},{3,67},{67,3},{4,68},{68... | collective-permute-start | bytes 3932168 | tf_op jit(solution)/shard_map/swap_draft/ppermute | solution.py:27
  7.1 2.6 %copy-start.1 = (bf16[1024,2432]{1,0:T(8,128)(2,1)S(1)}, bf16[1024,2432]{1,0:T(8,128)(2,1)}, u32[]{:S(2)}) copy-start(bf16[1024,2432]{1,0:T(8,128)(2,1)} %weight.5) | copy-start | bytes 14942212
  7.9 5.4 %collective-permute-start.2 = (f32[256,1152]{1,0:T(8,128)S(1)}, f32[256,1152]{1,0:T(8,128)S(1)}, u32[]{:S(2)}, u32[]{:S(2)}) collective-permute-start(f32[256,1152]{1,0:T(8,128)S(1)} %cross_part.3), channel_id=1, source_target_pairs={{0,64},{64,0},{1,65},{65,1},{2,66},{66,2},{3,67},{67,3},{4,68},{68... | collective-permute-start | bytes 3538952 | tf_op jit(solution)/shard_map/swap_draft/ppermute | solution.py:27
  13.4 24.5 %collective-permute-start.3 = (bf16[256,2432]{1,0:T(8,128)(2,1)S(1)}, bf16[256,2432]{1,0:T(8,128)(2,1)S(1)}, u32[]{:S(2)}, u32[]{:S(2)}) collective-permute-start(bf16[256,2432]{1,0:T(8,128)(2,1)S(1)} %get-tuple-element.41.rest_0_), channel_id=1, source_target_pairs={{0,64},{64,0},{1,65},{65,1},{2,66},{66,2},{3,67},{67,3},{4,68},{68... | collective-permute-start | bytes 3735560 | tf_op jit(solution)/shard_map/swap_weight/ppermute | solution.py:27
  13.7 24.2 %collective-permute-start.4 = (bf16[256,2432]{1,0:T(8,128)(2,1)S(1)}, bf16[256,2432]{1,0:T(8,128)(2,1)S(1)}, u32[]{:S(2)}, u32[]{:S(2)}) collective-permute-start(bf16[256,2432]{1,0:T(8,128)(2,1)S(1)} %get-tuple-element.42.rest_1_), channel_id=1, source_target_pairs={{0,64},{64,0},{1,65},{65,1},{2,66},{66,2},{3,67},{67,3},{4,68},{68... | collective-permute-start | bytes 3735560 | tf_op jit(solution)/shard_map/swap_weight/ppermute | solution.py:27
  14.0 23.9 %collective-permute-start.5 = (bf16[256,2432]{1,0:T(8,128)(2,1)S(1)}, bf16[256,2432]{1,0:T(8,128)(2,1)S(1)}, u32[]{:S(2)}, u32[]{:S(2)}) collective-permute-start(bf16[256,2432]{1,0:T(8,128)(2,1)S(1)} %get-tuple-element.43.rest_2_), channel_id=1, source_target_pairs={{0,64},{64,0},{1,65},{65,1},{2,66},{66,2},{3,67},{67,3},{4,68},{68... | collective-permute-start | bytes 3735560 | tf_op jit(solution)/shard_map/swap_weight/ppermute | solution.py:27
  14.2 23.7 %collective-permute-start.6 = (bf16[256,2432]{1,0:T(8,128)(2,1)S(1)}, bf16[256,2432]{1,0:T(8,128)(2,1)S(1)}, u32[]{:S(2)}, u32[]{:S(2)}) collective-permute-start(bf16[256,2432]{1,0:T(8,128)(2,1)S(1)} %get-tuple-element.44.rest_3_), channel_id=1, source_target_pairs={{0,64},{64,0},{1,65},{65,1},{2,66},{66,2},{3,67},{67,3},{4,68},{68... | collective-permute-start | bytes 3735560 | tf_op jit(solution)/shard_map/swap_weight/ppermute | solution.py:27
  42.6 23.1 %all-to-all-start.1 = ((bf16[64,16,512]{2,1,0:T(8,128)(2,1)}), bf16[64,16,512]{2,1,0:T(8,128)(2,1)S(1)}, u32[]{:S(2)}, u32[]{:S(2)}) async-start(bf16[64,16,512]{2,1,0:T(8,128)(2,1)} %get-tuple-element.46), calls=%async_computation.1 | async-start | bytes 2097152 | tf_op jit(solution)/shard_map/scatter_sum/all_to_all | solution.py:338
  47.5 2.0 %collective-permute-start.7 = (bf16[256,1024]{1,0:T(8,128)(2,1)S(1)}, bf16[256,1024]{1,0:T(8,128)(2,1)S(1)}, u32[]{:S(2)}, u32[]{:S(2)}) collective-permute-start(bf16[256,1024]{1,0:T(8,128)(2,1)S(1)} %get-tuple-element.53), channel_id=1, source_target_pairs={{0,64},{64,0},{1,65},{65,1},{2,66},{66,2},{3,67},{67,3},{4,68},{68... | collective-permute-start | bytes 1572872 | tf_op jit(solution)/shard_map/swap_dlogits/ppermute | solution.py:27
  47.6 3.7 %collective-permute-start.8 = (bf16[256,896]{1,0:T(8,128)(2,1)S(1)}, bf16[256,896]{1,0:T(8,128)(2,1)S(1)}, u32[]{:S(2)}, u32[]{:S(2)}) collective-permute-start(bf16[256,896]{1,0:T(8,128)(2,1)S(1)} %get-tuple-element.48.rest_0_), channel_id=1, source_target_pairs={{0,64},{64,0},{1,65},{65,1},{2,66},{66,2},{3,67},{67,3},{4,68},{68... | collective-permute-start | bytes 1376264 | tf_op jit(solution)/shard_map/swap_dlogits/ppermute | solution.py:27
  48.1 3.2 %collective-permute-start.9 = (bf16[256,896]{1,0:T(8,128)(2,1)S(1)}, bf16[256,896]{1,0:T(8,128)(2,1)S(1)}, u32[]{:S(2)}, u32[]{:S(2)}) collective-permute-start(bf16[256,896]{1,0:T(8,128)(2,1)S(1)} %get-tuple-element.49.rest_1_), channel_id=1, source_target_pairs={{0,64},{64,0},{1,65},{65,1},{2,66},{66,2},{3,67},{67,3},{4,68},{68... | collective-permute-start | bytes 1376264 | tf_op jit(solution)/shard_map/swap_dlogits/ppermute | solution.py:27
  48.2 3.1 %collective-permute-start.10 = (bf16[256,640]{1,0:T(8,128)(2,1)S(1)}, bf16[256,640]{1,0:T(8,128)(2,1)S(1)}, u32[]{:S(2)}, u32[]{:S(2)}) collective-permute-start(bf16[256,640]{1,0:T(8,128)(2,1)S(1)} %get-tuple-element.50.rest_2_), channel_id=1, source_target_pairs={{0,64},{64,0},{1,65},{65,1},{2,66},{66,2},{3,67},{67,3},{4,68},{68... | collective-permute-start | bytes 983048 | tf_op jit(solution)/shard_map/swap_dlogits/ppermute | solution.py:27

commit v11 on v9

--- a/solution.py
+++ b/solution.py
@@ -10,7 +10,7 @@
 SWAP = ((0, 1), (1, 0))
 TOKENS_PIECE = 16
 COLS_PIECE = 512
-BLOCK = 640
+GROUP = 64
 LOG2E = math.log2(math.e)
 F32, BF16 = jnp.float32, jnp.bfloat16
 VMEM = pl.BlockSpec(memory_space=pltpu.VMEM)
@@ -38,35 +38,18 @@
     return jnp.exp2(x * LOG2E)
 
 
-def blocks(n):
-    return [(c, min(c + BLOCK, n)) for c in range(0, n, BLOCK)]
-
-
 def thirds(n):
     step = pl.cdiv(n // 128, 3) * 128
     return [(c, min(c + step, n)) for c in range(0, n, step)]
 
 
-def tiles(x):
-    return [x[:, c : c + 128] for c in range(0, x.shape[1], 128)]
-
-
 def stat_rows(tokens):
     return pl.cdiv(3 * tokens // 128, 8) * 8
 
 
-def load(source, target, sems):
-    copies = []
-    for j, (c, e) in enumerate(blocks(source.shape[1])):
-        part = pl.ds(c, e - c)
-        copies.append(pltpu.make_async_copy(source.at[:, part], target.at[:, part], sems.at[j]))
-        copies[-1].start()
-    return copies
-
-
-def own_kernel(mine, target, weight, acc, probs, stat, buffer, sems):
-    vocab = target.shape[1]
-    copies = load(weight, buffer, sems)
+def own_kernel(mine, target, weight, acc, probs, stat, buffer, sem):
+    copy = pltpu.make_async_copy(weight, buffer, sem)
+    copy.start()
     wide = target[...].astype(F32)
     peak = jnp.max(wide, axis=1, keepdims=True)
     terms = exp(wide - peak)
@@ -76,9 +59,8 @@
     mean = jnp.sum(terms * wide, axis=1, keepdims=True)
     lane = lax.broadcasted_iota(jnp.int32, stat.shape, 1)
     stat[...] = jnp.where(lane == 0, peak + jnp.log(total), mean)
-    for copy, (c, e) in zip(copies, blocks(vocab)):
-        copy.wait()
-        acc[:, c:e] = dot(mine[...], buffer[:, c:e], 1, 0)
+    copy.wait()
+    acc[...] = dot(mine[...], buffer[...], 1, 0)
 
 
 def own_part(mine, target, weight):
@@ -94,31 +76,35 @@
             jax.ShapeDtypeStruct((tokens, 128), F32),
             jax.ShapeDtypeStruct((half, vocab), BF16),
         ],
-        scratch_shapes=[pltpu.SemaphoreType.DMA((len(blocks(vocab)),))],
+        scratch_shapes=[pltpu.SemaphoreType.DMA],
         compiler_params=params(16),
         cost_estimate=cost(2 * tokens * half * vocab, 2 * half * vocab),
         name="own_part",
     )(mine, target, weight)
 
 
-def draft_kernel(theirs, acc, probs, stat, weight, draft, out, buffer, sems):
+def draft_kernel(theirs, acc, probs, stat, weight, draft, out, buffer, sem):
     tokens, vocab = draft.shape
-    copies = load(weight, buffer, sems)
-    peak = jnp.full((tokens, 128), -jnp.inf, F32)
-    cross = jnp.zeros((tokens, 128), F32)
-    for j, (c, e) in enumerate(blocks(vocab)):
-        copies[j].wait()
-        value = acc[:, c:e] + dot(theirs[...], buffer[:, c:e], 1, 0)
-        draft[:, c:e] = value
-        for tile, weighed in zip(tiles(value), tiles(probs[:, c:e] * value)):
-            peak = jnp.maximum(peak, tile)
-            cross = cross + weighed
-    top = jnp.max(peak, axis=1, keepdims=True)
-    total = jnp.zeros((tokens, 128), F32)
-    for tile in tiles(draft[...]):
-        total = total + exp(tile - top)
-    lse_q = top + jnp.log(jnp.sum(total, axis=1, keepdims=True))
-    mean = stat[:, 1:2] - jnp.sum(cross, axis=1, keepdims=True)
+    copy = pltpu.make_async_copy(weight, buffer, sem)
+    copy.start()
+    copy.wait()
+    draft[...] = acc[...] + dot(theirs[...], buffer[...], 1, 0)
+    lse_q, mean = [], []
+    for first in range(0, tokens, GROUP):
+        rows = slice(first, first + GROUP)
+        peak = jnp.full((GROUP, 128), -jnp.inf, F32)
+        cross = jnp.zeros((GROUP, 128), F32)
+        for t in range(0, vocab, 128):
+            value = draft[rows, t : t + 128]
+            peak = jnp.maximum(peak, value)
+            cross = cross + probs[rows, t : t + 128] * value
+        top = jnp.max(peak, axis=1, keepdims=True)
+        total = jnp.zeros((GROUP, 128), F32)
+        for t in range(0, vocab, 128):
+            total = total + exp(draft[rows, t : t + 128] - top)
+        lse_q.append(top + jnp.log(jnp.sum(total, axis=1, keepdims=True)))
+        mean.append(stat[rows, 1:2] - jnp.sum(cross, axis=1, keepdims=True))
+    lse_q, mean = jnp.concatenate(lse_q, axis=0), jnp.concatenate(mean, axis=0)
     lane = lax.broadcasted_iota(jnp.int32, stat.shape, 1)
     rows = jnp.where(lane == 0, stat[:, :1], jnp.where(lane == 1, mean, lse_q)).T
     out[...] = jnp.zeros(out.shape, F32)
@@ -131,7 +117,6 @@
 def draft_part(theirs, acc, probs, stat, weight):
     tokens, half = theirs.shape
     vocab = acc.shape[1]
-    steps = len(blocks(vocab))
     return pl.pallas_call(
         draft_kernel,
         in_specs=[VMEM] * 4 + [ANY],
@@ -141,7 +126,7 @@
             jax.ShapeDtypeStruct((stat_rows(tokens), 128), F32),
             jax.ShapeDtypeStruct((half, vocab), BF16),
         ],
-        scratch_shapes=[pltpu.SemaphoreType.DMA((steps,))],
+        scratch_shapes=[pltpu.SemaphoreType.DMA],
         compiler_params=params(20),
         cost_estimate=cost(2 * tokens * half * vocab, 2 * half * vocab),
         name="draft_part",

time: 87.5 us -> 87.3 us (level)
  transfers between devices with their start and end apart: 6 -> 6, of which waited for: 4 -> 4; matrix products, arithmetic and copies ran while one was open for 1% -> 1% of each run, Pallas kernels for 11% -> 10%
where the time goes in v11:
time: 87.3 us; the launch traced here: 87 us
  blocking collectives  43.4 us (50%)
  Pallas kernels  19.5 us (22%)
  waiting for transfers between devices  12.1 us (14%)
  starting transfers between devices  6.04 us (7%)
  local copies, waits for them, and re-layouts  5 us (6%)
  between operations  0.88 us (1%)
    all_to_all x1, blocking collectives, shards(): lax.all_to_all(jnp.broadcast_to(part[None], (n,) + part.shape), 'vocab',...  22.2 us
    all_to_all x1, blocking collectives, shards(): gathered = lax.all_to_all(totals, 'vocab', 0, 0)  21.2 us
    all_to_all x1, waiting for transfers between devices, shards(): terms = lax.all_to_all(pieces, 'vocab', 0, 0)  8.61 us
    pallas_call x1, Pallas kernels, head_part(): pl.pallas_call(head_kernel, in_specs=[VMEM] * 4 + [ANY] * 4, out_specs=AN...  5.69 us
    pallas_call x1, Pallas kernels, draft_part(): pl.pallas_call(draft_kernel, in_specs=[VMEM] * 4 + [ANY], out_specs=[VMEM...  4.87 us
    all_to_all x1, starting transfers between devices, shards(): terms = lax.all_to_all(pieces, 'vocab', 0, 0)  4.86 us
    pallas_call x1, Pallas kernels, back_part(): pl.pallas_call(functools.partial(back_kernel, factor), in_specs=[pl.Block...  4.62 us
    unnamed x6, local copies, waits for them, and re-layouts  3.7 us
  transfers between devices with their start and end apart: 6, of which 4 were waited for; matrix products, arithmetic and copies ran while one was open for 1% of the time, Pallas kernels for 10%

profile of v11, /device:TPU:0, one launch (start us, length us, event | category | flops | bytes accessed | tf_op | source)
XLA Modules:
  0.0 87.0 jit_solution(6226658173722595533)
XLA Ops:
  0.6 0.1 collective-permute-start
  0.7 1.3 %constant_dynamic-slice_fusion = (bf16[256,1024]{1,0:T(8,128)(2,1)S(1)}, bf16[256,1024]{1,0:T(8,128)(2,1)S(1)}) fusion(bf16[256,2048]{1,0:T(8,128)(2,1)} %param.3, s32[]{:T(128)S(6)} %select_n.7, s32[]{:T(128)S(6)} %select_n.6), kind=kLoop, calls=%fused_computation | loop fusion | bytes 2097160 | tf_op jit(solution)/shard_map/dynamic_slice | solution.py:286
  2.0 0.0 copy-start
  2.0 2.4 %copy-done = bf16[1024,2432]{1,0:T(8,128)(2,1)S(1)} copy-done((bf16[1024,2432]{1,0:T(8,128)(2,1)S(1)}, bf16[1024,2432]{1,0:T(8,128)(2,1)}, u32[]{:S(2)}) %copy-start) | copy-done | bytes 4980760
  4.4 0.0 copy-start.1
  4.4 1.3 %copy-done.1 = bf16[256,2432]{1,0:T(8,128)(2,1)S(1)} copy-done((bf16[256,2432]{1,0:T(8,128)(2,1)S(1)}, bf16[256,2432]{1,0:T(8,128)(2,1)}, u32[]{:S(2)}) %copy-start.1) | copy-done | bytes 1245208
  5.7 2.7 %own_part.1 = (f32[256,2432]{1,0:T(8,128)S(1)}, f32[256,2432]{1,0:T(8,128)S(1)}, f32[256,128]{1,0:T(8,128)S(1)}, bf16[1024,2432]{1,0:T(8,128)(2,1)S(1)}) custom-call(bf16[256,1024]{1,0:T(8,128)(2,1)S(1)} %get-tuple-element.31.mine, bf16[256,2432]{1,0:T(8,128)(2,1)S(1)} %copy-done.1, bf16[1024,2432]{1,0:T(8,128)(2,1)S(1)} %copy-done), custom_call_target="tpu_custom_call" | custom-call | flops 1275068416 | bytes 4980736 | tf_op jit(solution)/shard_map/own_part/pallas_call | solution.py:69
  8.5 0.9 collective-permute-done.weight
  9.3 0.0 copy-start.2
  9.3 4.9 %draft_part.1 = (f32[256,2432]{1,0:T(8,128)S(1)}, f32[8,128]{1,0:T(8,128)S(1)}, bf16[1024,2432]{1,0:T(8,128)(2,1)S(1)}) custom-call(bf16[256,1024]{1,0:T(8,128)(2,1)S(1)} %get-tuple-element.32.theirs, f32[256,2432]{1,0:T(8,128)S(1)} %get-tuple-element.17.acc, f32[256,2432]{1,0:T(8,128)S(1)} %get-tuple-element.18.probs, ...), custom_call_target="tpu_custom_call" | custom-call | flops 1275068416 | bytes 4980736 | tf_op jit(solution)/shard_map/draft_part/pallas_call | solution.py:120
  14.2 22.2 %all_to_all.15.parts = f32[64,8,128]{2,1,0:T(8,128)S(1)} all-to-all(f32[64,8,128]{2,1,0:T(8,128)S(1)} %broadcast_in_dim.10), channel_id=1, replica_groups=mesh['rows'=2,'vocab'=64] {'vocab'}, dimensions={0} | all-to-all | bytes 524288 | tf_op jit(solution)/shard_map/share_stats/all_to_all | solution.py:292
  36.4 0.0 copy-done.2
  36.4 4.6 %back_part.1 = (f32[1,256]{1,0:T(1,128)}, bf16[64,16,512]{2,1,0:T(8,128)(2,1)}, bf16[256,896]{1,0:T(8,128)(2,1)S(1)}, bf16[256,896]{1,0:T(8,128)(2,1)S(1)}, bf16[256,640]{1,0:T(8,128)(2,1)S(1)}) custom-call(s32[1]{0:T(128)} %bitcast.row, f32[64,8,128]{2,1,0:T(8,128)S(1)} %all_to_all.15.parts, f32[256,2432]{1,0:T(8,128)S(1)} %get-tuple-element.21.draft, ...), custom_call_target="tpu_custom_call" | custom-call | flops 2550136832 | bytes 9961472 | tf_op jit(solution)/shard_map/back_part/pallas_call | solution.py:173
  41.1 4.9 %all-to-all-start.1 = ((bf16[64,16,512]{2,1,0:T(8,128)(2,1)}), bf16[64,16,512]{2,1,0:T(8,128)(2,1)S(1)}, u32[]{:S(2)}, u32[]{:S(2)}) async-start(bf16[64,16,512]{2,1,0:T(8,128)(2,1)} %get-tuple-element.25), calls=%async_computation.1 | async-start | bytes 2097152 | tf_op jit(solution)/shard_map/scatter_sum/all_to_all | solution.py:297
  45.9 0.1 collective-permute-start.1
  46.0 0.5 collective-permute-start.2
  46.5 0.1 collective-permute-start.3
  46.6 0.4 collective-permute-start.4
  47.0 0.9 %collective-permute-done.1.rest_3_ = bf16[256,1024]{1,0:T(8,128)(2,1)S(1)} collective-permute-done((bf16[256,1024]{1,0:T(8,128)(2,1)S(1)}, bf16[256,1024]{1,0:T(8,128)(2,1)S(1)}, u32[]{:S(2)}, u32[]{:S(2)}) %collective-permute-start.1) | collective-permute-done | bytes 524320 | tf_op jit(solution)/shard_map/swap_back/ppermute | solution.py:26
  47.9 1.8 %collective-permute-done.4.rest_6_ = bf16[256,640]{1,0:T(8,128)(2,1)S(1)} collective-permute-done((bf16[256,640]{1,0:T(8,128)(2,1)S(1)}, bf16[256,640]{1,0:T(8,128)(2,1)S(1)}, u32[]{:S(2)}, u32[]{:S(2)}) %collective-permute-start.4) | collective-permute-done | bytes 327712 | tf_op jit(solution)/shard_map/swap_back/ppermute | solution.py:26
  49.7 0.0 collective-permute-done.2.rest_4_
  49.7 0.0 collective-permute-done.3.rest_5_
  49.7 5.7 %head_part.1 = f32[1024,2432]{1,0:T(8,128)} custom-call(bf16[256,1024]{1,0:T(8,128)(2,1)S(1)} %get-tuple-element.31.mine, bf16[256,896]{1,0:T(8,128)(2,1)S(1)} %get-tuple-element.26.rest_0_, bf16[256,896]{1,0:T(8,128)(2,1)S(1)} %get-tuple-element.27.rest_1_, bf16[256,640]{1,0:T(8,128)(2,1)S(1)} %get-tuple-element.28.rest_2_, ...), custom_call_target="tpu_custom_call" | custom-call | flops 2550136832 | bytes 9961472 | tf_op jit(solution)/shard_map/head_part/pallas_call | solution.py:261
  55.4 8.6 %all-to-all-done.1.terms = bf16[64,16,512]{2,1,0:T(8,128)(2,1)S(1)} async-done(((bf16[64,16,512]{2,1,0:T(8,128)(2,1)}), bf16[64,16,512]{2,1,0:T(8,128)(2,1)S(1)}, u32[]{:S(2)}, u32[]{:S(2)}) %all-to-all-start.1) | async-done | bytes 1048608 | tf_op jit(solution)/shard_map/scatter_sum/all_to_all | solution.py:297
  64.0 0.2 sum_part.1
  64.3 21.2 %all_to_all.16.pieces = bf16[64,16,512]{2,1,0:T(8,128)(2,1)S(1)} all-to-all(bf16[64,16,512]{2,1,0:T(8,128)(2,1)S(1)} %sum_part.1), channel_id=1, replica_groups=mesh['rows'=2,'vocab'=64] {'vocab'}, dimensions={0} | all-to-all | bytes 2097152 | tf_op jit(solution)/shard_map/gather/all_to_all | solution.py:304
  85.4 1.4 %join_part.1 = f32[256,2048]{1,0:T(8,128)} custom-call(bf16[64,16,512]{2,1,0:T(8,128)(2,1)S(1)} %all_to_all.16.pieces), custom_call_target="tpu_custom_call" | custom-call | tf_op jit(solution)/shard_map/join_part/pallas_call | solution.py:224
  (1 shorter events, 0.0 us)
Async XLA Ops:
  0.6 8.7 %collective-permute-start = (bf16[1024,2432]{1,0:T(8,128)(2,1)}, bf16[1024,2432]{1,0:T(8,128)(2,1)}, u32[]{:S(2)}, u32[]{:S(2)}) collective-permute-start(bf16[1024,2432]{1,0:T(8,128)(2,1)} %weight.1), channel_id=1, source_target_pairs={{0,64},{64,0},{1,65},{65,1},{2,66},{66,2},{3,67},{67,3},{4,68},{68... | collective-permute-start | bytes 14942216 | tf_op jit(solution)/shard_map/swap_weight/ppermute | solution.py:26
  2.0 2.4 %copy-start = (bf16[1024,2432]{1,0:T(8,128)(2,1)S(1)}, bf16[1024,2432]{1,0:T(8,128)(2,1)}, u32[]{:S(2)}) copy-start(bf16[1024,2432]{1,0:T(8,128)(2,1)} %weight.1) | copy-start | bytes 14942212
  4.4 1.3 %copy-start.1 = (bf16[256,2432]{1,0:T(8,128)(2,1)S(1)}, bf16[256,2432]{1,0:T(8,128)(2,1)}, u32[]{:S(2)}) copy-start(bf16[256,2432]{1,0:T(8,128)(2,1)} %target.3) | copy-start | bytes 3735556
  9.3 27.1 %copy-start.2 = (bf16[256,2432]{1,0:T(8,128)(2,1)S(1)}, bf16[256,2432]{1,0:T(8,128)(2,1)}, u32[]{:S(2)}) copy-start(bf16[256,2432]{1,0:T(8,128)(2,1)} %target.3) | copy-start | bytes 3735556
  41.1 22.9 %all-to-all-start.1 = ((bf16[64,16,512]{2,1,0:T(8,128)(2,1)}), bf16[64,16,512]{2,1,0:T(8,128)(2,1)S(1)}, u32[]{:S(2)}, u32[]{:S(2)}) async-start(bf16[64,16,512]{2,1,0:T(8,128)(2,1)} %get-tuple-element.25), calls=%async_computation.1 | async-start | bytes 2097152 | tf_op jit(solution)/shard_map/scatter_sum/all_to_all | solution.py:297
  45.9 2.0 %collective-permute-start.1 = (bf16[256,1024]{1,0:T(8,128)(2,1)S(1)}, bf16[256,1024]{1,0:T(8,128)(2,1)S(1)}, u32[]{:S(2)}, u32[]{:S(2)}) collective-permute-start(bf16[256,1024]{1,0:T(8,128)(2,1)S(1)} %get-tuple-element.32.theirs), channel_id=1, source_target_pairs={{0,64},{64,0},{1,65},{65,1},{2,66},{66,2},{3,67},{67,3},{4,68},{68... | collective-permute-start | bytes 1572872 | tf_op jit(solution)/shard_map/swap_back/ppermute | solution.py:26
  46.0 3.7 %collective-permute-start.2 = (bf16[256,896]{1,0:T(8,128)(2,1)S(1)}, bf16[256,896]{1,0:T(8,128)(2,1)S(1)}, u32[]{:S(2)}, u32[]{:S(2)}) collective-permute-start(bf16[256,896]{1,0:T(8,128)(2,1)S(1)} %get-tuple-element.26.rest_0_), channel_id=1, source_target_pairs={{0,64},{64,0},{1,65},{65,1},{2,66},{66,2},{3,67},{67,3},{4,68},{68... | collective-permute-start | bytes 1376264 | tf_op jit(solution)/shard_map/swap_back/ppermute | solution.py:26
  46.5 3.2 %collective-permute-start.3 = (bf16[256,896]{1,0:T(8,128)(2,1)S(1)}, bf16[256,896]{1,0:T(8,128)(2,1)S(1)}, u32[]{:S(2)}, u32[]{:S(2)}) collective-permute-start(bf16[256,896]{1,0:T(8,128)(2,1)S(1)} %get-tuple-element.27.rest_1_), channel_id=1, source_target_pairs={{0,64},{64,0},{1,65},{65,1},{2,66},{66,2},{3,67},{67,3},{4,68},{68... | collective-permute-start | bytes 1376264 | tf_op jit(solution)/shard_map/swap_back/ppermute | solution.py:26
  46.6 3.1 %collective-permute-start.4 = (bf16[256,640]{1,0:T(8,128)(2,1)S(1)}, bf16[256,640]{1,0:T(8,128)(2,1)S(1)}, u32[]{:S(2)}, u32[]{:S(2)}) collective-permute-start(bf16[256,640]{1,0:T(8,128)(2,1)S(1)} %get-tuple-element.28.rest_2_), channel_id=1, source_target_pairs={{0,64},{64,0},{1,65},{65,1},{2,66},{66,2},{3,67},{67,3},{4,68},{68... | collective-permute-start | bytes 983048 | tf_op jit(solution)/shard_map/swap_back/ppermute | solution.py:26

commit v12 on v11

--- a/solution.py
+++ b/solution.py
@@ -83,12 +83,16 @@
     )(mine, target, weight)
 
 
-def draft_kernel(theirs, acc, probs, stat, weight, draft, out, buffer, sem):
+def draft_kernel(theirs, acc, probs, stat, weight, draft, out, buffer, sems):
     tokens, vocab = draft.shape
-    copy = pltpu.make_async_copy(weight, buffer, sem)
-    copy.start()
-    copy.wait()
-    draft[...] = acc[...] + dot(theirs[...], buffer[...], 1, 0)
+    copies = []
+    for j, (c, e) in enumerate(thirds(vocab)):
+        part = pl.ds(c, e - c)
+        copies.append(pltpu.make_async_copy(weight.at[:, part], buffer.at[:, part], sems.at[j]))
+        copies[-1].start()
+    for copy, (c, e) in zip(copies, thirds(vocab)):
+        copy.wait()
+        draft[:, c:e] = acc[:, c:e] + dot(theirs[...], buffer[:, c:e], 1, 0)
     lse_q, mean = [], []
     for first in range(0, tokens, GROUP):
         rows = slice(first, first + GROUP)
@@ -126,7 +130,7 @@
             jax.ShapeDtypeStruct((stat_rows(tokens), 128), F32),
             jax.ShapeDtypeStruct((half, vocab), BF16),
         ],
-        scratch_shapes=[pltpu.SemaphoreType.DMA],
+        scratch_shapes=[pltpu.SemaphoreType.DMA((3,))],
         compiler_params=params(20),
         cost_estimate=cost(2 * tokens * half * vocab, 2 * half * vocab),
         name="draft_part",

time: 87.3 us -> 86.9 us (level)
  no operation moved by 1% of the time
where the time goes in v12:
time: 86.9 us; the launch traced here: 86.5 us
  blocking collectives  43.4 us (50%)
  Pallas kernels  19.1 us (22%)
  waiting for transfers between devices  12.1 us (14%)
  starting transfers between devices  6.04 us (7%)
  local copies, waits for them, and re-layouts  5 us (6%)
  between operations  0.88 us (1%)
    all_to_all x1, blocking collectives, shards(): lax.all_to_all(jnp.broadcast_to(part[None], (n,) + part.shape), 'vocab',...  22.2 us
    all_to_all x1, blocking collectives, shards(): gathered = lax.all_to_all(totals, 'vocab', 0, 0)  21.2 us
    all_to_all x1, waiting for transfers between devices, shards(): terms = lax.all_to_all(pieces, 'vocab', 0, 0)  8.59 us
    pallas_call x1, Pallas kernels, head_part(): pl.pallas_call(head_kernel, in_specs=[VMEM] * 4 + [ANY] * 4, out_specs=AN...  5.69 us
    all_to_all x1, starting transfers between devices, shards(): terms = lax.all_to_all(pieces, 'vocab', 0, 0)  4.86 us
    pallas_call x1, Pallas kernels, back_part(): pl.pallas_call(functools.partial(back_kernel, factor), in_specs=[pl.Block...  4.62 us
    pallas_call x1, Pallas kernels, draft_part(): pl.pallas_call(draft_kernel, in_specs=[VMEM] * 4 + [ANY], out_specs=[VMEM...  4.42 us
    unnamed x6, local copies, waits for them, and re-layouts  3.7 us
  transfers between devices with their start and end apart: 6, of which 4 were waited for; matrix products, arithmetic and copies ran while one was open for 1% of the time, Pallas kernels for 10%

profile of v12, /device:TPU:0, one launch (start us, length us, event | category | flops | bytes accessed | tf_op | source)
XLA Modules:
  0.0 86.5 jit_solution(10506491401245116142)
XLA Ops:
  0.6 0.1 collective-permute-start
  0.7 1.3 %constant_dynamic-slice_fusion = (bf16[256,1024]{1,0:T(8,128)(2,1)S(1)}, bf16[256,1024]{1,0:T(8,128)(2,1)S(1)}) fusion(bf16[256,2048]{1,0:T(8,128)(2,1)} %param.3, s32[]{:T(128)S(6)} %select_n.7, s32[]{:T(128)S(6)} %select_n.6), kind=kLoop, calls=%fused_computation | loop fusion | bytes 2097160 | tf_op jit(solution)/shard_map/dynamic_slice | solution.py:290
  2.0 0.0 copy-start
  2.0 2.4 %copy-done = bf16[1024,2432]{1,0:T(8,128)(2,1)S(1)} copy-done((bf16[1024,2432]{1,0:T(8,128)(2,1)S(1)}, bf16[1024,2432]{1,0:T(8,128)(2,1)}, u32[]{:S(2)}) %copy-start) | copy-done | bytes 4980760
  4.4 0.0 copy-start.1
  4.4 1.3 %copy-done.1 = bf16[256,2432]{1,0:T(8,128)(2,1)S(1)} copy-done((bf16[256,2432]{1,0:T(8,128)(2,1)S(1)}, bf16[256,2432]{1,0:T(8,128)(2,1)}, u32[]{:S(2)}) %copy-start.1) | copy-done | bytes 1245208
  5.7 2.7 %own_part.1 = (f32[256,2432]{1,0:T(8,128)S(1)}, f32[256,2432]{1,0:T(8,128)S(1)}, f32[256,128]{1,0:T(8,128)S(1)}, bf16[1024,2432]{1,0:T(8,128)(2,1)S(1)}) custom-call(bf16[256,1024]{1,0:T(8,128)(2,1)S(1)} %get-tuple-element.31.mine, bf16[256,2432]{1,0:T(8,128)(2,1)S(1)} %copy-done.1, bf16[1024,2432]{1,0:T(8,128)(2,1)S(1)} %copy-done), custom_call_target="tpu_custom_call" | custom-call | flops 1275068416 | bytes 4980736 | tf_op jit(solution)/shard_map/own_part/pallas_call | solution.py:69
  8.5 0.9 collective-permute-done.weight
  9.3 0.0 copy-start.2
  9.3 4.4 %draft_part.1 = (f32[256,2432]{1,0:T(8,128)S(1)}, f32[8,128]{1,0:T(8,128)S(1)}, bf16[1024,2432]{1,0:T(8,128)(2,1)S(1)}) custom-call(bf16[256,1024]{1,0:T(8,128)(2,1)S(1)} %get-tuple-element.32.theirs, f32[256,2432]{1,0:T(8,128)S(1)} %get-tuple-element.17.acc, f32[256,2432]{1,0:T(8,128)S(1)} %get-tuple-element.18.probs, ...), custom_call_target="tpu_custom_call" | custom-call | flops 1275068416 | bytes 4980736 | tf_op jit(solution)/shard_map/draft_part/pallas_call | solution.py:124
  13.8 22.2 %all_to_all.15.parts = f32[64,8,128]{2,1,0:T(8,128)S(1)} all-to-all(f32[64,8,128]{2,1,0:T(8,128)S(1)} %broadcast_in_dim.10), channel_id=1, replica_groups=mesh['rows'=2,'vocab'=64] {'vocab'}, dimensions={0} | all-to-all | bytes 524288 | tf_op jit(solution)/shard_map/share_stats/all_to_all | solution.py:296
  36.0 0.0 copy-done.2
  36.0 4.6 %back_part.1 = (f32[1,256]{1,0:T(1,128)}, bf16[64,16,512]{2,1,0:T(8,128)(2,1)}, bf16[256,896]{1,0:T(8,128)(2,1)S(1)}, bf16[256,896]{1,0:T(8,128)(2,1)S(1)}, bf16[256,640]{1,0:T(8,128)(2,1)S(1)}) custom-call(s32[1]{0:T(128)} %bitcast.row, f32[64,8,128]{2,1,0:T(8,128)S(1)} %all_to_all.15.parts, f32[256,2432]{1,0:T(8,128)S(1)} %get-tuple-element.21.draft, ...), custom_call_target="tpu_custom_call" | custom-call | flops 2550136832 | bytes 9961472 | tf_op jit(solution)/shard_map/back_part/pallas_call | solution.py:177
  40.6 4.9 %all-to-all-start.1 = ((bf16[64,16,512]{2,1,0:T(8,128)(2,1)}), bf16[64,16,512]{2,1,0:T(8,128)(2,1)S(1)}, u32[]{:S(2)}, u32[]{:S(2)}) async-start(bf16[64,16,512]{2,1,0:T(8,128)(2,1)} %get-tuple-element.25), calls=%async_computation.1 | async-start | bytes 2097152 | tf_op jit(solution)/shard_map/scatter_sum/all_to_all | solution.py:301
  45.5 0.1 collective-permute-start.1
  45.6 0.5 collective-permute-start.2
  46.1 0.1 collective-permute-start.3
  46.2 0.4 collective-permute-start.4
  46.6 0.9 %collective-permute-done.1.rest_3_ = bf16[256,1024]{1,0:T(8,128)(2,1)S(1)} collective-permute-done((bf16[256,1024]{1,0:T(8,128)(2,1)S(1)}, bf16[256,1024]{1,0:T(8,128)(2,1)S(1)}, u32[]{:S(2)}, u32[]{:S(2)}) %collective-permute-start.1) | collective-permute-done | bytes 524320 | tf_op jit(solution)/shard_map/swap_back/ppermute | solution.py:26
  47.5 1.8 %collective-permute-done.4.rest_6_ = bf16[256,640]{1,0:T(8,128)(2,1)S(1)} collective-permute-done((bf16[256,640]{1,0:T(8,128)(2,1)S(1)}, bf16[256,640]{1,0:T(8,128)(2,1)S(1)}, u32[]{:S(2)}, u32[]{:S(2)}) %collective-permute-start.4) | collective-permute-done | bytes 327712 | tf_op jit(solution)/shard_map/swap_back/ppermute | solution.py:26
  49.2 0.0 collective-permute-done.2.rest_4_
  49.2 0.0 collective-permute-done.3.rest_5_
  49.3 5.7 %head_part.1 = f32[1024,2432]{1,0:T(8,128)} custom-call(bf16[256,1024]{1,0:T(8,128)(2,1)S(1)} %get-tuple-element.31.mine, bf16[256,896]{1,0:T(8,128)(2,1)S(1)} %get-tuple-element.26.rest_0_, bf16[256,896]{1,0:T(8,128)(2,1)S(1)} %get-tuple-element.27.rest_1_, bf16[256,640]{1,0:T(8,128)(2,1)S(1)} %get-tuple-element.28.rest_2_, ...), custom_call_target="tpu_custom_call" | custom-call | flops 2550136832 | bytes 9961472 | tf_op jit(solution)/shard_map/head_part/pallas_call | solution.py:265
  55.0 8.6 %all-to-all-done.1.terms = bf16[64,16,512]{2,1,0:T(8,128)(2,1)S(1)} async-done(((bf16[64,16,512]{2,1,0:T(8,128)(2,1)}), bf16[64,16,512]{2,1,0:T(8,128)(2,1)S(1)}, u32[]{:S(2)}, u32[]{:S(2)}) %all-to-all-start.1) | async-done | bytes 1048608 | tf_op jit(solution)/shard_map/scatter_sum/all_to_all | solution.py:301
  63.5 0.2 sum_part.1
  63.8 21.2 %all_to_all.16.pieces = bf16[64,16,512]{2,1,0:T(8,128)(2,1)S(1)} all-to-all(bf16[64,16,512]{2,1,0:T(8,128)(2,1)S(1)} %sum_part.1), channel_id=1, replica_groups=mesh['rows'=2,'vocab'=64] {'vocab'}, dimensions={0} | all-to-all | bytes 2097152 | tf_op jit(solution)/shard_map/gather/all_to_all | solution.py:308
  85.0 1.4 %join_part.1 = f32[256,2048]{1,0:T(8,128)} custom-call(bf16[64,16,512]{2,1,0:T(8,128)(2,1)S(1)} %all_to_all.16.pieces), custom_call_target="tpu_custom_call" | custom-call | tf_op jit(solution)/shard_map/join_part/pallas_call | solution.py:228
  (1 shorter events, 0.0 us)
Async XLA Ops:
  0.6 8.7 %collective-permute-start = (bf16[1024,2432]{1,0:T(8,128)(2,1)}, bf16[1024,2432]{1,0:T(8,128)(2,1)}, u32[]{:S(2)}, u32[]{:S(2)}) collective-permute-start(bf16[1024,2432]{1,0:T(8,128)(2,1)} %weight.1), channel_id=1, source_target_pairs={{0,64},{64,0},{1,65},{65,1},{2,66},{66,2},{3,67},{67,3},{4,68},{68... | collective-permute-start | bytes 14942216 | tf_op jit(solution)/shard_map/swap_weight/ppermute | solution.py:26
  2.0 2.4 %copy-start = (bf16[1024,2432]{1,0:T(8,128)(2,1)S(1)}, bf16[1024,2432]{1,0:T(8,128)(2,1)}, u32[]{:S(2)}) copy-start(bf16[1024,2432]{1,0:T(8,128)(2,1)} %weight.1) | copy-start | bytes 14942212
  4.4 1.3 %copy-start.1 = (bf16[256,2432]{1,0:T(8,128)(2,1)S(1)}, bf16[256,2432]{1,0:T(8,128)(2,1)}, u32[]{:S(2)}) copy-start(bf16[256,2432]{1,0:T(8,128)(2,1)} %target.3) | copy-start | bytes 3735556
  9.3 26.7 %copy-start.2 = (bf16[256,2432]{1,0:T(8,128)(2,1)S(1)}, bf16[256,2432]{1,0:T(8,128)(2,1)}, u32[]{:S(2)}) copy-start(bf16[256,2432]{1,0:T(8,128)(2,1)} %target.3) | copy-start | bytes 3735556
  40.6 22.9 %all-to-all-start.1 = ((bf16[64,16,512]{2,1,0:T(8,128)(2,1)}), bf16[64,16,512]{2,1,0:T(8,128)(2,1)S(1)}, u32[]{:S(2)}, u32[]{:S(2)}) async-start(bf16[64,16,512]{2,1,0:T(8,128)(2,1)} %get-tuple-element.25), calls=%async_computation.1 | async-start | bytes 2097152 | tf_op jit(solution)/shard_map/scatter_sum/all_to_all | solution.py:301
  45.5 2.0 %collective-permute-start.1 = (bf16[256,1024]{1,0:T(8,128)(2,1)S(1)}, bf16[256,1024]{1,0:T(8,128)(2,1)S(1)}, u32[]{:S(2)}, u32[]{:S(2)}) collective-permute-start(bf16[256,1024]{1,0:T(8,128)(2,1)S(1)} %get-tuple-element.32.theirs), channel_id=1, source_target_pairs={{0,64},{64,0},{1,65},{65,1},{2,66},{66,2},{3,67},{67,3},{4,68},{68... | collective-permute-start | bytes 1572872 | tf_op jit(solution)/shard_map/swap_back/ppermute | solution.py:26
  45.6 3.7 %collective-permute-start.2 = (bf16[256,896]{1,0:T(8,128)(2,1)S(1)}, bf16[256,896]{1,0:T(8,128)(2,1)S(1)}, u32[]{:S(2)}, u32[]{:S(2)}) collective-permute-start(bf16[256,896]{1,0:T(8,128)(2,1)S(1)} %get-tuple-element.26.rest_0_), channel_id=1, source_target_pairs={{0,64},{64,0},{1,65},{65,1},{2,66},{66,2},{3,67},{67,3},{4,68},{68... | collective-permute-start | bytes 1376264 | tf_op jit(solution)/shard_map/swap_back/ppermute | solution.py:26
  46.1 3.2 %collective-permute-start.3 = (bf16[256,896]{1,0:T(8,128)(2,1)S(1)}, bf16[256,896]{1,0:T(8,128)(2,1)S(1)}, u32[]{:S(2)}, u32[]{:S(2)}) collective-permute-start(bf16[256,896]{1,0:T(8,128)(2,1)S(1)} %get-tuple-element.27.rest_1_), channel_id=1, source_target_pairs={{0,64},{64,0},{1,65},{65,1},{2,66},{66,2},{3,67},{67,3},{4,68},{68... | collective-permute-start | bytes 1376264 | tf_op jit(solution)/shard_map/swap_back/ppermute | solution.py:26
  46.2 3.1 %collective-permute-start.4 = (bf16[256,640]{1,0:T(8,128)(2,1)S(1)}, bf16[256,640]{1,0:T(8,128)(2,1)S(1)}, u32[]{:S(2)}, u32[]{:S(2)}) collective-permute-start(bf16[256,640]{1,0:T(8,128)(2,1)S(1)} %get-tuple-element.28.rest_2_), channel_id=1, source_target_pairs={{0,64},{64,0},{1,65},{65,1},{2,66},{66,2},{3,67},{67,3},{4,68},{68... | collective-permute-start | bytes 983048 | tf_op jit(solution)/shard_map/swap_back/ppermute | solution.py:26

commit v13 on v12

--- a/solution.py
+++ b/solution.py
@@ -137,7 +137,8 @@
     )(theirs, acc, probs, stat, weight)
 
 
-def back_kernel(factor, row, parts, draft, target, weight, weight_o, divergence, out, *dlogits):
+def back_kernel(factor, row, parts, draft, target, weight, weight_o, divergence, out, *rest):
+    *dlogits, stage, sems = rest
     lines = draft.shape[0] // 128
     every = parts[...]
     top = jnp.max(every, axis=0)
@@ -155,7 +156,7 @@
     half = weight.shape[0]
     per = half // COLS_PIECE
     down = draft.shape[0] // TOKENS_PIECE
-    sums = [None] * (2 * per)
+    sums, copies = [None] * (2 * per), []
     for kept, (c, e) in zip(dlogits, thirds(draft.shape[1])):
         probs_q = exp(draft[:, c:e] - lse_q)
         probs_t = exp(target[:, c:e].astype(F32) - lse_t)
@@ -165,9 +166,13 @@
             rows = pl.ds(j % per * COLS_PIECE, COLS_PIECE)
             term = dot(block, (weight, weight_o)[j // per][rows, c:e], 1, 1)
             sums[j] = term if sums[j] is None else sums[j] + term
-    for j in range(2 * per):
-        place = lax.rem(row[0] * per + j, 2 * per)
-        out[pl.ds(place * down, down)] = sums[j].astype(BF16).reshape(down, TOKENS_PIECE, COLS_PIECE)
+            if e == draft.shape[1]:
+                place = lax.rem(row[0] * per + j, 2 * per)
+                stage[j] = sums[j].astype(BF16).reshape(down, TOKENS_PIECE, COLS_PIECE)
+                copies.append(pltpu.make_async_copy(stage.at[j], out.at[pl.ds(place * down, down)], sems.at[j]))
+                copies[-1].start()
+    for copy in copies:
+        copy.wait()
 
 
 def back_part(factor, row, parts, draft, target, weight, weight_o):
@@ -177,12 +182,16 @@
     return pl.pallas_call(
         functools.partial(back_kernel, factor),
         in_specs=[pl.BlockSpec(memory_space=pltpu.SMEM)] + [VMEM] * 5,
-        out_specs=[VMEM] * 5,
+        out_specs=[VMEM, ANY] + [VMEM] * 3,
         out_shape=[
             jax.ShapeDtypeStruct((1, tokens), F32),
             jax.ShapeDtypeStruct((pieces, TOKENS_PIECE, COLS_PIECE), BF16),
         ]
         + [jax.ShapeDtypeStruct((tokens, e - c), BF16) for c, e in thirds(vocab)],
+        scratch_shapes=[
+            pltpu.VMEM((2 * half // COLS_PIECE, tokens // TOKENS_PIECE, TOKENS_PIECE, COLS_PIECE), BF16),
+            pltpu.SemaphoreType.DMA((2 * half // COLS_PIECE,)),
+        ],
         compiler_params=params(16),
         cost_estimate=cost(4 * tokens * half * vocab, 4 * half * vocab),
         name="back_part",

time: 86.9 us -> 87.2 us (level)
  no operation moved by 1% of the time
where the time goes in v13:
time: 87.2 us; the launch traced here: 86.9 us
  blocking collectives  43.4 us (50%)
  Pallas kernels  19.4 us (22%)
  waiting for transfers between devices  12.1 us (14%)
  starting transfers between devices  6.05 us (7%)
  local copies, waits for them, and re-layouts  5 us (6%)
  between operations  0.89 us (1%)
    all_to_all x1, blocking collectives, shards(): lax.all_to_all(jnp.broadcast_to(part[None], (n,) + part.shape), 'vocab',...  22.2 us
    all_to_all x1, blocking collectives, shards(): gathered = lax.all_to_all(totals, 'vocab', 0, 0)  21.2 us
    all_to_all x1, waiting for transfers between devices, shards(): terms = lax.all_to_all(pieces, 'vocab', 0, 0)  8.59 us
    pallas_call x1, Pallas kernels, head_part(): pl.pallas_call(head_kernel, in_specs=[VMEM] * 4 + [ANY] * 4, out_specs=AN...  5.69 us
    pallas_call x1, Pallas kernels, back_part(): pl.pallas_call(functools.partial(back_kernel, factor), in_specs=[pl.Block...  4.97 us
    all_to_all x1, starting transfers between devices, shards(): terms = lax.all_to_all(pieces, 'vocab', 0, 0)  4.87 us
    pallas_call x1, Pallas kernels, draft_part(): pl.pallas_call(draft_kernel, in_specs=[VMEM] * 4 + [ANY], out_specs=[VMEM...  4.42 us
    unnamed x6, local copies, waits for them, and re-layouts  3.7 us
  transfers between devices with their start and end apart: 6, of which 4 were waited for; matrix products, arithmetic and copies ran while one was open for 1% of the time, Pallas kernels for 10%

profile of v13, /device:TPU:0, one launch (start us, length us, event | category | flops | bytes accessed | tf_op | source)
XLA Modules:
  0.0 86.9 jit_solution(11923154732908024620)
XLA Ops:
  0.6 0.1 collective-permute-start
  0.7 1.3 %constant_dynamic-slice_fusion = (bf16[256,1024]{1,0:T(8,128)(2,1)S(1)}, bf16[256,1024]{1,0:T(8,128)(2,1)S(1)}) fusion(bf16[256,2048]{1,0:T(8,128)(2,1)} %param.3, s32[]{:T(128)S(6)} %select_n.7, s32[]{:T(128)S(6)} %select_n.6), kind=kLoop, calls=%fused_computation | loop fusion | bytes 2097160 | tf_op jit(solution)/shard_map/dynamic_slice | solution.py:299
  2.0 0.0 copy-start
  2.0 2.4 %copy-done = bf16[1024,2432]{1,0:T(8,128)(2,1)S(1)} copy-done((bf16[1024,2432]{1,0:T(8,128)(2,1)S(1)}, bf16[1024,2432]{1,0:T(8,128)(2,1)}, u32[]{:S(2)}) %copy-start) | copy-done | bytes 4980760
  4.4 0.0 copy-start.1
  4.4 1.3 %copy-done.1 = bf16[256,2432]{1,0:T(8,128)(2,1)S(1)} copy-done((bf16[256,2432]{1,0:T(8,128)(2,1)S(1)}, bf16[256,2432]{1,0:T(8,128)(2,1)}, u32[]{:S(2)}) %copy-start.1) | copy-done | bytes 1245208
  5.7 2.7 %own_part.1 = (f32[256,2432]{1,0:T(8,128)S(1)}, f32[256,2432]{1,0:T(8,128)S(1)}, f32[256,128]{1,0:T(8,128)S(1)}, bf16[1024,2432]{1,0:T(8,128)(2,1)S(1)}) custom-call(bf16[256,1024]{1,0:T(8,128)(2,1)S(1)} %get-tuple-element.31.mine, bf16[256,2432]{1,0:T(8,128)(2,1)S(1)} %copy-done.1, bf16[1024,2432]{1,0:T(8,128)(2,1)S(1)} %copy-done), custom_call_target="tpu_custom_call" | custom-call | flops 1275068416 | bytes 4980736 | tf_op jit(solution)/shard_map/own_part/pallas_call | solution.py:69
  8.5 0.9 collective-permute-done.weight
  9.3 0.0 copy-start.2
  9.3 4.4 %draft_part.1 = (f32[256,2432]{1,0:T(8,128)S(1)}, f32[8,128]{1,0:T(8,128)S(1)}, bf16[1024,2432]{1,0:T(8,128)(2,1)S(1)}) custom-call(bf16[256,1024]{1,0:T(8,128)(2,1)S(1)} %get-tuple-element.32.theirs, f32[256,2432]{1,0:T(8,128)S(1)} %get-tuple-element.17.acc, f32[256,2432]{1,0:T(8,128)S(1)} %get-tuple-element.18.probs, ...), custom_call_target="tpu_custom_call" | custom-call | flops 1275068416 | bytes 4980736 | tf_op jit(solution)/shard_map/draft_part/pallas_call | solution.py:124
  13.8 22.2 %all_to_all.15.parts = f32[64,8,128]{2,1,0:T(8,128)S(1)} all-to-all(f32[64,8,128]{2,1,0:T(8,128)S(1)} %broadcast_in_dim.10), channel_id=1, replica_groups=mesh['rows'=2,'vocab'=64] {'vocab'}, dimensions={0} | all-to-all | bytes 524288 | tf_op jit(solution)/shard_map/share_stats/all_to_all | solution.py:305
  36.0 0.0 copy-done.2
  36.0 5.0 %back_part.1 = (f32[1,256]{1,0:T(1,128)}, bf16[64,16,512]{2,1,0:T(8,128)(2,1)}, bf16[256,896]{1,0:T(8,128)(2,1)S(1)}, bf16[256,896]{1,0:T(8,128)(2,1)S(1)}, bf16[256,640]{1,0:T(8,128)(2,1)S(1)}) custom-call(s32[1]{0:T(128)} %bitcast.row, f32[64,8,128]{2,1,0:T(8,128)S(1)} %all_to_all.15.parts, f32[256,2432]{1,0:T(8,128)S(1)} %get-tuple-element.21.draft, ...), custom_call_target="tpu_custom_call" | custom-call | flops 2550136832 | bytes 9961472 | tf_op jit(solution)/shard_map/back_part/pallas_call | solution.py:182
  41.0 4.9 %all-to-all-start.1 = ((bf16[64,16,512]{2,1,0:T(8,128)(2,1)}), bf16[64,16,512]{2,1,0:T(8,128)(2,1)S(1)}, u32[]{:S(2)}, u32[]{:S(2)}) async-start(bf16[64,16,512]{2,1,0:T(8,128)(2,1)} %get-tuple-element.25), calls=%async_computation.1 | async-start | bytes 2097152 | tf_op jit(solution)/shard_map/scatter_sum/all_to_all | solution.py:310
  45.8 0.1 collective-permute-start.1
  45.9 0.5 collective-permute-start.2
  46.4 0.1 collective-permute-start.3
  46.5 0.4 collective-permute-start.4
  46.9 0.9 %collective-permute-done.1.rest_3_ = bf16[256,1024]{1,0:T(8,128)(2,1)S(1)} collective-permute-done((bf16[256,1024]{1,0:T(8,128)(2,1)S(1)}, bf16[256,1024]{1,0:T(8,128)(2,1)S(1)}, u32[]{:S(2)}, u32[]{:S(2)}) %collective-permute-start.1) | collective-permute-done | bytes 524320 | tf_op jit(solution)/shard_map/swap_back/ppermute | solution.py:26
  47.8 1.8 %collective-permute-done.4.rest_6_ = bf16[256,640]{1,0:T(8,128)(2,1)S(1)} collective-permute-done((bf16[256,640]{1,0:T(8,128)(2,1)S(1)}, bf16[256,640]{1,0:T(8,128)(2,1)S(1)}, u32[]{:S(2)}, u32[]{:S(2)}) %collective-permute-start.4) | collective-permute-done | bytes 327712 | tf_op jit(solution)/shard_map/swap_back/ppermute | solution.py:26
  49.6 0.0 collective-permute-done.2.rest_4_
  49.6 0.0 collective-permute-done.3.rest_5_
  49.6 5.7 %head_part.1 = f32[1024,2432]{1,0:T(8,128)} custom-call(bf16[256,1024]{1,0:T(8,128)(2,1)S(1)} %get-tuple-element.31.mine, bf16[256,896]{1,0:T(8,128)(2,1)S(1)} %get-tuple-element.26.rest_0_, bf16[256,896]{1,0:T(8,128)(2,1)S(1)} %get-tuple-element.27.rest_1_, bf16[256,640]{1,0:T(8,128)(2,1)S(1)} %get-tuple-element.28.rest_2_, ...), custom_call_target="tpu_custom_call" | custom-call | flops 2550136832 | bytes 9961472 | tf_op jit(solution)/shard_map/head_part/pallas_call | solution.py:274
  55.3 8.6 %all-to-all-done.1.terms = bf16[64,16,512]{2,1,0:T(8,128)(2,1)S(1)} async-done(((bf16[64,16,512]{2,1,0:T(8,128)(2,1)}), bf16[64,16,512]{2,1,0:T(8,128)(2,1)S(1)}, u32[]{:S(2)}, u32[]{:S(2)}) %all-to-all-start.1) | async-done | bytes 1048608 | tf_op jit(solution)/shard_map/scatter_sum/all_to_all | solution.py:310
  63.9 0.2 sum_part.1
  64.2 21.2 %all_to_all.16.pieces = bf16[64,16,512]{2,1,0:T(8,128)(2,1)S(1)} all-to-all(bf16[64,16,512]{2,1,0:T(8,128)(2,1)S(1)} %sum_part.1), channel_id=1, replica_groups=mesh['rows'=2,'vocab'=64] {'vocab'}, dimensions={0} | all-to-all | bytes 2097152 | tf_op jit(solution)/shard_map/gather/all_to_all | solution.py:317
  85.3 1.4 %join_part.1 = f32[256,2048]{1,0:T(8,128)} custom-call(bf16[64,16,512]{2,1,0:T(8,128)(2,1)S(1)} %all_to_all.16.pieces), custom_call_target="tpu_custom_call" | custom-call | tf_op jit(solution)/shard_map/join_part/pallas_call | solution.py:237
  (1 shorter events, 0.0 us)
Async XLA Ops:
  0.6 8.7 %collective-permute-start = (bf16[1024,2432]{1,0:T(8,128)(2,1)}, bf16[1024,2432]{1,0:T(8,128)(2,1)}, u32[]{:S(2)}, u32[]{:S(2)}) collective-permute-start(bf16[1024,2432]{1,0:T(8,128)(2,1)} %weight.1), channel_id=1, source_target_pairs={{0,64},{64,0},{1,65},{65,1},{2,66},{66,2},{3,67},{67,3},{4,68},{68... | collective-permute-start | bytes 14942216 | tf_op jit(solution)/shard_map/swap_weight/ppermute | solution.py:26
  2.0 2.4 %copy-start = (bf16[1024,2432]{1,0:T(8,128)(2,1)S(1)}, bf16[1024,2432]{1,0:T(8,128)(2,1)}, u32[]{:S(2)}) copy-start(bf16[1024,2432]{1,0:T(8,128)(2,1)} %weight.1) | copy-start | bytes 14942212
  4.4 1.3 %copy-start.1 = (bf16[256,2432]{1,0:T(8,128)(2,1)S(1)}, bf16[256,2432]{1,0:T(8,128)(2,1)}, u32[]{:S(2)}) copy-start(bf16[256,2432]{1,0:T(8,128)(2,1)} %target.3) | copy-start | bytes 3735556
  9.3 26.7 %copy-start.2 = (bf16[256,2432]{1,0:T(8,128)(2,1)S(1)}, bf16[256,2432]{1,0:T(8,128)(2,1)}, u32[]{:S(2)}) copy-start(bf16[256,2432]{1,0:T(8,128)(2,1)} %target.3) | copy-start | bytes 3735556
  41.0 22.9 %all-to-all-start.1 = ((bf16[64,16,512]{2,1,0:T(8,128)(2,1)}), bf16[64,16,512]{2,1,0:T(8,128)(2,1)S(1)}, u32[]{:S(2)}, u32[]{:S(2)}) async-start(bf16[64,16,512]{2,1,0:T(8,128)(2,1)} %get-tuple-element.25), calls=%async_computation.1 | async-start | bytes 2097152 | tf_op jit(solution)/shard_map/scatter_sum/all_to_all | solution.py:310
  45.8 2.0 %collective-permute-start.1 = (bf16[256,1024]{1,0:T(8,128)(2,1)S(1)}, bf16[256,1024]{1,0:T(8,128)(2,1)S(1)}, u32[]{:S(2)}, u32[]{:S(2)}) collective-permute-start(bf16[256,1024]{1,0:T(8,128)(2,1)S(1)} %get-tuple-element.32.theirs), channel_id=1, source_target_pairs={{0,64},{64,0},{1,65},{65,1},{2,66},{66,2},{3,67},{67,3},{4,68},{68... | collective-permute-start | bytes 1572872 | tf_op jit(solution)/shard_map/swap_back/ppermute | solution.py:26
  45.9 3.7 %collective-permute-start.2 = (bf16[256,896]{1,0:T(8,128)(2,1)S(1)}, bf16[256,896]{1,0:T(8,128)(2,1)S(1)}, u32[]{:S(2)}, u32[]{:S(2)}) collective-permute-start(bf16[256,896]{1,0:T(8,128)(2,1)S(1)} %get-tuple-element.26.rest_0_), channel_id=1, source_target_pairs={{0,64},{64,0},{1,65},{65,1},{2,66},{66,2},{3,67},{67,3},{4,68},{68... | collective-permute-start | bytes 1376264 | tf_op jit(solution)/shard_map/swap_back/ppermute | solution.py:26
  46.4 3.2 %collective-permute-start.3 = (bf16[256,896]{1,0:T(8,128)(2,1)S(1)}, bf16[256,896]{1,0:T(8,128)(2,1)S(1)}, u32[]{:S(2)}, u32[]{:S(2)}) collective-permute-start(bf16[256,896]{1,0:T(8,128)(2,1)S(1)} %get-tuple-element.27.rest_1_), channel_id=1, source_target_pairs={{0,64},{64,0},{1,65},{65,1},{2,66},{66,2},{3,67},{67,3},{4,68},{68... | collective-permute-start | bytes 1376264 | tf_op jit(solution)/shard_map/swap_back/ppermute | solution.py:26
  46.5 3.1 %collective-permute-start.4 = (bf16[256,640]{1,0:T(8,128)(2,1)S(1)}, bf16[256,640]{1,0:T(8,128)(2,1)S(1)}, u32[]{:S(2)}, u32[]{:S(2)}) collective-permute-start(bf16[256,640]{1,0:T(8,128)(2,1)S(1)} %get-tuple-element.28.rest_2_), channel_id=1, source_target_pairs={{0,64},{64,0},{1,65},{65,1},{2,66},{66,2},{3,67},{67,3},{4,68},{68... | collective-permute-start | bytes 983048 | tf_op jit(solution)/shard_map/swap_back/ppermute | solution.py:26
